TPU v7x, 256 devices: a whole 4x4x8 slice. The times are simulated.
256 devices in a mesh: dp: 64 (over x_hi, z, y), pair: 4 (over x_lo, core).
Axes of the slice: x: 4 (x_hi: 2, x_lo: 2; x = x_hi * 2 + x_lo), y: 4, z: 8, core: 2. Of those that a mesh axis runs over, the one named last changes fastest.
Arguments:
- image_feats: bfloat16 [65536, 1152], P(('dp', 'pair')), may hold values from -24 to 24
- text_feats: bfloat16 [65536, 1152], P(('dp', 'pair')), may hold values from -24 to 24
- image_head: bfloat16 [1152, 1152], replicated, may hold values from -0.1875 to 0.1875
- text_head: bfloat16 [1152, 1152], replicated, may hold values from -0.1875 to 0.1875
- logit_scale: float32 [1], replicated, may hold values from 4 to 16
- logit_bias: float32 [1], replicated, may hold values from -3 to -1
Outputs:
- image_grads: bfloat16 [65536, 1152], P(('dp', 'pair'))
- text_grads: bfloat16 [65536, 1152], P(('dp', 'pair'))
- head_grads: float32 [1152, 2304], P('pair')
All inputs are finite; a program needn't handle non-finite values.
Results may differ from a plain program's by a relative error of at most 0.008.
Values may be sent and summed in bfloat16 or wider, within the bound.
No kernel may reach another device: no remote copies, remote signals or barrier semaphores. Data moves between devices by JAX's collectives and lax.ppermute only.
A program may use at most 128 MiB of HBM per device.

v0:
```python
import jax
import jax.numpy as jnp
from jax import lax
from jax.sharding import PartitionSpec as P


def partner(block, axis, apart):
    count = lax.axis_size(axis)
    route = []
    for low in range(count):
        high = low | 1 << apart
        if high != low and high < count:
            route += [(low, high), (high, low)]
    return lax.ppermute(block, axis, route)


def embed(feats, weight):
    u = jnp.dot(feats, weight, preferred_element_type=jnp.float32)
    inv = lax.rsqrt(jnp.sum(u * u, axis=1, keepdims=True) + 1e-06)
    return (u * inv, inv)


def tile_weights(img, txt, scale, bias, positive):
    logits = (
        scale
        * lax.dot_general(img, txt, (((1,), (1,)), ((), ())), preferred_element_type=jnp.float32)
        + bias
    )
    sign = jnp.where(positive, 1.0, -1.0).astype(jnp.float32)
    deriv = -sign * jax.nn.sigmoid(-sign * logits)
    return (scale * deriv).astype(jnp.bfloat16)


def image_side(weights, txt):
    return jnp.dot(weights, txt, preferred_element_type=jnp.float32)


def text_side(weights, img):
    return lax.dot_general(
        weights, img, (((0,), (0,)), ((), ())), preferred_element_type=jnp.float32
    )


def backward(z_val, inv, dz_val):
    return (inv * (dz_val - z_val * jnp.sum(z_val * dz_val, axis=1, keepdims=True))).astype(
        jnp.bfloat16
    )


def per_device(image_feats, text_feats, image_head, text_head, logit_scale, logit_bias):
    rows_dev = image_feats.shape[0]
    scale = logit_scale[0]
    bias = logit_bias[0]
    z_img, inv_img = embed(image_feats, image_head)
    z_txt, inv_txt = embed(text_feats, text_head)
    zb_img = z_img.astype(jnp.bfloat16)
    zb_txt = z_txt.astype(jnp.bfloat16)
    group_txt = lax.all_gather(zb_txt, "pair", axis=0, tiled=True)
    group_rows = group_txt.shape[0]
    offset = lax.axis_index("pair") * rows_dev
    row_ids = lax.broadcasted_iota(jnp.int32, (rows_dev, group_rows), 0)
    col_ids = lax.broadcasted_iota(jnp.int32, (rows_dev, group_rows), 1)
    positive = col_ids == row_ids + offset
    negative = jnp.zeros((rows_dev, group_rows), bool)
    home = tile_weights(zb_img, group_txt, scale, bias, positive)
    dz_img = image_side(home, group_txt)
    levels = lax.axis_size("dp").bit_length() - 1
    dz_group = text_side(home, zb_img)
    for step in range(2):
        bit = levels - 1 - step
        partner_txt = partner(group_txt, "dp", bit)
        weights = tile_weights(zb_img, partner_txt, scale, bias, negative)
        dz_img = dz_img + image_side(weights, partner_txt)
        sent_back = text_side(weights, zb_img)
        dz_group = dz_group + partner(sent_back, "dp", bit)
    dz_txt = lax.psum_scatter(dz_group, "pair", scatter_dimension=0, tiled=True)
    du_img = backward(z_img, inv_img, dz_img)
    du_txt = backward(z_txt, inv_txt, dz_txt)
    contract = (((1,), (1,)), ((), ()))
    image_grads = lax.dot_general(
        du_img, image_head, contract, preferred_element_type=jnp.float32
    ).astype(jnp.bfloat16)
    text_grads = lax.dot_general(
        du_txt, text_head, contract, preferred_element_type=jnp.float32
    ).astype(jnp.bfloat16)
    head_img = text_side(image_feats, du_img)
    head_txt = text_side(text_feats, du_txt)
    shares = lax.psum_scatter(
        jnp.concatenate([head_img, head_txt], axis=1).astype(jnp.bfloat16),
        "pair",
        scatter_dimension=0,
        tiled=True,
    ).astype(jnp.float32)
    total = lax.psum(shares, "dp")
    head_grads = total / (lax.axis_size("dp") * lax.axis_size("pair"))
    return (image_grads, text_grads, head_grads)


def solution(mesh):
    in_specs = (P(("dp", "pair"), None), P(("dp", "pair"), None), P(), P(), P(), P())
    out_specs = (P(("dp", "pair"), None), P(("dp", "pair"), None), P("pair", None))
    return jax.shard_map(
        per_device, mesh=mesh, in_specs=in_specs, out_specs=out_specs, check_vma=False
    )
```

profile of v0, /device:TPU:2, one launch (start us, length us, event | category | flops | bytes accessed | tf_op | source)
XLA Modules:
  0.0 923.3 jit_solution(9715816921250055304)
XLA Ops:
  7.2 0.0 copy-start
  7.2 0.0 copy-start.18
  7.2 0.0 all-gather.2.cloned.1.call-start
  7.2 3.2 multiply_reduce_fusion.2
  10.4 1.0 copy-done.2
  11.4 0.9 multiply_convert_fusion.2
  12.4 0.0 all-gather.2.cloned.1.call-update
  12.4 0.0 reduce-scatter.5.cloned.1.call-start
  12.4 35.2 %all-gather.2.cloned.1.call-done = bf16[1024,1152]{1,0:T(8,128)(2,1)} async-done(((bf16[256,1152]{1,0:T(8,128)(2,1)}), bf16[1024,1152]{1,0:T(8,128)(2,1)}) %all-gather.2.cloned.1.call-update) | async-done | bytes 2359312 | tf_op jit(solution)/shard_map/all_gather | solution.py:58
  47.6 6.3 collective-permute-start.1
  53.9 2.4 collective-permute-start
  57.6 1.1 multiply_reduce_fusion.3
  58.7 1.1 copy-done.4
  59.8 0.1 multiply_convert_fusion.3
  59.9 97.2 %collective-permute-done.1 = bf16[1024,1152]{1,0:T(8,128)(2,1)S(1)} collective-permute-done((bf16[1024,1152]{1,0:T(8,128)(2,1)}, bf16[1024,1152]{1,0:T(8,128)(2,1)S(1)}, u32[]{:S(2)}, u32[]{:S(2)}) %collective-permute-start.1) | collective-permute-done | bytes 2359328 | tf_op jit(solution)/shard_map/ppermute | solution.py:14
  157.1 1.0 fusion.23
  158.1 0.4 copy-done.13
  158.5 3.0 fusion.28
  161.6 6.3 collective-permute-start.3
  167.9 0.0 collective-permute-done
  167.9 1.0 fusion.24
  168.9 0.4 copy-done.15
  169.3 3.0 fusion.27
  172.4 2.4 collective-permute-start.2
  174.7 2.8 fusion.25
  177.5 0.0 copy-start.17
  177.6 194.2 %collective-permute-done.3 = f32[1024,1152]{1,0:T(8,128)} collective-permute-done((f32[1024,1152]{1,0:T(8,128)}, f32[1024,1152]{1,0:T(8,128)}, u32[]{:S(2)}, u32[]{:S(2)}) %collective-permute-start.3) | collective-permute-done | bytes 4718624 | tf_op jit(solution)/shard_map/ppermute | solution.py:14
  371.8 0.0 collective-permute-done.2
  371.8 0.0 copy-done.17
  371.8 6.8 fusion.2
  378.6 0.0 reduce-scatter.5.cloned.1.call-update
  378.6 0.0 copy-start.12
  378.6 0.2 reduce-scatter.7.cloned.1.call-start
  378.8 0.0 copy-start.16
  378.9 2.8 fusion.26
  381.7 0.9 convolution_add_fusion.2
  382.6 0.4 copy-done.5
  383.0 0.1 copy-done.10
  383.1 0.8 copy-done.14
  383.9 1.0 multiply_reduce_fusion.1
  384.9 0.2 multiply_convert_fusion.1
  385.1 0.8 copy-done.19
  385.9 2.5 fusion
  388.4 43.0 %reduce-scatter.5.cloned.1.call-done = f32[256,1152]{1,0:T(8,128)} async-done(((f32[1024,1152]{1,0:T(8,128)}), f32[256,1152]{1,0:T(8,128)}) %reduce-scatter.5.cloned.1.call-update) | async-done | bytes 1179664 | tf_op jit(solution)/shard_map/reduce_scatter | solution.py:76
  431.5 2.0 multiply_reduce_fusion
  433.5 0.3 copy-done.6
  433.8 0.2 multiply_convert_fusion
  434.1 0.0 copy-start.7
  434.1 0.0 copy-start.1
  434.1 1.0 fusion.1
  435.1 1.0 copy-done.1
  436.0 2.8 pad_maximum_fusion
  438.9 8.5 copy.11
  447.4 0.0 reduce-scatter.7.cloned.1.call-update
  447.4 0.0 copy-start.8
  447.4 0.0 copy-start.21
  447.4 1.9 convolution_convert_fusion.3
  449.3 0.1 copy-done.21
  449.4 1.9 convolution_convert_fusion.2
  451.2 54.3 %reduce-scatter.7.cloned.1.call-done = bf16[288,2304]{1,0:T(8,128)(2,1)} async-done(((bf16[1152,2304]{1,0:T(8,128)(2,1)}), bf16[288,2304]{1,0:T(8,128)(2,1)}) %reduce-scatter.7.cloned.1.call-update) | async-done | bytes 1327120
  505.6 2.6 copy.12
  508.2 401.0 %all-reduce.1 = f32[288,2304]{0,1:T(8,128)} all-reduce(bf16[288,2304]{0,1:T(8,128)(2,1)} %copy.12), channel_id=1, replica_groups=mesh['dp'=64,'pair'=4] {'dp'}, use_global_device_ids=true, to_apply=%region_6.7 | all-reduce | flops 663552 | bytes 3981312 | tf_op jit(solution)/shard_map/psum | solution.py:94
  909.2 4.0 broadcast_multiply_fusion
  913.2 3.6 copy.10
  (26 shorter events, 0.1 us)
Async XLA Ops:
  7.2 50.4 %copy-start = (bf16[1152,1152]{1,0:T(8,128)(2,1)S(1)}, bf16[1152,1152]{1,0:T(8,128)(2,1)}, u32[]{:S(2)}) copy-start(bf16[1152,1152]{1,0:T(8,128)(2,1)} %param.8) | copy-start | bytes 7962628
  7.2 50.4 %copy-start.18 = (bf16[256,1152]{1,0:T(8,128)(2,1)S(1)}, bf16[256,1152]{1,0:T(8,128)(2,1)}, u32[]{:S(2)}) copy-start(bf16[256,1152]{1,0:T(8,128)(2,1)} %param.6) | copy-start | bytes 1769476
  7.2 40.4 %all-gather.2.cloned.1.call-start = ((), (), s32[]{:S(2)}) async-start(), calls=%async_computation.2 | async-start | bytes 2949120 | tf_op jit(solution)/shard_map/all_gather | solution.py:58
  10.4 1.0 copy-start.2
  12.4 419.1 %reduce-scatter.5.cloned.1.call-start = ((), (), s32[]{:S(2)}) async-start(), calls=%async_computation.3 | async-start | bytes 5898240 | tf_op jit(solution)/shard_map/reduce_scatter | solution.py:76
  47.6 109.5 %collective-permute-start.1 = (bf16[1024,1152]{1,0:T(8,128)(2,1)}, bf16[1024,1152]{1,0:T(8,128)(2,1)S(1)}, u32[]{:S(2)}, u32[]{:S(2)}) collective-permute-start(bf16[1024,1152]{1,0:T(8,128)(2,1)} %all-gather.2.cloned.1.call-done), channel_id=1, source_target_pairs={{0,64},{64,0},{4,68},{68,4},{8,72},{72,8},{12,76},{76,12},{16,80},... | collective-permute-start | bytes 7077896 | tf_op jit(solution)/shard_map/ppermute | solution.py:14
  53.9 114.0 %collective-permute-start = (bf16[1024,1152]{1,0:T(8,128)(2,1)}, bf16[1024,1152]{1,0:T(8,128)(2,1)S(1)}, u32[]{:S(2)}, u32[]{:S(2)}) collective-permute-start(bf16[1024,1152]{1,0:T(8,128)(2,1)} %all-gather.2.cloned.1.call-done), channel_id=1, source_target_pairs={{0,128},{128,0},{4,132},{132,4},{8,136},{136,8},{12,140},{140,12},... | collective-permute-start | bytes 7077896 | tf_op jit(solution)/shard_map/ppermute | solution.py:14
  58.7 1.1 copy-start.4
  157.1 1.4 copy-start.13
  158.5 3.0 copy-start.9
  161.6 210.2 %collective-permute-start.3 = (f32[1024,1152]{1,0:T(8,128)}, f32[1024,1152]{1,0:T(8,128)}, u32[]{:S(2)}, u32[]{:S(2)}) collective-permute-start(f32[1024,1152]{1,0:T(8,128)} %fusion.28), channel_id=1, source_target_pairs={{0,64},{64,0},{4,68},{68,4},{8,72},{72,8},{12,76},{76,12},{16,80},... | collective-permute-start | bytes 14155784 | tf_op jit(solution)/shard_map/ppermute | solution.py:14
  167.9 1.4 copy-start.15
  169.3 3.0 copy-start.11
  172.4 199.4 %collective-permute-start.2 = (f32[1024,1152]{1,0:T(8,128)}, f32[1024,1152]{1,0:T(8,128)}, u32[]{:S(2)}, u32[]{:S(2)}) collective-permute-start(f32[1024,1152]{1,0:T(8,128)} %fusion.27), channel_id=1, source_target_pairs={{0,128},{128,0},{4,132},{132,4},{8,136},{136,8},{12,140},{140,12},... | collective-permute-start | bytes 14155784 | tf_op jit(solution)/shard_map/ppermute | solution.py:14
  177.5 194.2 %copy-start.17 = (bf16[256,1024]{1,0:T(8,128)(2,1)}, bf16[256,1024]{1,0:T(8,128)(2,1)S(1)}, u32[]{:S(2)}) copy-start(bf16[256,1024]{1,0:T(8,128)(2,1)S(1)} %fusion.25) | copy-start | bytes 1572868
  378.6 3.1 copy-start.12
  378.6 126.9 %reduce-scatter.7.cloned.1.call-start = ((), (), s32[]{:S(2)}) async-start(), calls=%async_computation.4 | async-start | bytes 6635520
  378.8 2.8 copy-start.16
  381.7 1.3 copy-start.5
  381.7 1.4 copy-start.10
  381.7 2.2 copy-start.14
  384.9 1.1 copy-start.19
  431.5 2.0 copy-start.3
  431.5 2.3 copy-start.6
  431.5 2.6 copy-start.20
  434.1 1.0 copy-start.7
  434.1 2.0 copy-start.1
  447.4 1.9 copy-start.8
  447.4 1.9 copy-start.21
Sparse Core Ops, SparseCore 0:
  12.5 35.0 all-gather.1
  378.7 52.6 reduce-scatter.4
  447.5 57.9 reduce-scatter.6
where the time goes:
time: 924 us; the launch traced here: 923 us
  waiting for transfers between devices  424 us (46%)
  blocking collectives  401 us (43%)
  matrix products  33.7 us (4%)
  local copies, waits for them, and re-layouts  21.2 us (2%)
  starting transfers between devices  17.7 us (2%)
  between operations  15.3 us (2%)
  other arithmetic  10.4 us (1%)
    psum x1, blocking collectives, per_device(): total = lax.psum(shares, 'dp')  401 us
    ppermute x4, waiting for transfers between devices, partner(): return lax.ppermute(block, axis, route)  291 us
    unnamed x4, waiting for transfers between devices  54.4 us
    reduce_scatter x1, waiting for transfers between devices, per_device(): dz_txt = lax.psum_scatter(dz_group, 'pair', scatter_dimension=0, tiled=True)  43 us
    all_gather x1, waiting for transfers between devices, per_device(): group_txt = lax.all_gather(zb_txt, 'pair', axis=0, tiled=True)  35.2 us
    unnamed x47, local copies, waits for them, and re-layouts  21.2 us
  transfers between devices with their start and end apart: 7, of which 5 were waited for; matrix products, arithmetic and copies ran while one was open for 3% of the time, Pallas kernels for 0%

commit v1 on v0

v1 whole, which is shorter than its diff:
```python
import functools

import jax
import jax.numpy as jnp
from jax import lax
from jax.experimental import pallas as pl
from jax.experimental.pallas import tpu as pltpu
from jax.sharding import Mesh, PartitionSpec as P

ROWS = ("xh", "z", "y", "xl", "c")
X_RING = ("xh", "xl")
SWAP = [(0, 1), (1, 0)]
CROSS = [(0, 3), (3, 0), (1, 2), (2, 1)]
F32 = jnp.float32
BF16 = jnp.bfloat16
LANES_BOTH = (((1,), (1,)), ((), ()))
ROWS_BOTH = (((0,), (0,)), ((), ()))


def shape(dims, dtype):
    return jax.ShapeDtypeStruct(dims, dtype)


def local(kernel, outs, *args, scalars=0, scratch=(), mib=14):
    vmem = pl.BlockSpec(memory_space=pltpu.VMEM)
    smem = pl.BlockSpec(memory_space=pltpu.SMEM)
    many = isinstance(outs, (tuple, list))
    return pl.pallas_call(
        kernel,
        out_shape=outs,
        in_specs=[smem] * scalars + [vmem] * (len(args) - scalars),
        out_specs=[vmem] * len(outs) if many else vmem,
        scratch_shapes=scratch,
        compiler_params=pltpu.CompilerParams(vmem_limit_bytes=mib << 20),
        cost_estimate=pl.CostEstimate(flops=1000, bytes_accessed=1000, transcendentals=0),
    )(*args)


def embedding(feats, head):
    u = jnp.dot(feats, head, preferred_element_type=F32)
    inv = lax.rsqrt(jnp.sum(u * u, axis=1, keepdims=True) + 1e-06)
    return u * inv, inv


def tangent(z, inv, dz):
    return inv * (dz - z * jnp.sum(z * dz, axis=1, keepdims=True))


def embed_kernel(head_ref, feats_ref, z_ref, inv_ref, zb_ref):
    z, inv = embedding(feats_ref[...], head_ref[...])
    z_ref[...] = z
    inv_ref[...] = inv
    zb_ref[...] = z.astype(BF16)


def embed_other_kernel(head_ref, feats_ref, zb_ref):
    zb_ref[...] = embedding(feats_ref[...], head_ref[...])[0].astype(BF16)


def embed(head, feats):
    rows, wide = feats.shape
    outs = [shape((rows, wide), F32), shape((rows, 1), F32), shape((rows, wide), BF16)]
    return local(embed_kernel, outs, head, feats)


def embed_other(head, feats):
    return local(embed_other_kernel, shape(feats.shape, BF16), head, feats)


def weigh(scale, bias, txt, img_refs, w_ref, home):
    total = None
    for i, img_ref in enumerate(img_refs):
        img = img_ref[...]
        logits = scale * lax.dot_general(txt, img, LANES_BOTH, preferred_element_type=F32) + bias
        if home and i == 0:
            row_ids = lax.broadcasted_iota(jnp.int32, logits.shape, 0)
            col_ids = lax.broadcasted_iota(jnp.int32, logits.shape, 1)
            sign = jnp.where(row_ids == col_ids, 1.0, -1.0).astype(F32)
            deriv = -sign * jax.nn.sigmoid(-sign * logits)
        else:
            deriv = jax.nn.sigmoid(logits)
        w = (scale * deriv).astype(BF16)
        w_ref[i] = w
        part = jnp.dot(w, img, preferred_element_type=F32)
        total = part if total is None else total + part
    return total


def home_first_kernel(scale_ref, bias_ref, feats_ref, head_ref, *refs):
    img_refs, (zb_ref, z_ref, inv_ref, w_ref, dz_ref) = refs[:-5], refs[-5:]
    z, inv = embedding(feats_ref[...], head_ref[...])
    txt = z.astype(BF16)
    z_ref[...] = z
    inv_ref[...] = inv
    zb_ref[...] = txt
    dz_ref[...] = weigh(scale_ref[0], bias_ref[0], txt, img_refs, w_ref, True)


def home_first(scale, bias, feats, head, imgs):
    rows, wide = feats.shape
    outs = [
        shape((rows, wide), BF16),
        shape((rows, wide), F32),
        shape((rows, 1), F32),
        shape((len(imgs), rows, imgs[0].shape[0]), BF16),
        shape((rows, wide), F32),
    ]
    return local(home_first_kernel, outs, scale, bias, feats, head, *imgs, scalars=2)


def home_rest_kernel(scale_ref, bias_ref, zb_ref, z_ref, inv_ref, part_ref, *refs):
    img_refs, (w_ref, dz_ref, du_ref) = refs[:-3], refs[-3:]
    dz = part_ref[...] + weigh(scale_ref[0], bias_ref[0], zb_ref[...], img_refs, w_ref, False)
    dz_ref[...] = dz
    du_ref[...] = tangent(z_ref[...], inv_ref[...], dz).astype(BF16)


def home_rest(scale, bias, zb, z, inv, part, imgs):
    rows, wide = zb.shape
    outs = [
        shape((len(imgs), rows, imgs[0].shape[0]), BF16),
        shape((rows, wide), F32),
        shape((rows, wide), BF16),
    ]
    return local(home_rest_kernel, outs, scale, bias, zb, z, inv, part, *imgs, scalars=2)


def text_kernel(scale_ref, bias_ref, feats_ref, head_ref, *refs):
    img_refs, (zb_ref, w_ref, dz_ref, du_ref) = refs[:-4], refs[-4:]
    z, inv = embedding(feats_ref[...], head_ref[...])
    txt = z.astype(BF16)
    zb_ref[...] = txt
    dz = weigh(scale_ref[0], bias_ref[0], txt, img_refs, w_ref, False)
    dz_ref[...] = dz.astype(BF16)
    du_ref[...] = tangent(z, inv, dz).astype(BF16)


def text_block(scale, bias, feats, head, imgs):
    rows, wide = feats.shape
    block = shape((rows, wide), BF16)
    outs = [block, shape((len(imgs), rows, imgs[0].shape[0]), BF16), block, block]
    return local(text_kernel, outs, scale, bias, feats, head, *imgs, scalars=2)


def image_side_kernel(count, *refs):
    first_ref, rest_ref = refs[:2]
    w_refs, txt_refs, (keep_ref, send_ref) = refs[2 : count + 1], refs[count + 1 : -2], refs[-2:]
    for i in range(4):
        home = first_ref[i] if i < 2 else rest_ref[i - 2]
        weights = [home] + [ref[i] for ref in w_refs]
        dz = None
        for w, txt_ref in zip(weights, txt_refs):
            part = lax.dot_general(w, txt_ref[...], ROWS_BOTH, preferred_element_type=F32)
            dz = part if dz is None else dz + part
        if i % 2 == 0:
            keep_ref[i // 2] = dz
        else:
            send_ref[i // 2] = dz.astype(BF16)


def image_side(home, weights, txts):
    rows, wide = txts[0].shape
    dims = (2, rows, wide)
    return local(
        functools.partial(image_side_kernel, len(txts)),
        [shape(dims, F32), shape(dims, BF16)],
        *home,
        *weights,
        *txts,
    )


def image_tangent_kernel(keep_ref, got_ref, *refs):
    z_refs, inv_refs, (du_ref, own_ref, send_ref) = refs[:2], refs[2:4], refs[4:]
    for i in range(2):
        dz = keep_ref[i] + got_ref[i].astype(F32)
        if i == 0:
            own_ref[...] = dz
        else:
            send_ref[...] = dz.astype(BF16)
        du_ref[i] = tangent(z_refs[i][...], inv_refs[i][...], dz).astype(BF16)


def image_tangent(keep, got, zs, invs):
    dims = keep.shape[1:]
    return local(
        image_tangent_kernel,
        [shape(keep.shape, BF16), shape(dims, F32), shape(dims, BF16)],
        keep,
        got,
        *zs,
        *invs,
    )


def backward_kernel(z_ref, inv_ref, own_ref, *refs):
    dz = own_ref[...]
    for ref in refs[:-1]:
        dz = dz + ref[...].astype(F32)
    refs[-1][...] = tangent(z_ref[...], inv_ref[...], dz).astype(BF16)


def backward(z, inv, own, *parts):
    return local(backward_kernel, shape(z.shape, BF16), z, inv, own, *parts)


def head_early_kernel(count, *refs):
    total = None
    for feats_ref, du_ref in zip(refs[:count], refs[count : 2 * count]):
        part = lax.dot_general(
            feats_ref[...], du_ref[...], ROWS_BOTH, preferred_element_type=F32
        )
        total = part if total is None else total + part
    refs[-1][...] = total


def head_early(feats, dus):
    depth, wide = feats[0].shape[1], dus[0].shape[1]
    return local(
        functools.partial(head_early_kernel, len(feats)),
        shape((depth, wide), F32),
        *feats,
        *dus,
        mib=20,
    )


def head_late_kernel(core_ref, *refs):
    early, (keep_ref, send_ref, held) = refs[:-3], refs[-3:]
    if len(early[1].shape) == len(early[2].shape):
        total = early[2][...] + lax.dot_general(
            early[0][...], early[1][...], ROWS_BOTH, preferred_element_type=F32
        )
    else:
        du_ref = early[-1]
        total = None
        for i, feats_ref in enumerate(early[:-1]):
            part = lax.dot_general(
                feats_ref[...], du_ref[i], ROWS_BOTH, preferred_element_type=F32
            )
            total = part if total is None else total + part
    rows = held.shape[2]
    for k in range(4):
        held[k % 2, k // 2] = total[k * rows : (k + 1) * rows]
    core = core_ref[0]
    keep_ref[...] = held[core]
    send_ref[...] = held[1 - core].astype(BF16)


def head_late(core, *args):
    depth = args[0].shape[1]
    wide = args[-1].shape[-1]
    dims = (2, depth // 4, wide)
    return local(
        head_late_kernel,
        [shape(dims, F32), shape(dims, BF16)],
        core,
        *args,
        scalars=1,
        scratch=[pltpu.VMEM((2,) + dims, F32)],
        mib=20,
    )


def split_x_kernel(keep_ref, got_ref, out_ref):
    rows = out_ref.shape[1]
    for k in range(out_ref.shape[0]):
        at = pl.ds(k % 2 * rows, rows)
        out_ref[k] = (keep_ref[k // 2, at] + got_ref[k // 2, at].astype(F32)).astype(BF16)


def split_x(keep, got):
    _, rows, wide = keep.shape
    return local(split_x_kernel, shape((4, rows // 2, wide), BF16), keep, got)


def split_y_kernel(me_ref, keep_ref, got_ref, *refs):
    outs, held = refs[:-1], refs[-1]
    count, blocks, rows = held.shape[:3]
    total = (keep_ref[...] + got_ref[...].astype(F32)).astype(BF16)
    for b in range(blocks):
        for k in range(count):
            at = (b % 2 * count + k) * rows
            held[k, b] = total[b // 2, at : at + rows]
    for s, out_ref in enumerate(outs):
        out_ref[...] = held[lax.rem(me_ref[0] + s, count)]


def split_y(me, keep, got):
    count = lax.axis_size("y")
    _, rows, wide = keep.shape
    part = (4, rows // 2 // count, wide)
    return local(
        split_y_kernel,
        [shape(part, BF16)] * count,
        me,
        keep,
        got,
        scalars=1,
        scratch=[pltpu.VMEM((count,) + part, BF16)],
    )


def sum_kernel(*refs):
    total = refs[0][...].astype(F32)
    for ref in refs[1:-1]:
        total = total + ref[...].astype(F32)
    refs[-1][...] = total.astype(BF16)


def add_up(*parts):
    return local(sum_kernel, shape(parts[0].shape, BF16), *parts)


def sum_first_kernel(in_ref, out_ref):
    total = in_ref[0].astype(F32)
    for k in range(1, in_ref.shape[0]):
        total = total + in_ref[k].astype(F32)
    out_ref[...] = total.astype(BF16)


def add_first(parts):
    return local(sum_first_kernel, shape(parts.shape[1:], BF16), parts)


def sum_split_kernel(me_ref, in_ref, *refs):
    outs, held = refs[:-1], refs[-1]
    total = in_ref[0].astype(F32)
    for k in range(1, in_ref.shape[0]):
        total = total + in_ref[k].astype(F32)
    total = total.astype(BF16)
    count, rows = held.shape[:2]
    for k in range(count):
        held[k] = total[k * rows : (k + 1) * rows]
    for s, out_ref in enumerate(outs):
        out_ref[...] = held[lax.rem(me_ref[0] + s, count)]


def add_split(me, parts):
    count = lax.axis_size("y")
    _, rows, wide = parts.shape
    part = (rows // count, wide)
    return local(
        sum_split_kernel,
        [shape(part, BF16)] * count,
        me,
        parts,
        scalars=1,
        scratch=[pltpu.VMEM((count,) + part, BF16)],
    )


def split_z_kernel(*refs):
    out_ref, ins = refs[-1], refs[:-1]
    both = jnp.concatenate([ref[...] for ref in ins], axis=0)
    rows = out_ref.shape[1]
    for k in range(out_ref.shape[0]):
        out_ref[k] = both[k * rows : (k + 1) * rows]


def split_z(*parts):
    count = lax.axis_size("z")
    rows, wide = parts[0].shape
    dims = (count, len(parts) * rows // count, wide)
    return local(split_z_kernel, shape(dims, BF16), *parts)


def sum_spread_kernel(in_ref, out_ref):
    total = in_ref[0].astype(F32)
    for k in range(1, in_ref.shape[0]):
        total = total + in_ref[k].astype(F32)
    for k in range(out_ref.shape[0]):
        out_ref[k] = total.astype(BF16)


def sum_spread(parts):
    return local(sum_spread_kernel, shape(parts.shape, BF16), parts)


def join_z_kernel(in_ref, out_ref):
    both = jnp.concatenate([in_ref[k] for k in range(in_ref.shape[0])], axis=0)
    for k in range(out_ref.shape[0]):
        out_ref[k] = both


def join_z(pieces, copies):
    count, rows, wide = pieces.shape
    return local(join_z_kernel, shape((copies, count * rows, wide), BF16), pieces)


def finish_kernel(part, in_ref, out_ref):
    count, both, wide = in_ref.shape
    rows = both // 2
    for k in range(count):
        for j in range(2):
            out_ref[k * rows : (k + 1) * rows, j * wide : (j + 1) * wide] = (
                in_ref[k, j * rows : (j + 1) * rows].astype(F32) * part
            )


def finish(part, pieces):
    count, both, wide = pieces.shape
    return local(
        functools.partial(finish_kernel, part), shape((count * both // 2, 2 * wide), F32), pieces
    )


def grads_kernel(du_ref, head_ref, out_ref):
    out = lax.dot_general(du_ref[...], head_ref[...], LANES_BOTH, preferred_element_type=F32)
    out_ref[...] = out.astype(BF16)


def feature_grads(du, head):
    return local(grads_kernel, shape(du.shape, BF16), du, head)


def far_z(block):
    count = lax.axis_size("z")
    return lax.ppermute(block, "z", [(i, (i + count // 2) % count) for i in range(count)])


def along_y(parts):
    count = lax.axis_size("y")
    return [parts[0]] + [
        lax.ppermute(part, "y", [(i, (i + s) % count) for i in range(count)])
        for s, part in enumerate(parts)
        if s > 0
    ]


def swap(block, axes):
    return lax.all_to_all(block, axes, 0, 0, tiled=True)


def per_device(image_feats, text_feats, image_head, text_head, scale, bias):
    rows, depth = image_feats.shape
    core = lax.axis_index("c").astype(jnp.int32).reshape(1)
    me_y = lax.axis_index("y").astype(jnp.int32).reshape(1)

    def unit(work):
        def nothing():
            return jax.tree.map(lambda s: jnp.zeros(s.shape, s.dtype), jax.eval_shape(work))

        return lax.cond(scale[0] > 0, work, nothing)

    far = far_z(text_feats)

    def early_unit():
        near = lax.ppermute(text_feats, X_RING, CROSS)
        next_feats = lax.ppermute(image_feats, "xl", SWAP)
        core_feats = lax.ppermute(image_feats, "c", SWAP)
        z_img, inv_img, zb_img = embed(image_head, image_feats)
        zb_core = embed_other(image_head, core_feats)
        zb_txt, z_txt, inv_txt, w_first, part = home_first(
            scale, bias, text_feats, text_head, [zb_img, zb_core]
        )
        near, next_feats, part = lax.optimization_barrier((near, next_feats, part))
        next_core_feats = lax.ppermute(next_feats, "c", SWAP)
        z_next, inv_next, zb_next = embed(image_head, next_feats)
        zb_next_core = embed_other(image_head, next_core_feats)
        w_rest, dz_txt, du_home = home_rest(
            scale, bias, zb_txt, z_txt, inv_txt, part, [zb_next, zb_next_core]
        )
        imgs = [zb_img, zb_core, zb_next, zb_next_core]
        zb_near, w_near, back_near, du_near = text_block(scale, bias, near, text_head, imgs)
        head_txt = head_early([text_feats, near], [du_home, du_near])
        return dict(
            imgs=imgs, next_feats=next_feats, z_img=z_img, inv_img=inv_img, z_next=z_next, inv_next=inv_next,
            zb_txt=zb_txt, z_txt=z_txt, inv_txt=inv_txt, home=[w_first, w_rest], dz_txt=dz_txt,
            zb_near=zb_near, w_near=w_near, back_near=back_near, head_txt=head_txt,
        )

    got = unit(early_unit)
    far, head_txt = lax.optimization_barrier((far, got["head_txt"]))
    zb_far, w_far, back_far, du_far = text_block(scale, bias, far, text_head, got["imgs"])
    back_far = far_z(back_far)
    back_near = lax.ppermute(got["back_near"], X_RING, CROSS)
    keep, send = head_late(core, far, du_far, head_txt)
    txt = split_y(me_y, keep, lax.ppermute(send, "c", SWAP))
    txt, w_far = lax.optimization_barrier((txt, w_far))
    txt = along_y(txt)

    def image_unit():
        keep, send = image_side(
            got["home"], [got["w_near"], w_far], [got["zb_txt"], got["zb_near"], zb_far]
        )
        du_part, own, send = image_tangent(
            keep,
            lax.ppermute(send, "c", SWAP),
            [got["z_img"], got["z_next"]],
            [got["inv_img"], got["inv_next"]],
        )
        keep, part = head_late(core, image_feats, got["next_feats"], du_part)
        return own, send, split_x(keep, lax.ppermute(part, "c", SWAP))

    own, send, img = unit(image_unit)
    img = swap(img, ("xl", "xh"))
    txt = add_up(*txt)
    txt, img = lax.optimization_barrier((txt, img))
    img = add_split(me_y, img)

    def second_unit():
        both = along_y(img)
        return split_z(add_up(*both), add_first(swap(txt, ("xl", "xh"))))

    piece = unit(second_unit)
    back_img = lax.ppermute(send, "xl", SWAP)
    piece, back_far, back_near = lax.optimization_barrier((piece, back_far, back_near))
    piece = swap(piece, "z")
    piece, back_img, back_far, back_near = lax.optimization_barrier(
        (piece, back_img, back_far, back_near)
    )
    du_img = backward(got["z_img"], got["inv_img"], own, back_img)
    du_txt = backward(got["z_txt"], got["inv_txt"], got["dz_txt"], back_near, back_far)
    image_grads = feature_grads(du_img, image_head)
    text_grads = feature_grads(du_txt, text_head)

    piece = join_z(swap(sum_spread(piece), "z"), lax.axis_size(("xh", "y")))
    parts = lax.axis_size(("xh", "z", "y")) * lax.axis_size(("xl", "c"))
    head_grads = finish(1.0 / parts, swap(piece, ("xh", "y")))
    return (image_grads, text_grads, head_grads)


def solution(mesh):
    fine = Mesh(mesh.devices.reshape(2, 8, 4, 2, 2), ROWS)
    split = P(ROWS, None)
    return jax.shard_map(
        per_device,
        mesh=fine,
        in_specs=(split, split, P(), P(), P(), P()),
        out_specs=(split, split, P(("xl", "c"), None)),
        check_vma=False,
    )
```

time: 924 us -> 167 us (0.18)
  blocking collectives: 401 us -> 13.2 us
  waiting for transfers between devices: 424 us -> 46.8 us
  Pallas kernels: 0 us -> 57.7 us
  matrix products: 33.7 us -> 0 us
  starting transfers between devices: 17.7 us -> 44.4 us
  local copies, waits for them, and re-layouts: 21.2 us -> 1.37 us
  between operations: 15.3 us -> 2.09 us
  other arithmetic: 10.4 us -> 0 us
    psum x1 -> x0, blocking collectives: 401 us -> none  [per_device(): total = lax.psum(shares, 'dp')]
    ppermute x4 -> x17, waiting for transfers between devices: 291 us -> 39 us  [the longest x6 16.9 us: along_y(): lax.ppermute(part, 'y', [(i, (i + s) % count) for i in range(count)])]
    pallas_call x0 -> x27, Pallas kernels: none -> 57.7 us  [local(): pl.pallas_call(kernel, out_shape=outs, in_specs=[smem] * scalars + [vmem]...]
    unnamed x4 -> x0, waiting for transfers between devices: 54.4 us -> none
    reduce_scatter x1 -> x0, waiting for transfers between devices: 43 us -> none  [per_device(): dz_txt = lax.psum_scatter(dz_group, 'pair', scatter_dimension=0, tiled=True)]
    all_gather x1 -> x0, waiting for transfers between devices: 35.2 us -> none  [per_device(): group_txt = lax.all_gather(zb_txt, 'pair', axis=0, tiled=True)]
    dot_general x15 -> x0, matrix products: 33.7 us -> none  [the longest x5 16.3 us: text_side(): lax.dot_general(weights, img, (((0,), (0,)), ((), ())), preferred_element...]
    unnamed x47 -> x28, local copies, waits for them, and re-layouts: 21.2 us -> 0.32 us
  transfers between devices with their start and end apart: 7 -> 21, of which waited for: 5 -> 13; matrix products, arithmetic and copies ran while one was open for 3% -> 0% of each run, Pallas kernels for 0% -> 21%
where the time goes in v1:
time: 167 us; the launch traced here: 166 us
  Pallas kernels  57.7 us (35%)
  waiting for transfers between devices  46.8 us (28%)
  starting transfers between devices  44.4 us (27%)
  blocking collectives  13.2 us (8%)
  between operations  2.09 us (1%)
    pallas_call x27, Pallas kernels, local(): pl.pallas_call(kernel, out_shape=outs, in_specs=[smem] * scalars + [vmem]...  57.7 us
    all_to_all x4, starting transfers between devices, swap(): return lax.all_to_all(block, axes, 0, 0, tiled=True)  19.5 us
    ppermute x6, waiting for transfers between devices, along_y(): lax.ppermute(part, 'y', [(i, (i + s) % count) for i in range(count)])  16.9 us
    all_to_all x1, blocking collectives, swap(): return lax.all_to_all(block, axes, 0, 0, tiled=True)  13.2 us
    ppermute x6, starting transfers between devices, along_y(): lax.ppermute(part, 'y', [(i, (i + s) % count) for i in range(count)])  11 us
    ppermute x1, waiting for transfers between devices, per_device(): back_img = lax.ppermute(send, 'xl', SWAP)  10.1 us
    all_to_all x4, waiting for transfers between devices, swap(): return lax.all_to_all(block, axes, 0, 0, tiled=True)  7.76 us
    ppermute x2, starting transfers between devices, far_z(): lax.ppermute(block, 'z', [(i, (i + count // 2) % count) for i in range(co...  7.3 us
  transfers between devices with their start and end apart: 21, of which 13 were waited for; matrix products, arithmetic and copies ran while one was open for 0% of the time, Pallas kernels for 21%

profile of v1, /device:TPU:2, one launch (start us, length us, event | category | flops | bytes accessed | tf_op | source)
XLA Modules:
  0.0 166.0 jit_solution(17334296868892243005)
XLA Ops:
  0.6 7.3 %collective-permute-start.9 = (bf16[256,1152]{1,0:T(8,128)(2,1)}, bf16[256,1152]{1,0:T(8,128)(2,1)S(1)}, u32[]{:S(2)}, u32[]{:S(2)}) collective-permute-start(bf16[256,1152]{1,0:T(8,128)(2,1)} %param.13), channel_id=1, source_target_pairs={{0,64},{16,80},{32,96},{48,112},{64,0},{80,16},{96,32},{112,48},{1... | collective-permute-start | bytes 1769480 | tf_op jit(solution)/shard_map/ppermute | solution.py:419
  9.2 31.7 %conditional.3 = (bf16[256,1152]{1,0:T(8,128)(2,1)}, f32[256,1152]{1,0:T(8,128)}, f32[1152,1152]{1,0:T(8,128)S(1)}, bf16[2,256,256]{2,1,0:T(8,128)(2,1)}, bf16[2...) conditional(s32[]{:T(128)} %bitcast, () %tuple.36, ...), branch_computations={%region_0.0_spmd, %region_1.0_spmd} | conditional | flops 8000 | bytes 61354524 | solution.py:444
  9.2 0.1 collective-permute-start.2
  9.3 1.6 collective-permute-start
  10.9 1.8 %collective-permute-start.1 = (bf16[256,1152]{1,0:T(8,128)(2,1)}, bf16[256,1152]{1,0:T(8,128)(2,1)S(1)}, u32[]{:S(2)}, u32[]{:S(2)}) collective-permute-start(bf16[256,1152]{1,0:T(8,128)(2,1)} %get-tuple-element.56.feats_ref), channel_id=1, source_target_pairs={{0,2},{2,0},{1,3},{3,1},{4,6},{6,4},{5,7},{7,5},{8,10},{10,8},{9,1... | collective-permute-start | bytes 1769480 | tf_op jit(solution)/shard_map/cond/branch_1_fun/ppermute | solution.py:450
  12.7 4.2 %branch_1_fun.15 = (f32[256,1152]{1,0:T(8,128)}, f32[256,1]{1,0:T(8,128)}, bf16[256,1152]{1,0:T(8,128)(2,1)S(1)}) custom-call(bf16[1152,1152]{1,0:T(8,128)(2,1)} %get-tuple-element.58.head_ref, bf16[256,1152]{1,0:T(8,128)(2,1)} %get-tuple-element.56.feats_ref), custom_call_target="tpu_custom_call" | custom-call | flops 1000 | bytes 1000 | tf_op jit(solution)/shard_map/cond/branch_1_fun/pallas_call | solution.py:28
  17.0 1.1 branch_1_fun.16.refs_1_
  18.1 0.8 copy-done.3
  18.9 0.2 copy-done.21
  19.1 3.6 %branch_1_fun.17 = (bf16[256,1152]{1,0:T(8,128)(2,1)S(1)}, f32[256,1152]{1,0:T(8,128)S(1)}, f32[256,1]{1,0:T(8,128)S(1)}, bf16[2,256,256]{2,1,0:T(8,128)(2,1)}, f32[256,1152]{1,0:T(8,128)S(1)}) custom-call(f32[1]{0:T(128)} %get-tuple-element.44.scale_ref, f32[1]{0:T(128)} %get-tuple-element.54.bias_ref, bf16[256,1152]{1,0:T(8,128)(2,1)S(1)} %copy-done.21, ...), custom_call_target="tpu_custom_call" | custom-call | flops 1000 | bytes 1000 | tf_op jit(solution)/shard_map/cond/branch_1_fun/pallas_call | solution.py:28
  22.8 2.5 %collective-permute-done.feats_ref.refs_1_ = bf16[256,1152]{1,0:T(8,128)(2,1)S(1)} collective-permute-done((bf16[256,1152]{1,0:T(8,128)(2,1)}, bf16[256,1152]{1,0:T(8,128)(2,1)S(1)}, u32[]{:S(2)}, u32[]{:S(2)}) %collective-permute-start) | collective-permute-done | bytes 589856 | tf_op jit(solution)/shard_map/cond/branch_1_fun/ppermute | solution.py:449
  25.3 1.3 collective-permute-done.1.feats_ref
  26.6 2.3 %branch_1_fun.18 = (f32[256,1152]{1,0:T(8,128)}, f32[256,1]{1,0:T(8,128)}, bf16[256,1152]{1,0:T(8,128)(2,1)S(1)}) custom-call(bf16[1152,1152]{1,0:T(8,128)(2,1)S(1)} %copy-done.1, bf16[256,1152]{1,0:T(8,128)(2,1)S(1)} %collective-permute-done.1.feats_ref), custom_call_target="tpu_custom_call" | custom-call | flops 1000 | bytes 1000 | tf_op jit(solution)/shard_map/cond/branch_1_fun/pallas_call | solution.py:28
  28.9 1.1 branch_1_fun.19.refs_3_.refs_1_
  30.0 5.4 %branch_1_fun.20 = (bf16[256,1152]{1,0:T(8,128)(2,1)}, bf16[4,256,256]{2,1,0:T(8,128)(2,1)}, bf16[256,1152]{1,0:T(8,128)(2,1)}, bf16[256,1152]{1,0:T(8,128)(2,1)S(1)}) custom-call(f32[1]{0:T(128)} %get-tuple-element.44.scale_ref, f32[1]{0:T(128)} %get-tuple-element.54.bias_ref, bf16[256,1152]{1,0:T(8,128)(2,1)S(1)} %collective-permute-done.feats_ref.refs_1_, ...), custom_call_target="tpu_custom_call" | custom-call | flops 1000 | bytes 1000 | tf_op jit(solution)/shard_map/cond/branch_1_fun/pallas_call | solution.py:28
  35.5 3.4 %branch_1_fun.21 = (bf16[2,256,256]{2,1,0:T(8,128)(2,1)}, f32[256,1152]{1,0:T(8,128)}, bf16[256,1152]{1,0:T(8,128)(2,1)S(1)}) custom-call(f32[1]{0:T(128)} %get-tuple-element.44.scale_ref, f32[1]{0:T(128)} %get-tuple-element.54.bias_ref, bf16[256,1152]{1,0:T(8,128)(2,1)S(1)} %get-tuple-element.250.zb_ref, f32[256,1152]{1,0:T(8,128)S(1)} %get-tuple-element.248.z_ref, ...), custom_call_target="tpu_custom_call" | custom-call | flops 1000 | bytes 1000 | tf_op jit(solution)/shard_map/cond/branch_1_fun/pallas_call | solution.py:28
  39.0 1.7 %branch_1_fun.22 = f32[1152,1152]{1,0:T(8,128)S(1)} custom-call(bf16[256,1152]{1,0:T(8,128)(2,1)S(1)} %copy-done.21, bf16[256,1152]{1,0:T(8,128)(2,1)S(1)} %collective-permute-done.feats_ref.refs_1_, bf16[256,1152]{1,0:T(8,128)(2,1)S(1)} %get-tuple-element.70.refs_2_, bf16[256,1152]{1,0:T(8,128)(2,1)S(1)} %get-tuple-element.71.refs_3_), custom_call_target="tpu_custom_call" | custom-call | flops 1000 | bytes 1000 | tf_op jit(solution)/shard_map/cond/branch_1_fun/pallas_call | solution.py:28
  41.0 5.9 %shard_map.85 = (bf16[256,1152]{1,0:T(8,128)(2,1)}, bf16[4,256,256]{2,1,0:T(8,128)(2,1)}, bf16[256,1152]{1,0:T(8,128)(2,1)}, bf16[256,1152]{1,0:T(8,128)(2,1)S(1)}) custom-call(f32[1]{0:T(128)S(6)} %copy.55.scale_ref, f32[1]{0:T(128)S(6)} %copy.56.bias_ref, bf16[256,1152]{1,0:T(8,128)(2,1)S(1)} %collective-permute-done.9.feats_ref.refs_0_, ...), custom_call_target="tpu_custom_call" | custom-call | flops 1000 | bytes 1000 | tf_op jit(solution)/shard_map/pallas_call | solution.py:28
  46.8 2.4 %shard_map.86 = (f32[2,288,1152]{2,1,0:T(8,128)S(1)}, bf16[2,288,1152]{2,1,0:T(8,128)(2,1)}) custom-call(s32[1]{0:T(128)} %bitcast.2.core_ref, bf16[256,1152]{1,0:T(8,128)(2,1)S(1)} %collective-permute-done.9.feats_ref.refs_0_, bf16[256,1152]{1,0:T(8,128)(2,1)S(1)} %get-tuple-element.172.refs_1_, f32[1152,1152]{1,0:T(8,128)S(1)} %get-tuple-element.173.refs_2_), custom_call_target="tpu_custom_call" | custom-call | flops 1000 | bytes 1000 | tf_op jit(solution)/shard_map/pallas_call | solution.py:28
  49.2 0.5 collective-permute-start.10
  49.7 3.0 %collective-permute-done.10.got_ref = bf16[2,288,1152]{2,1,0:T(8,128)(2,1)} collective-permute-done((bf16[2,288,1152]{2,1,0:T(8,128)(2,1)}, bf16[2,288,1152]{2,1,0:T(8,128)(2,1)}, u32[]{:S(2)}, u32[]{:S(2)}) %collective-permute-start.10) | collective-permute-done | bytes 1327136 | tf_op jit(solution)/shard_map/ppermute | solution.py:479
  52.8 3.2 %shard_map.87 = (bf16[4,36,1152]{2,1,0:T(8,128)(2,1)S(1)}, bf16[4,36,1152]{2,1,0:T(8,128)(2,1)}, bf16[4,36,1152]{2,1,0:T(8,128)(2,1)}, bf16[4,36,1152]{2,1,0:T(8,128)(2,1)}) custom-call(s32[1]{0:T(128)} %bitcast.1.me_ref, f32[2,288,1152]{2,1,0:T(8,128)S(1)} %get-tuple-element.174.keep_ref, bf16[2,288,1152]{2,1,0:T(8,128)(2,1)} %collective-permute-done.10.got_ref), custom_call_target="tpu_custom_call" | custom-call | flops 1000 | bytes 1000 | tf_op jit(solution)/shard_map/pallas_call | solution.py:28
  56.0 14.9 %conditional.4 = (f32[256,1152]{1,0:T(8,128)}, bf16[256,1152]{1,0:T(8,128)(2,1)}, bf16[4,144,1152]{2,1,0:T(8,128)(2,1)}) conditional(s32[]{:T(128)} %bitcast, () %tuple.38, (bf16[2,256,256]{2,1,0:T(8,128)(2,1)S(1)}, bf16[2,256,256]{2,1,0:T(8,128)(2,1)}, bf16[4,256,256]{2,1,0:T(8,128)(2,1)}, bf16[4,256,256]{2,1,0:T(8,128)(2,1)}, ...), branch_computations={%region_2.0_spmd, %region_3.0_spmd} | conditional | flops 4000 | bytes 12390436 | solution.py:444
  56.1 3.9 %branch_1_fun.23 = (f32[2,256,1152]{2,1,0:T(8,128)S(1)}, bf16[2,256,1152]{2,1,0:T(8,128)(2,1)S(1)}) custom-call(bf16[2,256,256]{2,1,0:T(8,128)(2,1)S(1)} %get-tuple-element.80.refs_0_, bf16[2,256,256]{2,1,0:T(8,128)(2,1)} %get-tuple-element.81.refs_1_, bf16[4,256,256]{2,1,0:T(8,128)(2,1)} %get-tuple-element.82.refs_2_, ...), custom_call_target="tpu_custom_call" | custom-call | flops 1000 | bytes 1000 | tf_op jit(solution)/shard_map/cond/branch_1_fun/pallas_call | solution.py:28
  59.9 0.5 collective-permute-start.4
  60.4 2.5 %collective-permute-done.4.got_ref = bf16[2,256,1152]{2,1,0:T(8,128)(2,1)S(1)} collective-permute-done((bf16[2,256,1152]{2,1,0:T(8,128)(2,1)S(1)}, bf16[2,256,1152]{2,1,0:T(8,128)(2,1)S(1)}, u32[]{:S(2)}, u32[]{:S(2)}) %collective-permute-start.4) | collective-permute-done | bytes 1179680 | tf_op jit(solution)/shard_map/cond/branch_1_fun/ppermute | solution.py:489
  62.9 1.5 branch_1_fun.24
  64.4 2.0 %branch_1_fun.25 = (f32[2,288,1152]{2,1,0:T(8,128)S(1)}, bf16[2,288,1152]{2,1,0:T(8,128)(2,1)S(1)}) custom-call(s32[1]{0:T(128)} %get-tuple-element.95.core_ref, bf16[256,1152]{1,0:T(8,128)(2,1)S(1)} %copy-done.20, bf16[256,1152]{1,0:T(8,128)(2,1)S(1)} %get-tuple-element.97.refs_1_, bf16[2,256,1152]{2,1,0:T(8,128)(2,1)S(1)} %get-tuple-element.98.refs_2_), custom_call_target="tpu_custom_call" | custom-call | flops 1000 | bytes 1000 | tf_op jit(solution)/shard_map/cond/branch_1_fun/pallas_call | solution.py:28
  66.5 0.5 collective-permute-start.5
  66.9 2.7 %collective-permute-done.5.got_ref = bf16[2,288,1152]{2,1,0:T(8,128)(2,1)S(1)} collective-permute-done((bf16[2,288,1152]{2,1,0:T(8,128)(2,1)S(1)}, bf16[2,288,1152]{2,1,0:T(8,128)(2,1)S(1)}, u32[]{:S(2)}, u32[]{:S(2)}) %collective-permute-start.5) | collective-permute-done | bytes 1327136 | tf_op jit(solution)/shard_map/cond/branch_1_fun/ppermute | solution.py:494
  69.6 1.3 branch_1_fun.26
  70.9 5.4 %all-to-all-start.1 = ((bf16[4,144,1152]{2,1,0:T(8,128)(2,1)}), bf16[4,144,1152]{2,1,0:T(8,128)(2,1)S(1)}, u32[]{:S(2)}, u32[]{:S(2)}) async-start(bf16[4,144,1152]{2,1,0:T(8,128)(2,1)} %get-tuple-element.193), calls=%async_computation.1 | async-start | bytes 2654208 | tf_op jit(solution)/shard_map/all_to_all | solution.py:432
  76.3 1.6 collective-permute-start.11
  77.9 2.9 %collective-permute-start.12 = (bf16[4,36,1152]{2,1,0:T(8,128)(2,1)}, bf16[4,36,1152]{2,1,0:T(8,128)(2,1)S(1)}, u32[]{:S(2)}, u32[]{:S(2)}) collective-permute-start(bf16[4,36,1152]{2,1,0:T(8,128)(2,1)} %get-tuple-element.191), channel_id=1, source_target_pairs={{0,8},{4,12},{8,0},{12,4},{1,9},{5,13},{9,1},{13,5},{2,10},{6,14},... | collective-permute-start | bytes 995336 | tf_op jit(solution)/shard_map/ppermute | solution.py:425
  80.8 1.3 collective-permute-start.13
  82.1 1.5 collective-permute-start.15
  83.6 4.7 %collective-permute-done.11.refs_1_ = bf16[4,36,1152]{2,1,0:T(8,128)(2,1)S(1)} collective-permute-done((bf16[4,36,1152]{2,1,0:T(8,128)(2,1)}, bf16[4,36,1152]{2,1,0:T(8,128)(2,1)S(1)}, u32[]{:S(2)}, u32[]{:S(2)}) %collective-permute-start.11) | collective-permute-done | bytes 331808 | tf_op jit(solution)/shard_map/ppermute | solution.py:425
  88.4 9.1 %collective-permute-done.12.refs_2_ = bf16[4,36,1152]{2,1,0:T(8,128)(2,1)S(1)} collective-permute-done((bf16[4,36,1152]{2,1,0:T(8,128)(2,1)}, bf16[4,36,1152]{2,1,0:T(8,128)(2,1)S(1)}, u32[]{:S(2)}, u32[]{:S(2)}) %collective-permute-start.12) | collective-permute-done | bytes 331808 | tf_op jit(solution)/shard_map/ppermute | solution.py:425
  97.4 0.9 shard_map.88
  98.4 1.1 shard_map.89
  99.5 15.0 %conditional.5 = (bf16[8,9,1152]{2,1,0:T(8,128)(2,1)}) conditional(s32[]{:T(128)} %bitcast, () %tuple.42, (bf16[36,1152]{1,0:T(8,128)(2,1)}, bf16[36,1152]{1,0:T(8,128)(2,1)}, bf16[36,1152]{1,0:T(8,128)(2,1)}, bf16[36,1152]{1,0:T(8,128)(2,1)}, bf16[4,36,1152]{2,1,0:T(8,128)(2,1)}) %tuple.44), branch_computations={%region_4.0_spmd, %region_5.0_spmd} | conditional | flops 3000 | bytes 2067544 | solution.py:444
  99.5 4.9 %all-to-all-start = ((bf16[4,36,1152]{2,1,0:T(8,128)(2,1)}), bf16[4,36,1152]{2,1,0:T(8,128)(2,1)S(1)}, u32[]{:S(2)}, u32[]{:S(2)}) async-start(bf16[4,36,1152]{2,1,0:T(8,128)(2,1)} %get-tuple-element.105), calls=%async_computation | async-start | bytes 737280 | tf_op jit(solution)/shard_map/cond/branch_1_fun/all_to_all | solution.py:432
  104.4 1.1 collective-permute-start.6
  105.5 2.4 %collective-permute-start.7 = (bf16[36,1152]{1,0:T(8,128)(2,1)}, bf16[36,1152]{1,0:T(8,128)(2,1)S(1)}, u32[]{:S(2)}, u32[]{:S(2)}) collective-permute-start(bf16[36,1152]{1,0:T(8,128)(2,1)} %get-tuple-element.103), channel_id=1, source_target_pairs={{0,8},{4,12},{8,0},{12,4},{1,9},{5,13},{9,1},{13,5},{2,10},{6,14},... | collective-permute-start | bytes 248840 | tf_op jit(solution)/shard_map/cond/branch_1_fun/ppermute | solution.py:425
  107.9 1.7 %collective-permute-start.8 = (bf16[36,1152]{1,0:T(8,128)(2,1)}, bf16[36,1152]{1,0:T(8,128)(2,1)S(1)}, u32[]{:S(2)}, u32[]{:S(2)}) collective-permute-start(bf16[36,1152]{1,0:T(8,128)(2,1)} %get-tuple-element.104), channel_id=1, source_target_pairs={{0,12},{4,0},{8,4},{12,8},{1,13},{5,1},{9,5},{13,9},{2,14},{6,2},{... | collective-permute-start | bytes 248840 | tf_op jit(solution)/shard_map/cond/branch_1_fun/ppermute | solution.py:425
  109.6 1.5 collective-permute-done.6.refs_1_
  111.1 1.0 collective-permute-done.7.refs_2_
  112.1 0.6 collective-permute-done.8.refs_3_
  112.7 0.9 branch_1_fun.27.refs_0_
  113.7 0.8 branch_1_fun.29
  114.5 0.2 collective-permute-start.16
  114.7 3.4 %all-to-all-start.2 = ((bf16[8,9,1152]{2,1,0:T(8,128)(2,1)}), bf16[8,9,1152]{2,1,0:T(8,128)(2,1)S(1)}, u32[]{:S(2)}, u32[]{:S(2)}) async-start(bf16[8,9,1152]{2,1,0:T(8,128)(2,1)} %get-tuple-element.257), calls=%async_computation.2 | async-start | bytes 589824 | tf_op jit(solution)/shard_map/all_to_all | solution.py:432
  118.1 10.1 %collective-permute-done.16.refs_0_ = bf16[256,1152]{1,0:T(8,128)(2,1)S(1)} collective-permute-done((bf16[256,1152]{1,0:T(8,128)(2,1)S(1)}, bf16[256,1152]{1,0:T(8,128)(2,1)S(1)}, u32[]{:S(2)}, u32[]{:S(2)}) %collective-permute-start.16) | collective-permute-done | bytes 589856 | tf_op jit(solution)/shard_map/ppermute | solution.py:507
  128.2 1.4 all-to-all-done.2.in_ref
  129.6 13.2 %all_to_all.24.in_ref = bf16[8,9,1152]{2,1,0:T(8,128)(2,1)S(1)} all-to-all(bf16[8,9,1152]{2,1,0:T(8,128)(2,1)S(1)} %shard_map.94), channel_id=1, replica_groups=mesh['xh'=2,'z'=8,'y'=4,'xl'=2,'c'=2] {'z'}, dimensions={0} | all-to-all | bytes 331776 | tf_op jit(solution)/shard_map/all_to_all | solution.py:432
  142.8 1.2 shard_map.95
  144.0 5.8 %all-to-all-start.4 = ((bf16[8,72,1152]{2,1,0:T(8,128)(2,1)}), bf16[8,72,1152]{2,1,0:T(8,128)(2,1)S(1)}, u32[]{:S(2)}, u32[]{:S(2)}) async-start(bf16[8,72,1152]{2,1,0:T(8,128)(2,1)} %shard_map.95), calls=%async_computation.4 | async-start | bytes 2654208 | tf_op jit(solution)/shard_map/all_to_all | solution.py:432
  149.8 2.2 %shard_map.92.du_ref = bf16[256,1152]{1,0:T(8,128)(2,1)S(1)} custom-call(f32[256,1152]{1,0:T(8,128)} %get-tuple-element.207.z_ref, f32[256,1]{1,0:T(8,128)S(1)} %copy-done.25, f32[256,1152]{1,0:T(8,128)} %get-tuple-element.209.own_ref, bf16[256,1152]{1,0:T(8,128)(2,1)S(1)} %collective-permute-done.15.refs_0_, ...), custom_call_target="tpu_custom_call" | custom-call | flops 1000 | bytes 1000 | tf_op jit(solution)/shard_map/pallas_call | solution.py:28
  152.0 1.8 %shard_map.90.du_ref = bf16[256,1152]{1,0:T(8,128)(2,1)S(1)} custom-call(f32[256,1152]{1,0:T(8,128)S(1)} %copy-done.5, f32[256,1]{1,0:T(8,128)S(1)} %copy-done.23, f32[256,1152]{1,0:T(8,128)} %get-tuple-element.188.own_ref, bf16[256,1152]{1,0:T(8,128)(2,1)S(1)} %collective-permute-done.16.refs_0_), custom_call_target="tpu_custom_call" | custom-call | flops 1000 | bytes 1000 | tf_op jit(solution)/shard_map/pallas_call | solution.py:28
  153.9 0.3 copy-done.2
  154.1 1.8 %shard_map.93 = bf16[256,1152]{1,0:T(8,128)(2,1)} custom-call(bf16[256,1152]{1,0:T(8,128)(2,1)S(1)} %shard_map.92.du_ref, bf16[1152,1152]{1,0:T(8,128)(2,1)S(1)} %copy-done.2), custom_call_target="tpu_custom_call" | custom-call | flops 1000 | bytes 1000 | tf_op jit(solution)/shard_map/pallas_call | solution.py:28
  156.0 1.8 %shard_map.91 = bf16[256,1152]{1,0:T(8,128)(2,1)} custom-call(bf16[256,1152]{1,0:T(8,128)(2,1)S(1)} %shard_map.90.du_ref, bf16[1152,1152]{1,0:T(8,128)(2,1)S(1)} %copy-done), custom_call_target="tpu_custom_call" | custom-call | flops 1000 | bytes 1000 | tf_op jit(solution)/shard_map/pallas_call | solution.py:28
  157.8 6.4 %all-to-all-done.4.in_ref = bf16[8,72,1152]{2,1,0:T(8,128)(2,1)S(1)} async-done(((bf16[8,72,1152]{2,1,0:T(8,128)(2,1)}), bf16[8,72,1152]{2,1,0:T(8,128)(2,1)S(1)}, u32[]{:S(2)}, u32[]{:S(2)}) %all-to-all-start.4) | async-done | bytes 1327136 | tf_op jit(solution)/shard_map/all_to_all | solution.py:432
  164.2 1.8 %shard_map.96 = f32[288,2304]{1,0:T(8,128)} custom-call(bf16[8,72,1152]{2,1,0:T(8,128)(2,1)S(1)} %all-to-all-done.4.in_ref), custom_call_target="tpu_custom_call" | custom-call | flops 1000 | bytes 1000 | tf_op jit(solution)/shard_map/pallas_call | solution.py:28
  (69 shorter events, 0.3 us)
Async XLA Ops:
  0.6 40.3 %collective-permute-start.9 = (bf16[256,1152]{1,0:T(8,128)(2,1)}, bf16[256,1152]{1,0:T(8,128)(2,1)S(1)}, u32[]{:S(2)}, u32[]{:S(2)}) collective-permute-start(bf16[256,1152]{1,0:T(8,128)(2,1)} %param.13), channel_id=1, source_target_pairs={{0,64},{16,80},{32,96},{48,112},{64,0},{80,16},{96,32},{112,48},{1... | collective-permute-start | bytes 1769480 | tf_op jit(solution)/shard_map/ppermute | solution.py:419
  9.2 7.7 %collective-permute-start.2 = (bf16[256,1152]{1,0:T(8,128)(2,1)}, bf16[256,1152]{1,0:T(8,128)(2,1)S(1)}, u32[]{:S(2)}, u32[]{:S(2)}) collective-permute-start(bf16[256,1152]{1,0:T(8,128)(2,1)} %get-tuple-element.56.feats_ref), channel_id=1, source_target_pairs={{0,1},{1,0},{2,3},{3,2},{4,5},{5,4},{6,7},{7,6},{8,9},{9,8},{10,11... | collective-permute-start | bytes 1769480 | tf_op jit(solution)/shard_map/cond/branch_1_fun/ppermute | solution.py:451
  9.3 16.0 %collective-permute-start = (bf16[256,1152]{1,0:T(8,128)(2,1)}, bf16[256,1152]{1,0:T(8,128)(2,1)S(1)}, u32[]{:S(2)}, u32[]{:S(2)}) collective-permute-start(bf16[256,1152]{1,0:T(8,128)(2,1)} %get-tuple-element.55.feats_ref.refs_0_), channel_id=1, source_target_pairs={{0,130},{130,0},{2,128},{128,2},{1,131},{131,1},{3,129},{129,3},{4... | collective-permute-start | bytes 1769480 | tf_op jit(solution)/shard_map/cond/branch_1_fun/ppermute | solution.py:449
  10.9 15.7 %collective-permute-start.1 = (bf16[256,1152]{1,0:T(8,128)(2,1)}, bf16[256,1152]{1,0:T(8,128)(2,1)S(1)}, u32[]{:S(2)}, u32[]{:S(2)}) collective-permute-start(bf16[256,1152]{1,0:T(8,128)(2,1)} %get-tuple-element.56.feats_ref), channel_id=1, source_target_pairs={{0,2},{2,0},{1,3},{3,1},{4,6},{6,4},{5,7},{7,5},{8,10},{10,8},{9,1... | collective-permute-start | bytes 1769480 | tf_op jit(solution)/shard_map/cond/branch_1_fun/ppermute | solution.py:450
  12.7 4.3 %copy-start.1 = (bf16[1152,1152]{1,0:T(8,128)(2,1)S(1)}, bf16[1152,1152]{1,0:T(8,128)(2,1)}, u32[]{:S(2)}) copy-start(bf16[1152,1152]{1,0:T(8,128)(2,1)} %get-tuple-element.58.head_ref) | copy-start | bytes 7962628 | tf_op jit(solution)/shard_map/cond
  17.0 13.1 %copy-start.7 = (bf16[256,1152]{1,0:T(8,128)(2,1)}, bf16[256,1152]{1,0:T(8,128)(2,1)S(1)}, u32[]{:S(2)}) copy-start(bf16[256,1152]{1,0:T(8,128)(2,1)S(1)} %get-tuple-element.237.refs_0_) | copy-start | bytes 1769476 | tf_op jit(solution)/shard_map/cond
  17.0 2.0 %copy-start.3 = (bf16[1152,1152]{1,0:T(8,128)(2,1)S(1)}, bf16[1152,1152]{1,0:T(8,128)(2,1)}, u32[]{:S(2)}) copy-start(bf16[1152,1152]{1,0:T(8,128)(2,1)} %get-tuple-element.57.head_ref) | copy-start | bytes 7962628 | tf_op jit(solution)/shard_map/cond
  17.0 2.1 %copy-start.21 = (bf16[256,1152]{1,0:T(8,128)(2,1)S(1)}, bf16[256,1152]{1,0:T(8,128)(2,1)}, u32[]{:S(2)}) copy-start(bf16[256,1152]{1,0:T(8,128)(2,1)} %get-tuple-element.55.feats_ref.refs_0_) | copy-start | bytes 1769476 | tf_op jit(solution)/shard_map/cond
  18.1 11.9 %copy-start.9 = (bf16[256,1152]{1,0:T(8,128)(2,1)}, bf16[256,1152]{1,0:T(8,128)(2,1)S(1)}, u32[]{:S(2)}) copy-start(bf16[256,1152]{1,0:T(8,128)(2,1)S(1)} %branch_1_fun.16.refs_1_) | copy-start | bytes 1769476 | tf_op jit(solution)/shard_map/cond
  22.8 12.7 %copy-start.6 = (f32[256,1152]{1,0:T(8,128)}, f32[256,1152]{1,0:T(8,128)S(1)}, u32[]{:S(2)}) copy-start(f32[256,1152]{1,0:T(8,128)S(1)} %get-tuple-element.248.z_ref) | copy-start | bytes 3538948 | tf_op jit(solution)/shard_map/cond
  22.8 12.7 %copy-start.15 = (bf16[256,1152]{1,0:T(8,128)(2,1)}, bf16[256,1152]{1,0:T(8,128)(2,1)S(1)}, u32[]{:S(2)}) copy-start(bf16[256,1152]{1,0:T(8,128)(2,1)S(1)} %get-tuple-element.250.zb_ref) | copy-start | bytes 1769476 | tf_op jit(solution)/shard_map/cond
  22.8 12.7 %copy-start.24 = (f32[256,1]{1,0:T(8,128)}, f32[256,1]{1,0:T(8,128)S(1)}, u32[]{:S(2)}) copy-start(f32[256,1]{1,0:T(8,128)S(1)} %get-tuple-element.243.inv_ref) | copy-start | bytes 3076 | tf_op jit(solution)/shard_map/cond
  26.6 2.3 %copy-start.17 = (bf16[256,1152]{1,0:T(8,128)(2,1)}, bf16[256,1152]{1,0:T(8,128)(2,1)S(1)}, u32[]{:S(2)}) copy-start(bf16[256,1152]{1,0:T(8,128)(2,1)S(1)} %collective-permute-done.1.feats_ref) | copy-start | bytes 1769476 | tf_op jit(solution)/shard_map/cond
  26.6 2.3 %collective-permute-start.3 = (bf16[256,1152]{1,0:T(8,128)(2,1)S(1)}, bf16[256,1152]{1,0:T(8,128)(2,1)S(1)}, u32[]{:S(2)}, u32[]{:S(2)}) collective-permute-start(bf16[256,1152]{1,0:T(8,128)(2,1)S(1)} %collective-permute-done.1.feats_ref), channel_id=1, source_target_pairs={{0,1},{1,0},{2,3},{3,2},{4,5},{5,4},{6,7},{7,6},{8,9},{9,8},{10,11... | collective-permute-start | bytes 1769480 | tf_op jit(solution)/shard_map/cond/branch_1_fun/ppermute | solution.py:458
  28.9 6.6 %copy-start.11 = (bf16[256,1152]{1,0:T(8,128)(2,1)}, bf16[256,1152]{1,0:T(8,128)(2,1)S(1)}, u32[]{:S(2)}) copy-start(bf16[256,1152]{1,0:T(8,128)(2,1)S(1)} %get-tuple-element.239.refs_2_.refs_0_) | copy-start | bytes 1769476 | tf_op jit(solution)/shard_map/cond
  30.0 5.5 %copy-start.13 = (bf16[256,1152]{1,0:T(8,128)(2,1)}, bf16[256,1152]{1,0:T(8,128)(2,1)S(1)}, u32[]{:S(2)}) copy-start(bf16[256,1152]{1,0:T(8,128)(2,1)S(1)} %branch_1_fun.19.refs_3_.refs_1_) | copy-start | bytes 1769476 | tf_op jit(solution)/shard_map/cond
  39.0 1.7 %copy-start.8 = (bf16[256,1152]{1,0:T(8,128)(2,1)S(1)}, bf16[256,1152]{1,0:T(8,128)(2,1)}, u32[]{:S(2)}) copy-start(bf16[256,1152]{1,0:T(8,128)(2,1)} %copy-done.7) | copy-start | bytes 1769476 | tf_op jit(solution)/shard_map/cond
  39.0 1.8 %copy-start.10 = (bf16[256,1152]{1,0:T(8,128)(2,1)S(1)}, bf16[256,1152]{1,0:T(8,128)(2,1)}, u32[]{:S(2)}) copy-start(bf16[256,1152]{1,0:T(8,128)(2,1)} %copy-done.9) | copy-start | bytes 1769476 | tf_op jit(solution)/shard_map/cond
  39.0 1.8 %copy-start.12 = (bf16[256,1152]{1,0:T(8,128)(2,1)S(1)}, bf16[256,1152]{1,0:T(8,128)(2,1)}, u32[]{:S(2)}) copy-start(bf16[256,1152]{1,0:T(8,128)(2,1)} %copy-done.11) | copy-start | bytes 1769476 | tf_op jit(solution)/shard_map/cond
  39.0 1.8 %copy-start.14 = (bf16[256,1152]{1,0:T(8,128)(2,1)S(1)}, bf16[256,1152]{1,0:T(8,128)(2,1)}, u32[]{:S(2)}) copy-start(bf16[256,1152]{1,0:T(8,128)(2,1)} %copy-done.13) | copy-start | bytes 1769476 | tf_op jit(solution)/shard_map/cond
  46.8 9.1 %copy-start.29 = (f32[256,1]{1,0:T(8,128)S(1)}, f32[256,1]{1,0:T(8,128)}, u32[]{:S(2)}) copy-start(f32[256,1]{1,0:T(8,128)} %get-tuple-element.186) | copy-start | bytes 3076
  49.2 3.5 %collective-permute-start.10 = (bf16[2,288,1152]{2,1,0:T(8,128)(2,1)}, bf16[2,288,1152]{2,1,0:T(8,128)(2,1)}, u32[]{:S(2)}, u32[]{:S(2)}) collective-permute-start(bf16[2,288,1152]{2,1,0:T(8,128)(2,1)} %get-tuple-element.175), channel_id=1, source_target_pairs={{0,1},{1,0},{2,3},{3,2},{4,5},{5,4},{6,7},{7,6},{8,9},{9,8},{10,11... | collective-permute-start | bytes 3981320 | tf_op jit(solution)/shard_map/ppermute | solution.py:479
  52.7 3.3 %copy-start.4 = (f32[256,1152]{1,0:T(8,128)S(1)}, f32[256,1152]{1,0:T(8,128)}, u32[]{:S(2)}) copy-start(f32[256,1152]{1,0:T(8,128)} %get-tuple-element.161.z_ref) | copy-start | bytes 3538948
  52.7 3.3 %copy-start.16 = (bf16[256,1152]{1,0:T(8,128)(2,1)S(1)}, bf16[256,1152]{1,0:T(8,128)(2,1)}, u32[]{:S(2)}) copy-start(bf16[256,1152]{1,0:T(8,128)(2,1)} %get-tuple-element.182) | copy-start | bytes 1769476
  52.7 3.3 %copy-start.18 = (bf16[256,1152]{1,0:T(8,128)(2,1)S(1)}, bf16[256,1152]{1,0:T(8,128)(2,1)}, u32[]{:S(2)}) copy-start(bf16[256,1152]{1,0:T(8,128)(2,1)} %get-tuple-element.187) | copy-start | bytes 1769476
  52.7 3.3 %copy-start.19 = (f32[256,1152]{1,0:T(8,128)S(1)}, f32[256,1152]{1,0:T(8,128)}, u32[]{:S(2)}) copy-start(f32[256,1152]{1,0:T(8,128)} %get-tuple-element.185) | copy-start | bytes 3538948
  52.7 3.3 %copy-start.22 = (f32[256,1]{1,0:T(8,128)S(1)}, f32[256,1]{1,0:T(8,128)}, u32[]{:S(2)}) copy-start(f32[256,1]{1,0:T(8,128)} %get-tuple-element.162.inv_ref) | copy-start | bytes 3076
  52.7 3.3 %copy-start.26 = (bf16[2,256,256]{2,1,0:T(8,128)(2,1)S(1)}, bf16[2,256,256]{2,1,0:T(8,128)(2,1)}, u32[]{:S(2)}) copy-start(bf16[2,256,256]{2,1,0:T(8,128)(2,1)} %get-tuple-element.163) | copy-start | bytes 786436
  59.9 2.9 %collective-permute-start.4 = (bf16[2,256,1152]{2,1,0:T(8,128)(2,1)S(1)}, bf16[2,256,1152]{2,1,0:T(8,128)(2,1)S(1)}, u32[]{:S(2)}, u32[]{:S(2)}) collective-permute-start(bf16[2,256,1152]{2,1,0:T(8,128)(2,1)S(1)} %get-tuple-element.88), channel_id=1, source_target_pairs={{0,1},{1,0},{2,3},{3,2},{4,5},{5,4},{6,7},{7,6},{8,9},{9,8},{10,11... | collective-permute-start | bytes 3538952 | tf_op jit(solution)/shard_map/cond/branch_1_fun/ppermute | solution.py:489
  62.9 1.5 copy-start.20
  66.5 3.1 %collective-permute-start.5 = (bf16[2,288,1152]{2,1,0:T(8,128)(2,1)S(1)}, bf16[2,288,1152]{2,1,0:T(8,128)(2,1)S(1)}, u32[]{:S(2)}, u32[]{:S(2)}) collective-permute-start(bf16[2,288,1152]{2,1,0:T(8,128)(2,1)S(1)} %get-tuple-element.100), channel_id=1, source_target_pairs={{0,1},{1,0},{2,3},{3,2},{4,5},{5,4},{6,7},{7,6},{8,9},{9,8},{10,11... | collective-permute-start | bytes 3981320 | tf_op jit(solution)/shard_map/cond/branch_1_fun/ppermute | solution.py:494
  70.9 11.2 %copy-start.27 = (bf16[256,1152]{1,0:T(8,128)(2,1)S(1)}, bf16[256,1152]{1,0:T(8,128)(2,1)}, u32[]{:S(2)}) copy-start(bf16[256,1152]{1,0:T(8,128)(2,1)} %get-tuple-element.201) | copy-start | bytes 1769476
  70.9 27.5 %all-to-all-start.1 = ((bf16[4,144,1152]{2,1,0:T(8,128)(2,1)}), bf16[4,144,1152]{2,1,0:T(8,128)(2,1)S(1)}, u32[]{:S(2)}, u32[]{:S(2)}) async-start(bf16[4,144,1152]{2,1,0:T(8,128)(2,1)} %get-tuple-element.193), calls=%async_computation.1 | async-start | bytes 2654208 | tf_op jit(solution)/shard_map/all_to_all | solution.py:432
  76.3 12.1 %collective-permute-start.11 = (bf16[4,36,1152]{2,1,0:T(8,128)(2,1)}, bf16[4,36,1152]{2,1,0:T(8,128)(2,1)S(1)}, u32[]{:S(2)}, u32[]{:S(2)}) collective-permute-start(bf16[4,36,1152]{2,1,0:T(8,128)(2,1)} %get-tuple-element.190), channel_id=1, source_target_pairs={{0,4},{4,8},{8,12},{12,0},{1,5},{5,9},{9,13},{13,1},{2,6},{6,10},{... | collective-permute-start | bytes 995336 | tf_op jit(solution)/shard_map/ppermute | solution.py:425
  77.9 19.6 %collective-permute-start.12 = (bf16[4,36,1152]{2,1,0:T(8,128)(2,1)}, bf16[4,36,1152]{2,1,0:T(8,128)(2,1)S(1)}, u32[]{:S(2)}, u32[]{:S(2)}) collective-permute-start(bf16[4,36,1152]{2,1,0:T(8,128)(2,1)} %get-tuple-element.191), channel_id=1, source_target_pairs={{0,8},{4,12},{8,0},{12,4},{1,9},{5,13},{9,1},{13,5},{2,10},{6,14},... | collective-permute-start | bytes 995336 | tf_op jit(solution)/shard_map/ppermute | solution.py:425
  80.8 16.7 %collective-permute-start.13 = (bf16[4,36,1152]{2,1,0:T(8,128)(2,1)}, bf16[4,36,1152]{2,1,0:T(8,128)(2,1)S(1)}, u32[]{:S(2)}, u32[]{:S(2)}) collective-permute-start(bf16[4,36,1152]{2,1,0:T(8,128)(2,1)} %get-tuple-element.192), channel_id=1, source_target_pairs={{0,12},{4,0},{8,4},{12,8},{1,13},{5,1},{9,5},{13,9},{2,14},{6,2},{... | collective-permute-start | bytes 995336 | tf_op jit(solution)/shard_map/ppermute | solution.py:425
  82.1 32.6 %collective-permute-start.15 = (bf16[256,1152]{1,0:T(8,128)(2,1)S(1)}, bf16[256,1152]{1,0:T(8,128)(2,1)S(1)}, u32[]{:S(2)}, u32[]{:S(2)}) collective-permute-start(bf16[256,1152]{1,0:T(8,128)(2,1)S(1)} %copy-done.27), channel_id=1, source_target_pairs={{0,130},{130,0},{2,128},{128,2},{1,131},{131,1},{3,129},{129,3},{4... | collective-permute-start | bytes 1769480 | tf_op jit(solution)/shard_map/ppermute | solution.py:477
  83.6 31.1 %collective-permute-start.14 = (bf16[256,1152]{1,0:T(8,128)(2,1)}, bf16[256,1152]{1,0:T(8,128)(2,1)S(1)}, u32[]{:S(2)}, u32[]{:S(2)}) collective-permute-start(bf16[256,1152]{1,0:T(8,128)(2,1)} %get-tuple-element.200), channel_id=1, source_target_pairs={{0,64},{16,80},{32,96},{48,112},{64,0},{80,16},{96,32},{112,48},{1... | collective-permute-start | bytes 1769480 | tf_op jit(solution)/shard_map/ppermute | solution.py:419
  99.5 15.0 %copy-start.28 = (bf16[256,1152]{1,0:T(8,128)(2,1)S(1)}, bf16[256,1152]{1,0:T(8,128)(2,1)}, u32[]{:S(2)}) copy-start(bf16[256,1152]{1,0:T(8,128)(2,1)} %get-tuple-element.203) | copy-start | bytes 1769476
  99.5 14.2 %all-to-all-start = ((bf16[4,36,1152]{2,1,0:T(8,128)(2,1)}), bf16[4,36,1152]{2,1,0:T(8,128)(2,1)S(1)}, u32[]{:S(2)}, u32[]{:S(2)}) async-start(bf16[4,36,1152]{2,1,0:T(8,128)(2,1)} %get-tuple-element.105), calls=%async_computation | async-start | bytes 737280 | tf_op jit(solution)/shard_map/cond/branch_1_fun/all_to_all | solution.py:432
  104.4 6.7 %collective-permute-start.6 = (bf16[36,1152]{1,0:T(8,128)(2,1)}, bf16[36,1152]{1,0:T(8,128)(2,1)S(1)}, u32[]{:S(2)}, u32[]{:S(2)}) collective-permute-start(bf16[36,1152]{1,0:T(8,128)(2,1)} %get-tuple-element.102), channel_id=1, source_target_pairs={{0,4},{4,8},{8,12},{12,0},{1,5},{5,9},{9,13},{13,1},{2,6},{6,10},{... | collective-permute-start | bytes 248840 | tf_op jit(solution)/shard_map/cond/branch_1_fun/ppermute | solution.py:425
  105.5 6.6 %collective-permute-start.7 = (bf16[36,1152]{1,0:T(8,128)(2,1)}, bf16[36,1152]{1,0:T(8,128)(2,1)S(1)}, u32[]{:S(2)}, u32[]{:S(2)}) collective-permute-start(bf16[36,1152]{1,0:T(8,128)(2,1)} %get-tuple-element.103), channel_id=1, source_target_pairs={{0,8},{4,12},{8,0},{12,4},{1,9},{5,13},{9,1},{13,5},{2,10},{6,14},... | collective-permute-start | bytes 248840 | tf_op jit(solution)/shard_map/cond/branch_1_fun/ppermute | solution.py:425
  107.9 4.8 %collective-permute-start.8 = (bf16[36,1152]{1,0:T(8,128)(2,1)}, bf16[36,1152]{1,0:T(8,128)(2,1)S(1)}, u32[]{:S(2)}, u32[]{:S(2)}) collective-permute-start(bf16[36,1152]{1,0:T(8,128)(2,1)} %get-tuple-element.104), channel_id=1, source_target_pairs={{0,12},{4,0},{8,4},{12,8},{1,13},{5,1},{9,5},{13,9},{2,14},{6,2},{... | collective-permute-start | bytes 248840 | tf_op jit(solution)/shard_map/cond/branch_1_fun/ppermute | solution.py:425
  114.5 13.7 %collective-permute-start.16 = (bf16[256,1152]{1,0:T(8,128)(2,1)S(1)}, bf16[256,1152]{1,0:T(8,128)(2,1)S(1)}, u32[]{:S(2)}, u32[]{:S(2)}) collective-permute-start(bf16[256,1152]{1,0:T(8,128)(2,1)S(1)} %copy-done.28), channel_id=1, source_target_pairs={{0,2},{2,0},{1,3},{3,1},{4,6},{6,4},{5,7},{7,5},{8,10},{10,8},{9,1... | collective-permute-start | bytes 1769480 | tf_op jit(solution)/shard_map/ppermute | solution.py:507
  114.7 14.9 %all-to-all-start.2 = ((bf16[8,9,1152]{2,1,0:T(8,128)(2,1)}), bf16[8,9,1152]{2,1,0:T(8,128)(2,1)S(1)}, u32[]{:S(2)}, u32[]{:S(2)}) async-start(bf16[8,9,1152]{2,1,0:T(8,128)(2,1)} %get-tuple-element.257), calls=%async_computation.2 | async-start | bytes 589824 | tf_op jit(solution)/shard_map/all_to_all | solution.py:432
  144.0 5.8 %copy-start.25 = (f32[256,1]{1,0:T(8,128)S(1)}, f32[256,1]{1,0:T(8,128)}, u32[]{:S(2)}) copy-start(f32[256,1]{1,0:T(8,128)} %get-tuple-element.208.inv_ref) | copy-start | bytes 3076
  144.0 20.2 %all-to-all-start.4 = ((bf16[8,72,1152]{2,1,0:T(8,128)(2,1)}), bf16[8,72,1152]{2,1,0:T(8,128)(2,1)S(1)}, u32[]{:S(2)}, u32[]{:S(2)}) async-start(bf16[8,72,1152]{2,1,0:T(8,128)(2,1)} %shard_map.95), calls=%async_computation.4 | async-start | bytes 2654208 | tf_op jit(solution)/shard_map/all_to_all | solution.py:432
  149.8 2.2 %copy-start.5 = (f32[256,1152]{1,0:T(8,128)S(1)}, f32[256,1152]{1,0:T(8,128)}, u32[]{:S(2)}) copy-start(f32[256,1152]{1,0:T(8,128)} %get-tuple-element.161.z_ref) | copy-start | bytes 3538948
  149.8 2.2 %copy-start.23 = (f32[256,1]{1,0:T(8,128)S(1)}, f32[256,1]{1,0:T(8,128)}, u32[]{:S(2)}) copy-start(f32[256,1]{1,0:T(8,128)} %get-tuple-element.162.inv_ref) | copy-start | bytes 3076
  152.0 2.1 %copy-start.2 = (bf16[1152,1152]{1,0:T(8,128)(2,1)S(1)}, bf16[1152,1152]{1,0:T(8,128)(2,1)}, u32[]{:S(2)}) copy-start(bf16[1152,1152]{1,0:T(8,128)(2,1)} %head_ref.5) | copy-start | bytes 7962628
  154.1 1.9 %copy-start = (bf16[1152,1152]{1,0:T(8,128)(2,1)S(1)}, bf16[1152,1152]{1,0:T(8,128)(2,1)}, u32[]{:S(2)}) copy-start(bf16[1152,1152]{1,0:T(8,128)(2,1)} %head_ref.4) | copy-start | bytes 7962628

commit v2 on v1

v2 whole, which is shorter than its diff:
```python
import functools

import jax
import jax.numpy as jnp
from jax import lax
from jax.experimental import pallas as pl
from jax.experimental.pallas import tpu as pltpu
from jax.sharding import Mesh, PartitionSpec as P

ROWS = ("xh", "z", "y", "xl", "c")
X_RING = ("xh", "xl")
SWAP = [(0, 1), (1, 0)]
CROSS = [(0, 3), (3, 0), (1, 2), (2, 1)]
F32 = jnp.float32
BF16 = jnp.bfloat16
LANES_BOTH = (((1,), (1,)), ((), ()))
ROWS_BOTH = (((0,), (0,)), ((), ()))


def shape(dims, dtype):
    return jax.ShapeDtypeStruct(dims, dtype)


def local(kernel, outs, *args, scalars=0, scratch=(), mib=16):
    vmem = pl.BlockSpec(memory_space=pltpu.VMEM)
    smem = pl.BlockSpec(memory_space=pltpu.SMEM)
    many = isinstance(outs, (tuple, list))
    return pl.pallas_call(
        kernel,
        out_shape=outs,
        in_specs=[smem] * scalars + [vmem] * (len(args) - scalars),
        out_specs=[vmem] * len(outs) if many else vmem,
        scratch_shapes=scratch,
        compiler_params=pltpu.CompilerParams(vmem_limit_bytes=mib << 20),
        cost_estimate=pl.CostEstimate(flops=1000, bytes_accessed=1000, transcendentals=0),
    )(*args)


def embedding(feats, head):
    u = jnp.dot(feats, head, preferred_element_type=F32)
    inv = lax.rsqrt(jnp.sum(u * u, axis=1, keepdims=True) + 1e-06)
    return u * inv, inv


def tangent(z, inv, dz):
    return inv * (dz - z * jnp.sum(z * dz, axis=1, keepdims=True))


def over_rows(a, b):
    return lax.dot_general(a, b, ROWS_BOTH, preferred_element_type=F32)


def embed_kernel(head_ref, feats_ref, zb_ref, late_ref, inv_ref):
    z, inv = embedding(feats_ref[...], head_ref[...])
    zb_ref[...] = z.astype(BF16)
    late_ref[...] = z.astype(BF16)
    inv_ref[...] = inv


def embed(head, feats):
    rows, wide = feats.shape
    block = shape((rows, wide), BF16)
    return local(embed_kernel, [block, block, shape((rows, 1), F32)], head, feats)


def embed_other_kernel(head_ref, feats_ref, zb_ref):
    zb_ref[...] = embedding(feats_ref[...], head_ref[...])[0].astype(BF16)


def embed_other(head, feats):
    return local(embed_other_kernel, shape(feats.shape, BF16), head, feats)


def weigh(scale, bias, txt, img_refs, w_ref, home):
    weights = []
    for i, img_ref in enumerate(img_refs):
        logits = (
            scale * lax.dot_general(txt, img_ref[...], LANES_BOTH, preferred_element_type=F32)
            + bias
        )
        if home and i == 0:
            row_ids = lax.broadcasted_iota(jnp.int32, logits.shape, 0)
            col_ids = lax.broadcasted_iota(jnp.int32, logits.shape, 1)
            sign = jnp.where(row_ids == col_ids, 1.0, -1.0).astype(F32)
            deriv = -sign * jax.nn.sigmoid(-sign * logits)
        else:
            deriv = jax.nn.sigmoid(logits)
        weights.append((scale * deriv).astype(BF16))
        w_ref[i] = weights[-1]
    return weights


def gather(weights, img_refs):
    total = None
    for w, img_ref in zip(weights, img_refs):
        part = jnp.dot(w, img_ref[...], preferred_element_type=F32)
        total = part if total is None else total + part
    return total


def home_first_kernel(scale_ref, bias_ref, feats_ref, head_ref, *refs):
    img_refs, (zb_ref, inv_ref, w_ref) = refs[:-3], refs[-3:]
    z, inv = embedding(feats_ref[...], head_ref[...])
    txt = z.astype(BF16)
    zb_ref[...] = txt
    inv_ref[...] = inv
    weigh(scale_ref[0], bias_ref[0], txt, img_refs, w_ref, True)


def home_first(scale, bias, feats, head, imgs):
    rows, wide = feats.shape
    outs = [
        shape((rows, wide), BF16),
        shape((rows, 1), F32),
        shape((len(imgs), rows, imgs[0].shape[0]), BF16),
    ]
    return local(home_first_kernel, outs, scale, bias, feats, head, *imgs, scalars=2)


def group_kernel(scale_ref, bias_ref, zb_ref, inv_ref, first_ref, feats_ref, head_ref, *refs):
    img_refs, (w_ref, dz_ref, du_ref), near_refs = refs[:4], refs[4:7], refs[7:]
    txt = zb_ref[...]
    done = first_ref.shape[0]
    weights = weigh(scale_ref[0], bias_ref[0], txt, img_refs[done:], w_ref, False)
    dz = gather([first_ref[i] for i in range(done)] + weights, img_refs)
    dz_ref[...] = dz.astype(BF16)
    du_ref[...] = tangent(txt.astype(F32), inv_ref[...], dz).astype(BF16)
    text_kernel(scale_ref, bias_ref, feats_ref, head_ref, *img_refs, *near_refs)


def group_block(scale, bias, zb, inv, first, feats, head, imgs):
    rows, wide = zb.shape
    block = shape((rows, wide), BF16)
    outs = [shape((len(imgs) - first.shape[0],) + first.shape[1:], BF16), block, block]
    outs += [block, shape((len(imgs),) + first.shape[1:], BF16), block, block]
    return local(group_kernel, outs, scale, bias, zb, inv, first, feats, head, *imgs, scalars=2)


def text_kernel(scale_ref, bias_ref, feats_ref, head_ref, *refs):
    img_refs, (zb_ref, w_ref, dz_ref, du_ref) = refs[:-4], refs[-4:]
    z, inv = embedding(feats_ref[...], head_ref[...])
    txt = z.astype(BF16)
    zb_ref[...] = txt
    dz = gather(weigh(scale_ref[0], bias_ref[0], txt, img_refs, w_ref, False), img_refs)
    dz_ref[...] = dz.astype(BF16)
    du_ref[...] = tangent(z, inv, dz).astype(BF16)


def text_block(scale, bias, feats, head, imgs):
    rows, wide = feats.shape
    block = shape((rows, wide), BF16)
    outs = [block, shape((len(imgs), rows, imgs[0].shape[0]), BF16), block, block]
    return local(text_kernel, outs, scale, bias, feats, head, *imgs, scalars=2)


def part_by_core(core, acc_ref, keep_ref, send_ref):
    rows = keep_ref.shape[1]
    for k in range(2):
        mine = pl.multiple_of((2 * k + core) * rows, 8)
        other = pl.multiple_of((2 * k + 1 - core) * rows, 8)
        send_ref[k] = acc_ref[pl.ds(other, rows), :].astype(BF16)
        keep_ref[k] = acc_ref[pl.ds(mine, rows), :].astype(BF16)


def text_head_kernel(core_ref, *refs):
    pairs, (keep_ref, send_ref, acc_ref) = refs[:-3], refs[-3:]
    total = None
    for i in range(0, len(pairs), 2):
        part = over_rows(pairs[i][...], pairs[i + 1][...])
        total = part if total is None else total + part
    acc_ref[...] = total
    part_by_core(core_ref[0], acc_ref, keep_ref, send_ref)


def text_head_part(core, *pairs):
    depth, wide = pairs[0].shape[1], pairs[1].shape[1]
    half = shape((2, depth // 4, wide), BF16)
    return local(
        text_head_kernel,
        [half, half],
        core,
        *pairs,
        scalars=1,
        scratch=[pltpu.VMEM((depth, wide), F32)],
        mib=20,
    )


def image_side_kernel(count, *refs):
    txt_refs, w_refs, first_ref, rest_ref = (
        refs[:count],
        refs[count : 2 * count - 1],
        refs[2 * count - 1],
        refs[2 * count],
    )
    keep_ref, send_ref = refs[-2:]
    for i in (1, 3, 0, 2):
        weights = [first_ref[i] if i < 2 else rest_ref[i - 2]] + [ref[i] for ref in w_refs]
        dz = None
        for w, txt_ref in zip(weights, txt_refs):
            part = over_rows(w, txt_ref[...])
            dz = part if dz is None else dz + part
        if i % 2 == 0:
            keep_ref[i // 2] = dz
        else:
            send_ref[i // 2] = dz.astype(BF16)


def image_side(txts, weights, home):
    rows, wide = txts[0].shape
    dims = (2, rows, wide)
    return local(
        functools.partial(image_side_kernel, len(txts)),
        [shape(dims, F32), shape(dims, BF16)],
        *txts,
        *weights,
        *home,
        mib=20,
    )


def image_head_kernel(core_ref, keep_ref, got_ref, *refs):
    zb_refs, inv_refs, feats_refs = refs[:2], refs[2:4], refs[4:6]
    own_ref, next_ref, left_ref, send_ref, acc_ref = refs[6:]
    total = None
    for i in (1, 0):
        dz = keep_ref[i] + got_ref[i].astype(F32)
        if i == 0:
            own_ref[...] = dz.astype(BF16)
        else:
            next_ref[...] = dz.astype(BF16)
        du = tangent(zb_refs[i][...].astype(F32), inv_refs[i][...], dz).astype(BF16)
        part = over_rows(feats_refs[i][...], du)
        total = part if total is None else total + part
    acc_ref[...] = total
    part_by_core(core_ref[0], acc_ref, left_ref, send_ref)


def image_head_part(core, keep, got, zbs, invs, feats):
    dims = keep.shape[1:]
    block = shape(dims, BF16)
    depth = feats[0].shape[1]
    half = shape((2, depth // 4, dims[1]), BF16)
    return local(
        image_head_kernel,
        [block, block, half, half],
        core,
        keep,
        got,
        *zbs,
        *invs,
        *feats,
        scalars=1,
        scratch=[pltpu.VMEM((depth, dims[1]), F32)],
        mib=24,
    )


def split_x_kernel(got_ref, keep_ref, out_ref):
    rows = out_ref.shape[1]
    for k in range(out_ref.shape[0]):
        at = pl.ds(k % 2 * rows, rows)
        out_ref[k] = (keep_ref[k // 2, at].astype(F32) + got_ref[k // 2, at].astype(F32)).astype(BF16)


def split_x(keep, got):
    _, rows, wide = keep.shape
    return local(split_x_kernel, shape((4, rows // 2, wide), BF16), got, keep)


def split_y_kernel(me_ref, got_ref, keep_ref, *refs):
    outs, held = refs[:-1], refs[-1]
    count, blocks, rows, _ = held.shape
    total = (keep_ref[...].astype(F32) + got_ref[...].astype(F32)).astype(BF16)
    for b in range(blocks):
        for k in range(count):
            at = (b % 2 * count + k) * rows
            held[k, b] = total[b // 2, at : at + rows]
    for s, out_ref in enumerate(outs):
        out_ref[...] = held[lax.rem(me_ref[0] + s, count)]


def split_y(me, keep, got):
    count = lax.axis_size("y")
    _, rows, wide = keep.shape
    part = (4, rows // 2 // count, wide)
    return local(
        split_y_kernel,
        [shape(part, BF16)] * count,
        me,
        got,
        keep,
        scalars=1,
        scratch=[pltpu.VMEM((count,) + part, BF16)],
    )


def sum_of(ref):
    total = ref[0].astype(F32)
    for k in range(1, ref.shape[0]):
        total = total + ref[k].astype(F32)
    return total


def sum_kernel(*refs):
    total = refs[0][...].astype(F32)
    for ref in refs[1:-1]:
        total = total + ref[...].astype(F32)
    refs[-1][...] = total.astype(BF16)


def add_up(*parts):
    return local(sum_kernel, shape(parts[0].shape, BF16), *parts)


def sum_split_y_kernel(me_ref, in_ref, *refs):
    outs, held = refs[:-1], refs[-1]
    total = sum_of(in_ref).astype(BF16)
    count, rows, _ = held.shape
    for k in range(count):
        held[k] = total[k * rows : (k + 1) * rows]
    for s, out_ref in enumerate(outs):
        out_ref[...] = held[lax.rem(me_ref[0] + s, count)]


def sum_split_y(me, parts):
    count = lax.axis_size("y")
    _, rows, wide = parts.shape
    part = (rows // count, wide)
    return local(
        sum_split_y_kernel,
        [shape(part, BF16)] * count,
        me,
        parts,
        scalars=1,
        scratch=[pltpu.VMEM((count,) + part, BF16)],
    )


def split_z_kernel(img_ref, *refs):
    txt_refs, out_ref = refs[:-1], refs[-1]
    txt = txt_refs[0][...].astype(F32)
    for ref in txt_refs[1:]:
        txt = txt + ref[...].astype(F32)
    both = jnp.concatenate([sum_of(img_ref), txt], axis=0).astype(BF16)
    rows = out_ref.shape[1]
    for k in range(out_ref.shape[0]):
        out_ref[k] = both[k * rows : (k + 1) * rows]


def split_z(img, txts):
    count = lax.axis_size("z")
    _, rows, wide = img.shape
    return local(split_z_kernel, shape((count, 2 * rows // count, wide), BF16), img, *txts)


def sum_spread_kernel(in_ref, out_ref):
    total = sum_of(in_ref).astype(BF16)
    for k in range(out_ref.shape[0]):
        out_ref[k] = total


def sum_spread(parts):
    return local(sum_spread_kernel, shape(parts.shape, BF16), parts)


def join_z_kernel(in_ref, out_ref):
    both = jnp.concatenate([in_ref[k] for k in range(in_ref.shape[0])], axis=0)
    for k in range(out_ref.shape[0]):
        out_ref[k] = both


def join_z(pieces, copies):
    count, rows, wide = pieces.shape
    return local(join_z_kernel, shape((copies, count * rows, wide), BF16), pieces)


def finish_kernel(part, in_ref, out_ref):
    count, both, wide = in_ref.shape
    rows = both // 2
    for k in range(count):
        for j in range(2):
            out_ref[k * rows : (k + 1) * rows, j * wide : (j + 1) * wide] = (
                in_ref[k, j * rows : (j + 1) * rows].astype(F32) * part
            )


def finish(part, pieces):
    count, both, wide = pieces.shape
    return local(
        functools.partial(finish_kernel, part), shape((count * both // 2, 2 * wide), F32), pieces
    )


def grads_kernel(feats_ref, head_ref, *refs):
    parts, out_ref = refs[:-1], refs[-1]
    z, inv = embedding(feats_ref[...], head_ref[...])
    dz = parts[0][...].astype(F32)
    for ref in parts[1:]:
        dz = dz + ref[...].astype(F32)
    du = tangent(z, inv, dz).astype(BF16)
    out = lax.dot_general(du, head_ref[...], LANES_BOTH, preferred_element_type=F32)
    out_ref[...] = out.astype(BF16)


def feature_grads(feats, head, *parts):
    return local(grads_kernel, shape(feats.shape, BF16), feats, head, *parts)


def far_z(block):
    count = lax.axis_size("z")
    return lax.ppermute(block, "z", [(i, (i + count // 2) % count) for i in range(count)])


def along_y(parts):
    count = lax.axis_size("y")
    return [parts[0]] + [
        lax.ppermute(part, "y", [(i, (i + s) % count) for i in range(count)])
        for s, part in enumerate(parts)
        if s > 0
    ]


def swap(block, axes):
    return lax.all_to_all(block, axes, 0, 0, tiled=True)


def per_device(image_feats, text_feats, image_head, text_head, scale, bias):
    core = lax.axis_index("c").astype(jnp.int32).reshape(1)
    me_y = lax.axis_index("y").astype(jnp.int32).reshape(1)

    def unit(work):
        def nothing():
            return jax.tree.map(lambda s: jnp.zeros(s.shape, s.dtype), jax.eval_shape(work))

        return lax.cond(scale[0] > 0, work, nothing)

    far = far_z(text_feats)

    near = lax.ppermute(text_feats, X_RING, CROSS)
    next_feats = lax.ppermute(image_feats, "xl", SWAP)

    def own_unit():
        core_feats = lax.ppermute(image_feats, "c", SWAP)
        zb_img, late_img, inv_img = embed(image_head, image_feats)
        zb_core = embed_other(image_head, core_feats)
        zb_txt, inv_txt, w_first = home_first(
            scale, bias, text_feats, text_head, [zb_img, zb_core]
        )
        return zb_img, zb_core, late_img, inv_img, zb_txt, inv_txt, w_first

    zb_img, zb_core, late_img, inv_img, zb_txt, inv_txt, w_first = unit(own_unit)
    near, next_feats, w_first = lax.optimization_barrier((near, next_feats, w_first))

    def group_unit():
        next_core_feats = lax.ppermute(next_feats, "c", SWAP)
        zb_next, late_next, inv_next = embed(image_head, next_feats)
        zb_next_core = embed_other(image_head, next_core_feats)
        imgs = [zb_img, zb_core, zb_next, zb_next_core]
        w_rest, dz_txt, du_home, zb_near, w_near, back_near, du_near = group_block(
            scale, bias, zb_txt, inv_txt, w_first, near, text_head, imgs
        )
        return dict(
            imgs=imgs[2:],
            late=late_next,
            inv=inv_next,
            w_rest=w_rest,
            dz_txt=dz_txt,
            zb_near=zb_near,
            w_near=w_near,
            back_near=back_near,
            dus=[du_home, du_near],
        )

    got = unit(group_unit)
    far, dus = lax.optimization_barrier((far, got["dus"]))
    zb_far, w_far, back_far, du_far = text_block(
        scale, bias, far, text_head, [zb_img, zb_core] + got["imgs"]
    )
    back_far = far_z(back_far)
    back_near = lax.ppermute(got["back_near"], X_RING, CROSS)
    keep_dz, send_dz = image_side(
        [zb_txt, got["zb_near"], zb_far], [got["w_near"], w_far], [w_first, got["w_rest"]]
    )
    got_dz = lax.ppermute(send_dz, "c", SWAP)
    keep_dz, du_far = lax.optimization_barrier((keep_dz, du_far))
    keep_txt, send = text_head_part(core, far, du_far, text_feats, dus[0], near, dus[1])
    got_txt = lax.ppermute(send, "c", SWAP)
    keep_txt, got_dz = lax.optimization_barrier((keep_txt, got_dz))
    own, send, keep, part = image_head_part(
        core, keep_dz, got_dz, [late_img, got["late"]], [inv_img, got["inv"]], [image_feats, next_feats]
    )
    got_img = lax.ppermute(part, "c", SWAP)
    txt = split_x(keep_txt, got_txt)
    txt, got_img = lax.optimization_barrier((txt, got_img))
    txt = swap(txt, ("xl", "xh"))
    img = along_y(split_y(me_y, keep, got_img))
    txt, img = lax.optimization_barrier((sum_split_y(me_y, txt), img))
    img = add_up(*img)

    def second_unit():
        return split_z(swap(img, ("xl", "xh")), along_y(txt))

    piece, send = lax.optimization_barrier((unit(second_unit), send))
    back_img = lax.ppermute(send, "xl", SWAP)
    piece, back_far, back_near = lax.optimization_barrier((piece, back_far, back_near))
    piece = swap(piece, "z")
    piece, back_img, back_far, back_near = lax.optimization_barrier(
        (piece, back_img, back_far, back_near)
    )
    image_grads = feature_grads(image_feats, image_head, own, back_img)
    text_grads = feature_grads(text_feats, text_head, got["dz_txt"], back_near, back_far)

    piece = join_z(swap(sum_spread(piece), "z"), lax.axis_size(("xh", "y")))
    parts = lax.axis_size(("xh", "z", "y")) * lax.axis_size(("xl", "c"))
    head_grads = finish(1.0 / parts, swap(piece, ("xh", "y")))
    return (image_grads, text_grads, head_grads)


def solution(mesh):
    fine = Mesh(mesh.devices.reshape(2, 8, 4, 2, 2), ROWS)
    split = P(ROWS, None)
    return jax.shard_map(
        per_device,
        mesh=fine,
        in_specs=(split, split, P(), P(), P(), P()),
        out_specs=(split, split, P(("xl", "c"), None)),
        check_vma=False,
    )
```

time: 167 us -> 159 us (0.952)
  waiting for transfers between devices: 46.8 us -> 20.1 us
  blocking collectives: 13.2 us -> 31.4 us
  starting transfers between devices: 44.4 us -> 40.3 us
  local copies, waits for them, and re-layouts: 1.37 us -> 5.21 us
  Pallas kernels: 57.7 us -> 59.4 us
    all_to_all x1 -> x2, blocking collectives: 13.2 us -> 31.4 us  [swap(): return lax.all_to_all(block, axes, 0, 0, tiled=True)]
    ppermute x7, waiting for transfers between devices: 12 us -> 1.44 us  [the longest x1 1.43 us: per_device(): got_img = lax.ppermute(part, 'c', SWAP)]
    ppermute x1, waiting for transfers between devices: 10.1 us -> 0.01 us  [per_device(): back_img = lax.ppermute(send, 'xl', SWAP)]
    all_to_all x4 -> x3, starting transfers between devices: 19.5 us -> 12.2 us  [swap(): return lax.all_to_all(block, axes, 0, 0, tiled=True)]
    ppermute x6, waiting for transfers between devices: 16.9 us -> 10 us  [along_y(): lax.ppermute(part, 'y', [(i, (i + s) % count) for i in range(count)])]
    unnamed x28 -> x54, local copies, waits for them, and re-layouts: 0.32 us -> 4.46 us
    ppermute x2, starting transfers between devices: 7.3 us -> 10.6 us  [far_z(): lax.ppermute(block, 'z', [(i, (i + count // 2) % count) for i in range(co...]
    pallas_call x27 -> x20, Pallas kernels: 57.7 us -> 59.4 us  [local(): pl.pallas_call(kernel, out_shape=outs, in_specs=[smem] * scalars + [vmem]...]
  transfers between devices with their start and end apart: 21 -> 20, of which waited for: 13 -> 7; matrix products, arithmetic and copies ran while one was open for 0% -> 0% of each run, Pallas kernels for 21% -> 30%
where the time goes in v2:
time: 159 us
  Pallas kernels  59.4 us (37%)
  starting transfers between devices  40.3 us (25%)
  blocking collectives  31.4 us (20%)
  waiting for transfers between devices  20.1 us (13%)
  local copies, waits for them, and re-layouts  5.21 us (3%)
  between operations  2.28 us (1%)
    pallas_call x20, Pallas kernels, local(): pl.pallas_call(kernel, out_shape=outs, in_specs=[smem] * scalars + [vmem]...  59.4 us
    all_to_all x2, blocking collectives, swap(): return lax.all_to_all(block, axes, 0, 0, tiled=True)  31.4 us
    all_to_all x3, starting transfers between devices, swap(): return lax.all_to_all(block, axes, 0, 0, tiled=True)  12.2 us
    ppermute x6, starting transfers between devices, along_y(): lax.ppermute(part, 'y', [(i, (i + s) % count) for i in range(count)])  11 us
    ppermute x2, starting transfers between devices, far_z(): lax.ppermute(block, 'z', [(i, (i + count // 2) % count) for i in range(co...  10.6 us
    ppermute x6, waiting for transfers between devices, along_y(): lax.ppermute(part, 'y', [(i, (i + s) % count) for i in range(count)])  10 us
    all_to_all x3, waiting for transfers between devices, swap(): return lax.all_to_all(block, axes, 0, 0, tiled=True)  8.59 us
    unnamed x54, local copies, waits for them, and re-layouts  4.46 us
  transfers between devices with their start and end apart: 20, of which 7 were waited for; matrix products, arithmetic and copies ran while one was open for 0% of the time, Pallas kernels for 30%

profile of v2, /device:TPU:2, one launch (start us, length us, event | category | flops | bytes accessed | tf_op | source)
XLA Modules:
  0.0 158.7 jit_solution(4614963587806034144)
XLA Ops:
  0.6 1.6 collective-permute-start.5
  2.2 1.8 %collective-permute-start.6 = (bf16[256,1152]{1,0:T(8,128)(2,1)}, bf16[256,1152]{1,0:T(8,128)(2,1)S(1)}, u32[]{:S(2)}, u32[]{:S(2)}) collective-permute-start(bf16[256,1152]{1,0:T(8,128)(2,1)} %feats_ref.2), channel_id=1, source_target_pairs={{0,2},{2,0},{1,3},{3,1},{4,6},{6,4},{5,7},{7,5},{8,10},{10,8},{9,1... | collective-permute-start | bytes 1769480 | tf_op jit(solution)/shard_map/ppermute | solution.py:441
  4.0 7.2 %collective-permute-start.7 = (bf16[256,1152]{1,0:T(8,128)(2,1)}, bf16[256,1152]{1,0:T(8,128)(2,1)S(1)}, u32[]{:S(2)}, u32[]{:S(2)}) collective-permute-start(bf16[256,1152]{1,0:T(8,128)(2,1)} %feats_ref.3), channel_id=1, source_target_pairs={{0,64},{16,80},{32,96},{48,112},{64,0},{80,16},{96,32},{112,48},{1... | collective-permute-start | bytes 1769480 | tf_op jit(solution)/shard_map/ppermute | solution.py:412
  12.5 10.4 %conditional.3 = (bf16[256,1152]{1,0:T(8,128)(2,1)}, bf16[256,1152]{1,0:T(8,128)(2,1)}, bf16[256,1152]{1,0:T(8,128)(2,1)}, f32[256,1]{1,0:T(8,128)}, bf16[256,11...) conditional(s32[]{:T(128)} %bitcast.1, () %tuple.39, ...), branch_computations={%region_0.0_spmd, %region_1.0_spmd} | conditional | flops 3000 | bytes 25955436 | solution.py:436
  12.5 0.1 collective-permute-start
  12.6 0.0 copy-start.8
  12.6 4.2 %branch_1_fun.7 = (bf16[256,1152]{1,0:T(8,128)(2,1)}, bf16[256,1152]{1,0:T(8,128)(2,1)}, f32[256,1]{1,0:T(8,128)}) custom-call(bf16[1152,1152]{1,0:T(8,128)(2,1)} %get-tuple-element.38.head_ref, bf16[256,1152]{1,0:T(8,128)(2,1)} %get-tuple-element.48.feats_ref), custom_call_target="tpu_custom_call" | custom-call | flops 1000 | bytes 1000 | tf_op jit(solution)/shard_map/cond/branch_1_fun/pallas_call | solution.py:28
  16.8 1.9 %branch_1_fun.8.refs_1_ = bf16[256,1152]{1,0:T(8,128)(2,1)} custom-call(bf16[1152,1152]{1,0:T(8,128)(2,1)S(1)} %copy-done.8, bf16[256,1152]{1,0:T(8,128)(2,1)S(1)} %collective-permute-done.feats_ref), custom_call_target="tpu_custom_call" | custom-call | flops 1000 | bytes 1000 | tf_op jit(solution)/shard_map/cond/branch_1_fun/pallas_call | solution.py:28
  18.8 4.1 %branch_1_fun.9 = (bf16[256,1152]{1,0:T(8,128)(2,1)S(1)}, f32[256,1]{1,0:T(8,128)S(1)}, bf16[2,256,256]{2,1,0:T(8,128)(2,1)S(1)}) custom-call(f32[1]{0:T(128)} %get-tuple-element.52.scale_ref, f32[1]{0:T(128)} %get-tuple-element.53.bias_ref, bf16[256,1152]{1,0:T(8,128)(2,1)S(1)} %copy-done.17, bf16[1152,1152]{1,0:T(8,128)(2,1)S(1)} %copy-done.11, ...), custom_call_target="tpu_custom_call" | custom-call | flops 1000 | bytes 1000 | tf_op jit(solution)/shard_map/cond/branch_1_fun/pallas_call | solution.py:28
  22.9 0.0 copy-start.14
  23.0 0.8 copy-done.14
  23.7 0.1 copy-done.23
  23.8 0.2 copy-done.26
  24.0 0.2 copy-done.18
  24.2 14.2 %conditional.4 = (bf16[256,1152]{1,0:T(8,128)(2,1)}, bf16[256,1152]{1,0:T(8,128)(2,1)}, bf16[256,1152]{1,0:T(8,128)(2,1)}, bf16[256,1152]{1,0:T(8,128)(2,1)}, bf...) conditional(s32[]{:T(128)} %bitcast.1, () %tuple.41, ...), branch_computations={%region_2.0_spmd, %region_3.0_spmd} | conditional | flops 3000 | bytes 23596144 | solution.py:436
  24.2 0.5 collective-permute-start.1
  24.7 4.1 %branch_1_fun.10 = (bf16[256,1152]{1,0:T(8,128)(2,1)}, bf16[256,1152]{1,0:T(8,128)(2,1)}, f32[256,1]{1,0:T(8,128)}) custom-call(bf16[1152,1152]{1,0:T(8,128)(2,1)} %get-tuple-element.68.head_ref, bf16[256,1152]{1,0:T(8,128)(2,1)S(1)} %get-tuple-element.69.feats_ref), custom_call_target="tpu_custom_call" | custom-call | flops 1000 | bytes 1000 | tf_op jit(solution)/shard_map/cond/branch_1_fun/pallas_call | solution.py:28
  28.8 1.9 %branch_1_fun.11.refs_3_ = bf16[256,1152]{1,0:T(8,128)(2,1)} custom-call(bf16[1152,1152]{1,0:T(8,128)(2,1)S(1)} %copy-done.9, bf16[256,1152]{1,0:T(8,128)(2,1)S(1)} %collective-permute-done.1.feats_ref), custom_call_target="tpu_custom_call" | custom-call | flops 1000 | bytes 1000 | tf_op jit(solution)/shard_map/cond/branch_1_fun/pallas_call | solution.py:28
  30.7 7.7 %branch_1_fun.12 = (bf16[2,256,256]{2,1,0:T(8,128)(2,1)}, bf16[256,1152]{1,0:T(8,128)(2,1)}, bf16[256,1152]{1,0:T(8,128)(2,1)}, bf16[256,1152]{1,0:T(8,128)(2,1)...) custom-call(f32[1]{0:T(128)} %get-tuple-element.59.scale_ref, ...), custom_call_target="tpu_custom_call" | custom-call | flops 1000 | bytes 1000 | tf_op jit(solution)/shard_map/cond/branch_1_fun/pallas_call | solution.py:28
  38.5 6.0 %shard_map.85 = (bf16[256,1152]{1,0:T(8,128)(2,1)S(1)}, bf16[4,256,256]{2,1,0:T(8,128)(2,1)S(1)}, bf16[256,1152]{1,0:T(8,128)(2,1)}, bf16[256,1152]{1,0:T(8,128)(2,1)S(1)}) custom-call(f32[1]{0:T(128)S(6)} %copy.47.scale_ref, f32[1]{0:T(128)S(6)} %copy.48.bias_ref, bf16[256,1152]{1,0:T(8,128)(2,1)S(1)} %collective-permute-done.7.feats_ref.refs_0_, ...), custom_call_target="tpu_custom_call" | custom-call | flops 1000 | bytes 1000 | tf_op jit(solution)/shard_map/pallas_call | solution.py:28
  44.6 2.2 %shard_map.86 = (f32[2,256,1152]{2,1,0:T(8,128)S(1)}, bf16[2,256,1152]{2,1,0:T(8,128)(2,1)}) custom-call(bf16[256,1152]{1,0:T(8,128)(2,1)S(1)} %copy-done.15, bf16[256,1152]{1,0:T(8,128)(2,1)S(1)} %copy-done.22, bf16[256,1152]{1,0:T(8,128)(2,1)S(1)} %get-tuple-element.169.refs_2_, bf16[4,256,256]{2,1,0:T(8,128)(2,1)S(1)} %copy-done.27, ...), custom_call_target="tpu_custom_call" | custom-call | flops 1000 | bytes 1000 | tf_op jit(solution)/shard_map/pallas_call | solution.py:28
  46.8 0.1 collective-permute-start.8
  47.0 4.5 %shard_map.87 = (bf16[2,288,1152]{2,1,0:T(8,128)(2,1)S(1)}, bf16[2,288,1152]{2,1,0:T(8,128)(2,1)S(1)}) custom-call(s32[1]{0:T(128)} %bitcast.core_ref, bf16[256,1152]{1,0:T(8,128)(2,1)S(1)} %collective-permute-done.7.feats_ref.refs_0_, bf16[256,1152]{1,0:T(8,128)(2,1)S(1)} %get-tuple-element.176.refs_1_, bf16[256,1152]{1,0:T(8,128)(2,1)} %feats_ref.3, ...), custom_call_target="tpu_custom_call" | custom-call | flops 1000 | bytes 1000 | tf_op jit(solution)/shard_map/pallas_call | solution.py:28
  51.5 0.5 collective-permute-start.9
  52.1 3.8 %shard_map.88 = (bf16[256,1152]{1,0:T(8,128)(2,1)S(1)}, bf16[256,1152]{1,0:T(8,128)(2,1)S(1)}, bf16[2,288,1152]{2,1,0:T(8,128)(2,1)S(1)}, bf16[2,288,1152]{2,1,0:T(8,128)(2,1)S(1)}) custom-call(s32[1]{0:T(128)} %bitcast.core_ref, f32[2,256,1152]{2,1,0:T(8,128)S(1)} %get-tuple-element.175.keep_ref, bf16[2,256,1152]{2,1,0:T(8,128)(2,1)} %collective-permute-done.8.got_ref, ...), custom_call_target="tpu_custom_call" | custom-call | flops 1000 | bytes 1000 | tf_op jit(solution)/shard_map/pallas_call | solution.py:28
  55.9 0.1 collective-permute-start.10
  56.0 1.6 shard_map.89
  57.6 1.4 collective-permute-done.10.got_ref
  59.0 1.1 copy-done.2
  60.1 3.9 %all-to-all-start.1 = ((bf16[4,144,1152]{2,1,0:T(8,128)(2,1)}), bf16[4,144,1152]{2,1,0:T(8,128)(2,1)S(1)}, u32[]{:S(2)}, u32[]{:S(2)}) async-start(bf16[4,144,1152]{2,1,0:T(8,128)(2,1)} %shard_map.89), calls=%async_computation.1 | async-start | bytes 2654208 | tf_op jit(solution)/shard_map/all_to_all | solution.py:425
  64.0 1.3 copy-done.3
  65.3 1.8 %shard_map.91 = (bf16[4,36,1152]{2,1,0:T(8,128)(2,1)S(1)}, bf16[4,36,1152]{2,1,0:T(8,128)(2,1)}, bf16[4,36,1152]{2,1,0:T(8,128)(2,1)}, bf16[4,36,1152]{2,1,0:T(8,128)(2,1)}) custom-call(s32[1]{0:T(128)} %bitcast.2.me_ref, bf16[2,288,1152]{2,1,0:T(8,128)(2,1)S(1)} %copy-done.3, bf16[2,288,1152]{2,1,0:T(8,128)(2,1)S(1)} %copy-done.1), custom_call_target="tpu_custom_call" | custom-call | flops 1000 | bytes 1000 | tf_op jit(solution)/shard_map/pallas_call | solution.py:28
  67.2 0.7 copy-done.4
  67.9 1.6 collective-permute-start.11
  69.5 2.9 %collective-permute-start.12 = (bf16[4,36,1152]{2,1,0:T(8,128)(2,1)}, bf16[4,36,1152]{2,1,0:T(8,128)(2,1)}, u32[]{:S(2)}, u32[]{:S(2)}) collective-permute-start(bf16[4,36,1152]{2,1,0:T(8,128)(2,1)} %get-tuple-element.199), channel_id=1, source_target_pairs={{0,8},{4,12},{8,0},{12,4},{1,9},{5,13},{9,1},{13,5},{2,10},{6,14},... | collective-permute-start | bytes 995336 | tf_op jit(solution)/shard_map/ppermute | solution.py:418
  72.4 1.3 collective-permute-start.13
  73.7 3.4 %collective-permute-start.14 = (bf16[256,1152]{1,0:T(8,128)(2,1)}, bf16[256,1152]{1,0:T(8,128)(2,1)S(1)}, u32[]{:S(2)}, u32[]{:S(2)}) collective-permute-start(bf16[256,1152]{1,0:T(8,128)(2,1)} %get-tuple-element.211), channel_id=1, source_target_pairs={{0,64},{16,80},{32,96},{48,112},{64,0},{80,16},{96,32},{112,48},{1... | collective-permute-start | bytes 1769480 | tf_op jit(solution)/shard_map/ppermute | solution.py:412
  77.1 1.5 collective-permute-start.15
  78.6 2.6 %all-to-all-done.1.in_ref = bf16[4,144,1152]{2,1,0:T(8,128)(2,1)S(1)} async-done(((bf16[4,144,1152]{2,1,0:T(8,128)(2,1)}), bf16[4,144,1152]{2,1,0:T(8,128)(2,1)S(1)}, u32[]{:S(2)}, u32[]{:S(2)}) %all-to-all-start.1) | async-done | bytes 1327136 | tf_op jit(solution)/shard_map/all_to_all | solution.py:425
  81.2 1.0 shard_map.90
  82.3 6.9 %collective-permute-done.12.refs_2_ = bf16[4,36,1152]{2,1,0:T(8,128)(2,1)} collective-permute-done((bf16[4,36,1152]{2,1,0:T(8,128)(2,1)}, bf16[4,36,1152]{2,1,0:T(8,128)(2,1)}, u32[]{:S(2)}, u32[]{:S(2)}) %collective-permute-start.12) | collective-permute-done | bytes 331808 | tf_op jit(solution)/shard_map/ppermute | solution.py:418
  89.2 1.4 shard_map.92
  90.6 0.0 copy-start.7
  90.6 13.7 %conditional.5 = (bf16[8,9,1152]{2,1,0:T(8,128)(2,1)S(1)}) conditional(s32[]{:T(128)} %bitcast.1, () %tuple.47, (bf16[4,36,1152]{2,1,0:T(8,128)(2,1)S(1)}, bf16[36,1152]{1,0:T(8,128)(2,1)S(1)}, bf16[36,1152]{1,0:T(8,128)(2,1)S(1)}, bf16[36,1152]{1,0:T(8,128)(2,1)}, bf16[36,1152]{1,0:T(8,128)(2,1)S(1)}) %tuple.61), branch_computations={%region_4.0_spmd, %region_5.0_spmd} | conditional | flops 1000 | bytes 3392676 | solution.py:436
  90.7 0.0 copy-start.28
  90.7 0.7 copy-done.28
  91.4 4.5 %all-to-all-start = ((bf16[4,36,1152]{2,1,0:T(8,128)(2,1)}), bf16[4,36,1152]{2,1,0:T(8,128)(2,1)S(1)}, u32[]{:S(2)}, u32[]{:S(2)}) async-start(bf16[4,36,1152]{2,1,0:T(8,128)(2,1)} %copy-done.28), calls=%async_computation | async-start | bytes 737280 | tf_op jit(solution)/shard_map/cond/branch_1_fun/all_to_all | solution.py:425
  95.9 1.1 collective-permute-start.2
  97.0 2.4 %collective-permute-start.3 = (bf16[36,1152]{1,0:T(8,128)(2,1)S(1)}, bf16[36,1152]{1,0:T(8,128)(2,1)S(1)}, u32[]{:S(2)}, u32[]{:S(2)}) collective-permute-start(bf16[36,1152]{1,0:T(8,128)(2,1)S(1)} %get-tuple-element.83), channel_id=1, source_target_pairs={{0,8},{4,12},{8,0},{12,4},{1,9},{5,13},{9,1},{13,5},{2,10},{6,14},... | collective-permute-start | bytes 248840 | tf_op jit(solution)/shard_map/cond/branch_1_fun/ppermute | solution.py:418
  99.4 1.7 %collective-permute-start.4 = (bf16[36,1152]{1,0:T(8,128)(2,1)}, bf16[36,1152]{1,0:T(8,128)(2,1)S(1)}, u32[]{:S(2)}, u32[]{:S(2)}) collective-permute-start(bf16[36,1152]{1,0:T(8,128)(2,1)} %get-tuple-element.84), channel_id=1, source_target_pairs={{0,12},{4,0},{8,4},{12,8},{1,13},{5,1},{9,5},{13,9},{2,14},{6,2},{... | collective-permute-start | bytes 248840 | tf_op jit(solution)/shard_map/cond/branch_1_fun/ppermute | solution.py:418
  101.1 1.3 collective-permute-done.2.refs_1_
  102.4 1.0 collective-permute-done.3.refs_2_
  103.4 0.8 collective-permute-done.4.refs_3_
  104.2 0.2 branch_1_fun.13
  104.3 0.3 collective-permute-start.16
  104.6 17.6 %all_to_all.24.in_ref = bf16[8,9,1152]{2,1,0:T(8,128)(2,1)S(1)} all-to-all(bf16[8,9,1152]{2,1,0:T(8,128)(2,1)S(1)} %get-tuple-element.258), channel_id=1, replica_groups=mesh['xh'=2,'z'=8,'y'=4,'xl'=2,'c'=2] {'z'}, dimensions={0} | all-to-all | bytes 331776 | tf_op jit(solution)/shard_map/all_to_all | solution.py:425
  122.3 13.8 %all_to_all.25.in_ref = bf16[8,9,1152]{2,1,0:T(8,128)(2,1)S(1)} all-to-all(bf16[8,9,1152]{2,1,0:T(8,128)(2,1)S(1)} %shard_map.95), channel_id=1, replica_groups=mesh['xh'=2,'z'=8,'y'=4,'xl'=2,'c'=2] {'z'}, dimensions={0} | all-to-all | bytes 331776 | tf_op jit(solution)/shard_map/all_to_all | solution.py:425
  136.1 1.2 shard_map.96
  137.3 3.8 %all-to-all-start.4 = ((bf16[8,72,1152]{2,1,0:T(8,128)(2,1)}), bf16[8,72,1152]{2,1,0:T(8,128)(2,1)S(1)}, u32[]{:S(2)}, u32[]{:S(2)}) async-start(bf16[8,72,1152]{2,1,0:T(8,128)(2,1)} %shard_map.96), calls=%async_computation.4 | async-start | bytes 2654208 | tf_op jit(solution)/shard_map/all_to_all | solution.py:425
  141.1 0.0 copy-start.16
  141.1 5.4 %shard_map.93 = bf16[256,1152]{1,0:T(8,128)(2,1)} custom-call(bf16[256,1152]{1,0:T(8,128)(2,1)} %feats_ref.2, bf16[1152,1152]{1,0:T(8,128)(2,1)} %head_ref.4, bf16[256,1152]{1,0:T(8,128)(2,1)S(1)} %get-tuple-element.186.refs_0_, bf16[256,1152]{1,0:T(8,128)(2,1)S(1)} %collective-permute-done.16.refs_1_), custom_call_target="tpu_custom_call" | custom-call | flops 1000 | bytes 1000 | tf_op jit(solution)/shard_map/pallas_call | solution.py:28
  146.5 4.5 %shard_map.94 = bf16[256,1152]{1,0:T(8,128)(2,1)} custom-call(bf16[256,1152]{1,0:T(8,128)(2,1)S(1)} %copy-done.16, bf16[1152,1152]{1,0:T(8,128)(2,1)S(1)} %copy-done.10, bf16[256,1152]{1,0:T(8,128)(2,1)S(1)} %copy-done.25, bf16[256,1152]{1,0:T(8,128)(2,1)} %collective-permute-done.15.refs_1_, bf16[256,1152]{1,0:T(8,128)(2,1)S(1)} %collective-permute-done.14.refs_2_), custom_call_target="tpu_custom_call" | custom-call | flops 1000 | bytes 1000 | tf_op jit(solution)/shard_map/pallas_call | solution.py:28
  151.0 5.9 %all-to-all-done.4.in_ref = bf16[8,72,1152]{2,1,0:T(8,128)(2,1)S(1)} async-done(((bf16[8,72,1152]{2,1,0:T(8,128)(2,1)}), bf16[8,72,1152]{2,1,0:T(8,128)(2,1)S(1)}, u32[]{:S(2)}, u32[]{:S(2)}) %all-to-all-start.4) | async-done | bytes 1327136 | tf_op jit(solution)/shard_map/all_to_all | solution.py:425
  156.9 1.8 %shard_map.97 = f32[288,2304]{1,0:T(8,128)} custom-call(bf16[8,72,1152]{2,1,0:T(8,128)(2,1)S(1)} %all-to-all-done.4.in_ref), custom_call_target="tpu_custom_call" | custom-call | flops 1000 | bytes 1000 | tf_op jit(solution)/shard_map/pallas_call | solution.py:28
  (67 shorter events, 0.2 us)
Async XLA Ops:
  0.6 22.3 %collective-permute-start.5 = (bf16[256,1152]{1,0:T(8,128)(2,1)}, bf16[256,1152]{1,0:T(8,128)(2,1)S(1)}, u32[]{:S(2)}, u32[]{:S(2)}) collective-permute-start(bf16[256,1152]{1,0:T(8,128)(2,1)} %feats_ref.3), channel_id=1, source_target_pairs={{0,130},{130,0},{2,128},{128,2},{1,131},{131,1},{3,129},{129,3},{4... | collective-permute-start | bytes 1769480 | tf_op jit(solution)/shard_map/ppermute | solution.py:440
  2.2 20.7 %collective-permute-start.6 = (bf16[256,1152]{1,0:T(8,128)(2,1)}, bf16[256,1152]{1,0:T(8,128)(2,1)S(1)}, u32[]{:S(2)}, u32[]{:S(2)}) collective-permute-start(bf16[256,1152]{1,0:T(8,128)(2,1)} %feats_ref.2), channel_id=1, source_target_pairs={{0,2},{2,0},{1,3},{3,1},{4,6},{6,4},{5,7},{7,5},{8,10},{10,8},{9,1... | collective-permute-start | bytes 1769480 | tf_op jit(solution)/shard_map/ppermute | solution.py:441
  4.0 34.4 %collective-permute-start.7 = (bf16[256,1152]{1,0:T(8,128)(2,1)}, bf16[256,1152]{1,0:T(8,128)(2,1)S(1)}, u32[]{:S(2)}, u32[]{:S(2)}) collective-permute-start(bf16[256,1152]{1,0:T(8,128)(2,1)} %feats_ref.3), channel_id=1, source_target_pairs={{0,64},{16,80},{32,96},{48,112},{64,0},{80,16},{96,32},{112,48},{1... | collective-permute-start | bytes 1769480 | tf_op jit(solution)/shard_map/ppermute | solution.py:412
  12.5 4.3 %collective-permute-start = (bf16[256,1152]{1,0:T(8,128)(2,1)}, bf16[256,1152]{1,0:T(8,128)(2,1)S(1)}, u32[]{:S(2)}, u32[]{:S(2)}) collective-permute-start(bf16[256,1152]{1,0:T(8,128)(2,1)} %get-tuple-element.48.feats_ref), channel_id=1, source_target_pairs={{0,1},{1,0},{2,3},{3,2},{4,5},{5,4},{6,7},{7,6},{8,9},{9,8},{10,11... | collective-permute-start | bytes 1769480 | tf_op jit(solution)/shard_map/cond/branch_1_fun/ppermute | solution.py:444
  12.6 4.2 %copy-start.8 = (bf16[1152,1152]{1,0:T(8,128)(2,1)S(1)}, bf16[1152,1152]{1,0:T(8,128)(2,1)}, u32[]{:S(2)}) copy-start(bf16[1152,1152]{1,0:T(8,128)(2,1)} %get-tuple-element.38.head_ref) | copy-start | bytes 7962628 | tf_op jit(solution)/shard_map/cond
  16.8 1.9 %copy-start.11 = (bf16[1152,1152]{1,0:T(8,128)(2,1)S(1)}, bf16[1152,1152]{1,0:T(8,128)(2,1)}, u32[]{:S(2)}) copy-start(bf16[1152,1152]{1,0:T(8,128)(2,1)} %get-tuple-element.55.head_ref) | copy-start | bytes 7962628 | tf_op jit(solution)/shard_map/cond
  16.8 1.9 %copy-start.17 = (bf16[256,1152]{1,0:T(8,128)(2,1)S(1)}, bf16[256,1152]{1,0:T(8,128)(2,1)}, u32[]{:S(2)}) copy-start(bf16[256,1152]{1,0:T(8,128)(2,1)} %get-tuple-element.54.feats_ref) | copy-start | bytes 1769476 | tf_op jit(solution)/shard_map/cond
  22.9 0.8 copy-start.14
  22.9 0.9 copy-start.23
  22.9 1.1 copy-start.26
  22.9 1.2 copy-start.18
  24.2 4.6 %collective-permute-start.1 = (bf16[256,1152]{1,0:T(8,128)(2,1)S(1)}, bf16[256,1152]{1,0:T(8,128)(2,1)S(1)}, u32[]{:S(2)}, u32[]{:S(2)}) collective-permute-start(bf16[256,1152]{1,0:T(8,128)(2,1)S(1)} %get-tuple-element.69.feats_ref), channel_id=1, source_target_pairs={{0,1},{1,0},{2,3},{3,2},{4,5},{5,4},{6,7},{7,6},{8,9},{9,8},{10,11... | collective-permute-start | bytes 1769480 | tf_op jit(solution)/shard_map/cond/branch_1_fun/ppermute | solution.py:456
  24.7 4.1 %copy-start.9 = (bf16[1152,1152]{1,0:T(8,128)(2,1)S(1)}, bf16[1152,1152]{1,0:T(8,128)(2,1)}, u32[]{:S(2)}) copy-start(bf16[1152,1152]{1,0:T(8,128)(2,1)} %get-tuple-element.68.head_ref) | copy-start | bytes 7962628 | tf_op jit(solution)/shard_map/cond
  28.8 1.9 %copy-start.12 = (bf16[1152,1152]{1,0:T(8,128)(2,1)S(1)}, bf16[1152,1152]{1,0:T(8,128)(2,1)}, u32[]{:S(2)}) copy-start(bf16[1152,1152]{1,0:T(8,128)(2,1)} %get-tuple-element.65.head_ref) | copy-start | bytes 7962628 | tf_op jit(solution)/shard_map/cond
  38.5 6.1 %copy-start.15 = (bf16[256,1152]{1,0:T(8,128)(2,1)S(1)}, bf16[256,1152]{1,0:T(8,128)(2,1)}, u32[]{:S(2)}) copy-start(bf16[256,1152]{1,0:T(8,128)(2,1)} %copy-done.14) | copy-start | bytes 1769476
  38.5 6.1 %copy-start.22 = (bf16[256,1152]{1,0:T(8,128)(2,1)S(1)}, bf16[256,1152]{1,0:T(8,128)(2,1)}, u32[]{:S(2)}) copy-start(bf16[256,1152]{1,0:T(8,128)(2,1)} %get-tuple-element.163.refs_1_) | copy-start | bytes 1769476
  38.5 6.1 %copy-start.24 = (bf16[2,256,256]{2,1,0:T(8,128)(2,1)S(1)}, bf16[2,256,256]{2,1,0:T(8,128)(2,1)}, u32[]{:S(2)}) copy-start(bf16[2,256,256]{2,1,0:T(8,128)(2,1)} %copy-done.23) | copy-start | bytes 786436
  38.5 6.1 %copy-start.27 = (bf16[4,256,256]{2,1,0:T(8,128)(2,1)S(1)}, bf16[4,256,256]{2,1,0:T(8,128)(2,1)}, u32[]{:S(2)}) copy-start(bf16[4,256,256]{2,1,0:T(8,128)(2,1)} %get-tuple-element.170.refs_3_) | copy-start | bytes 1572868
  38.5 6.1 %copy-start.29 = (bf16[2,256,256]{2,1,0:T(8,128)(2,1)S(1)}, bf16[2,256,256]{2,1,0:T(8,128)(2,1)}, u32[]{:S(2)}) copy-start(bf16[2,256,256]{2,1,0:T(8,128)(2,1)} %get-tuple-element.172.refs_6_) | copy-start | bytes 786436
  46.8 5.2 %collective-permute-start.8 = (bf16[2,256,1152]{2,1,0:T(8,128)(2,1)}, bf16[2,256,1152]{2,1,0:T(8,128)(2,1)}, u32[]{:S(2)}, u32[]{:S(2)}) collective-permute-start(bf16[2,256,1152]{2,1,0:T(8,128)(2,1)} %get-tuple-element.180), channel_id=1, source_target_pairs={{0,1},{1,0},{2,3},{3,2},{4,5},{5,4},{6,7},{7,6},{8,9},{9,8},{10,11... | collective-permute-start | bytes 3538952 | tf_op jit(solution)/shard_map/ppermute | solution.py:485
  46.9 5.1 %copy-start.13 = (bf16[256,1152]{1,0:T(8,128)(2,1)S(1)}, bf16[256,1152]{1,0:T(8,128)(2,1)}, u32[]{:S(2)}) copy-start(bf16[256,1152]{1,0:T(8,128)(2,1)} %feats_ref.2) | copy-start | bytes 1769476
  46.9 5.1 %copy-start.19 = (bf16[256,1152]{1,0:T(8,128)(2,1)S(1)}, bf16[256,1152]{1,0:T(8,128)(2,1)}, u32[]{:S(2)}) copy-start(bf16[256,1152]{1,0:T(8,128)(2,1)} %copy-done.18) | copy-start | bytes 1769476
  46.9 5.1 %copy-start.20 = (bf16[256,1152]{1,0:T(8,128)(2,1)S(1)}, bf16[256,1152]{1,0:T(8,128)(2,1)}, u32[]{:S(2)}) copy-start(bf16[256,1152]{1,0:T(8,128)(2,1)} %get-tuple-element.183.refs_1_) | copy-start | bytes 1769476
  46.9 5.1 %copy-start.21 = (bf16[256,1152]{1,0:T(8,128)(2,1)S(1)}, bf16[256,1152]{1,0:T(8,128)(2,1)}, u32[]{:S(2)}) copy-start(bf16[256,1152]{1,0:T(8,128)(2,1)} %get-tuple-element.182.refs_0_) | copy-start | bytes 1769476
  46.9 5.1 %copy-start.30 = (f32[256,1]{1,0:T(8,128)S(1)}, f32[256,1]{1,0:T(8,128)}, u32[]{:S(2)}) copy-start(f32[256,1]{1,0:T(8,128)} %get-tuple-element.185.refs_3_) | copy-start | bytes 3076
  46.9 5.1 %copy-start.31 = (f32[256,1]{1,0:T(8,128)S(1)}, f32[256,1]{1,0:T(8,128)}, u32[]{:S(2)}) copy-start(f32[256,1]{1,0:T(8,128)} %get-tuple-element.184.refs_2_) | copy-start | bytes 3076
  51.5 4.6 %collective-permute-start.9 = (bf16[2,288,1152]{2,1,0:T(8,128)(2,1)S(1)}, bf16[2,288,1152]{2,1,0:T(8,128)(2,1)S(1)}, u32[]{:S(2)}, u32[]{:S(2)}) collective-permute-start(bf16[2,288,1152]{2,1,0:T(8,128)(2,1)S(1)} %get-tuple-element.187), channel_id=1, source_target_pairs={{0,1},{1,0},{2,3},{3,2},{4,5},{5,4},{6,7},{7,6},{8,9},{9,8},{10,11... | collective-permute-start | bytes 3981320 | tf_op jit(solution)/shard_map/ppermute | solution.py:488
  55.9 1.7 %copy-start = (bf16[2,288,1152]{2,1,0:T(8,128)(2,1)}, bf16[2,288,1152]{2,1,0:T(8,128)(2,1)S(1)}, u32[]{:S(2)}) copy-start(bf16[2,288,1152]{2,1,0:T(8,128)(2,1)S(1)} %get-tuple-element.196.keep_ref) | copy-start | bytes 3981316
  55.9 1.7 %copy-start.6 = (bf16[256,1152]{1,0:T(8,128)(2,1)}, bf16[256,1152]{1,0:T(8,128)(2,1)S(1)}, u32[]{:S(2)}) copy-start(bf16[256,1152]{1,0:T(8,128)(2,1)S(1)} %get-tuple-element.214) | copy-start | bytes 1769476
  55.9 3.1 %collective-permute-start.10 = (bf16[2,288,1152]{2,1,0:T(8,128)(2,1)S(1)}, bf16[2,288,1152]{2,1,0:T(8,128)(2,1)S(1)}, u32[]{:S(2)}, u32[]{:S(2)}) collective-permute-start(bf16[2,288,1152]{2,1,0:T(8,128)(2,1)S(1)} %get-tuple-element.189), channel_id=1, source_target_pairs={{0,1},{1,0},{2,3},{3,2},{4,5},{5,4},{6,7},{7,6},{8,9},{9,8},{10,11... | collective-permute-start | bytes 3981320 | tf_op jit(solution)/shard_map/ppermute | solution.py:493
  59.0 1.1 copy-start.2
  60.1 3.9 %copy-start.1 = (bf16[2,288,1152]{2,1,0:T(8,128)(2,1)S(1)}, bf16[2,288,1152]{2,1,0:T(8,128)(2,1)}, u32[]{:S(2)}) copy-start(bf16[2,288,1152]{2,1,0:T(8,128)(2,1)} %copy-done) | copy-start | bytes 3981316
  60.1 21.1 %all-to-all-start.1 = ((bf16[4,144,1152]{2,1,0:T(8,128)(2,1)}), bf16[4,144,1152]{2,1,0:T(8,128)(2,1)S(1)}, u32[]{:S(2)}, u32[]{:S(2)}) async-start(bf16[4,144,1152]{2,1,0:T(8,128)(2,1)} %shard_map.89), calls=%async_computation.1 | async-start | bytes 2654208 | tf_op jit(solution)/shard_map/all_to_all | solution.py:425
  64.0 1.3 copy-start.3
  67.2 0.7 copy-start.4
  67.9 21.3 %copy-start.5 = (bf16[4,36,1152]{2,1,0:T(8,128)(2,1)S(1)}, bf16[4,36,1152]{2,1,0:T(8,128)(2,1)}, u32[]{:S(2)}) copy-start(bf16[4,36,1152]{2,1,0:T(8,128)(2,1)} %copy-done.4) | copy-start | bytes 995332
  67.9 14.4 %collective-permute-start.11 = (bf16[4,36,1152]{2,1,0:T(8,128)(2,1)}, bf16[4,36,1152]{2,1,0:T(8,128)(2,1)}, u32[]{:S(2)}, u32[]{:S(2)}) collective-permute-start(bf16[4,36,1152]{2,1,0:T(8,128)(2,1)} %get-tuple-element.198), channel_id=1, source_target_pairs={{0,4},{4,8},{8,12},{12,0},{1,5},{5,9},{9,13},{13,1},{2,6},{6,10},{... | collective-permute-start | bytes 995336 | tf_op jit(solution)/shard_map/ppermute | solution.py:418
  69.5 19.7 %collective-permute-start.12 = (bf16[4,36,1152]{2,1,0:T(8,128)(2,1)}, bf16[4,36,1152]{2,1,0:T(8,128)(2,1)}, u32[]{:S(2)}, u32[]{:S(2)}) collective-permute-start(bf16[4,36,1152]{2,1,0:T(8,128)(2,1)} %get-tuple-element.199), channel_id=1, source_target_pairs={{0,8},{4,12},{8,0},{12,4},{1,9},{5,13},{9,1},{13,5},{2,10},{6,14},... | collective-permute-start | bytes 995336 | tf_op jit(solution)/shard_map/ppermute | solution.py:418
  72.4 16.8 %collective-permute-start.13 = (bf16[4,36,1152]{2,1,0:T(8,128)(2,1)}, bf16[4,36,1152]{2,1,0:T(8,128)(2,1)}, u32[]{:S(2)}, u32[]{:S(2)}) collective-permute-start(bf16[4,36,1152]{2,1,0:T(8,128)(2,1)} %get-tuple-element.200), channel_id=1, source_target_pairs={{0,12},{4,0},{8,4},{12,8},{1,13},{5,1},{9,5},{13,9},{2,14},{6,2},{... | collective-permute-start | bytes 995336 | tf_op jit(solution)/shard_map/ppermute | solution.py:418
  73.7 30.9 %collective-permute-start.14 = (bf16[256,1152]{1,0:T(8,128)(2,1)}, bf16[256,1152]{1,0:T(8,128)(2,1)S(1)}, u32[]{:S(2)}, u32[]{:S(2)}) collective-permute-start(bf16[256,1152]{1,0:T(8,128)(2,1)} %get-tuple-element.211), channel_id=1, source_target_pairs={{0,64},{16,80},{32,96},{48,112},{64,0},{80,16},{96,32},{112,48},{1... | collective-permute-start | bytes 1769480 | tf_op jit(solution)/shard_map/ppermute | solution.py:412
  77.1 27.5 %collective-permute-start.15 = (bf16[256,1152]{1,0:T(8,128)(2,1)}, bf16[256,1152]{1,0:T(8,128)(2,1)}, u32[]{:S(2)}, u32[]{:S(2)}) collective-permute-start(bf16[256,1152]{1,0:T(8,128)(2,1)} %get-tuple-element.212), channel_id=1, source_target_pairs={{0,130},{130,0},{2,128},{128,2},{1,131},{131,1},{3,129},{129,3},{4... | collective-permute-start | bytes 1769480 | tf_op jit(solution)/shard_map/ppermute | solution.py:481
  82.3 8.3 %copy-start.32 = (bf16[36,1152]{1,0:T(8,128)(2,1)S(1)}, bf16[36,1152]{1,0:T(8,128)(2,1)}, u32[]{:S(2)}) copy-start(bf16[36,1152]{1,0:T(8,128)(2,1)} %get-tuple-element.206) | copy-start | bytes 248836
  90.6 13.7 %copy-start.7 = (bf16[256,1152]{1,0:T(8,128)(2,1)S(1)}, bf16[256,1152]{1,0:T(8,128)(2,1)}, u32[]{:S(2)}) copy-start(bf16[256,1152]{1,0:T(8,128)(2,1)} %copy-done.6) | copy-start | bytes 1769476
  90.7 0.7 copy-start.28
  91.4 12.8 %all-to-all-start = ((bf16[4,36,1152]{2,1,0:T(8,128)(2,1)}), bf16[4,36,1152]{2,1,0:T(8,128)(2,1)S(1)}, u32[]{:S(2)}, u32[]{:S(2)}) async-start(bf16[4,36,1152]{2,1,0:T(8,128)(2,1)} %copy-done.28), calls=%async_computation | async-start | bytes 737280 | tf_op jit(solution)/shard_map/cond/branch_1_fun/all_to_all | solution.py:425
  95.9 6.5 %collective-permute-start.2 = (bf16[36,1152]{1,0:T(8,128)(2,1)S(1)}, bf16[36,1152]{1,0:T(8,128)(2,1)S(1)}, u32[]{:S(2)}, u32[]{:S(2)}) collective-permute-start(bf16[36,1152]{1,0:T(8,128)(2,1)S(1)} %get-tuple-element.82), channel_id=1, source_target_pairs={{0,4},{4,8},{8,12},{12,0},{1,5},{5,9},{9,13},{13,1},{2,6},{6,10},{... | collective-permute-start | bytes 248840 | tf_op jit(solution)/shard_map/cond/branch_1_fun/ppermute | solution.py:418
  97.0 6.4 %collective-permute-start.3 = (bf16[36,1152]{1,0:T(8,128)(2,1)S(1)}, bf16[36,1152]{1,0:T(8,128)(2,1)S(1)}, u32[]{:S(2)}, u32[]{:S(2)}) collective-permute-start(bf16[36,1152]{1,0:T(8,128)(2,1)S(1)} %get-tuple-element.83), channel_id=1, source_target_pairs={{0,8},{4,12},{8,0},{12,4},{1,9},{5,13},{9,1},{13,5},{2,10},{6,14},... | collective-permute-start | bytes 248840 | tf_op jit(solution)/shard_map/cond/branch_1_fun/ppermute | solution.py:418
  99.4 4.8 %collective-permute-start.4 = (bf16[36,1152]{1,0:T(8,128)(2,1)}, bf16[36,1152]{1,0:T(8,128)(2,1)S(1)}, u32[]{:S(2)}, u32[]{:S(2)}) collective-permute-start(bf16[36,1152]{1,0:T(8,128)(2,1)} %get-tuple-element.84), channel_id=1, source_target_pairs={{0,12},{4,0},{8,4},{12,8},{1,13},{5,1},{9,5},{13,9},{2,14},{6,2},{... | collective-permute-start | bytes 248840 | tf_op jit(solution)/shard_map/cond/branch_1_fun/ppermute | solution.py:418
  104.3 17.9 %collective-permute-start.16 = (bf16[256,1152]{1,0:T(8,128)(2,1)S(1)}, bf16[256,1152]{1,0:T(8,128)(2,1)S(1)}, u32[]{:S(2)}, u32[]{:S(2)}) collective-permute-start(bf16[256,1152]{1,0:T(8,128)(2,1)S(1)} %copy-done.7), channel_id=1, source_target_pairs={{0,2},{2,0},{1,3},{3,1},{4,6},{6,4},{5,7},{7,5},{8,10},{10,8},{9,1... | collective-permute-start | bytes 1769480 | tf_op jit(solution)/shard_map/ppermute | solution.py:505
  137.3 19.7 %all-to-all-start.4 = ((bf16[8,72,1152]{2,1,0:T(8,128)(2,1)}), bf16[8,72,1152]{2,1,0:T(8,128)(2,1)S(1)}, u32[]{:S(2)}, u32[]{:S(2)}) async-start(bf16[8,72,1152]{2,1,0:T(8,128)(2,1)} %shard_map.96), calls=%async_computation.4 | async-start | bytes 2654208 | tf_op jit(solution)/shard_map/all_to_all | solution.py:425
  141.1 5.4 %copy-start.10 = (bf16[1152,1152]{1,0:T(8,128)(2,1)S(1)}, bf16[1152,1152]{1,0:T(8,128)(2,1)}, u32[]{:S(2)}) copy-start(bf16[1152,1152]{1,0:T(8,128)(2,1)} %head_ref.5) | copy-start | bytes 7962628
  141.1 5.4 %copy-start.16 = (bf16[256,1152]{1,0:T(8,128)(2,1)S(1)}, bf16[256,1152]{1,0:T(8,128)(2,1)}, u32[]{:S(2)}) copy-start(bf16[256,1152]{1,0:T(8,128)(2,1)} %feats_ref.3) | copy-start | bytes 1769476
  141.1 5.4 %copy-start.25 = (bf16[256,1152]{1,0:T(8,128)(2,1)S(1)}, bf16[256,1152]{1,0:T(8,128)(2,1)}, u32[]{:S(2)}) copy-start(bf16[256,1152]{1,0:T(8,128)(2,1)} %get-tuple-element.218.refs_0_) | copy-start | bytes 1769476

commit v3 on v2

--- a/solution.py
+++ b/solution.py
@@ -270,12 +270,12 @@
 
 def split_y_kernel(me_ref, got_ref, keep_ref, *refs):
     outs, held = refs[:-1], refs[-1]
-    count, blocks, rows, _ = held.shape
-    total = (keep_ref[...].astype(F32) + got_ref[...].astype(F32)).astype(BF16)
-    for b in range(blocks):
-        for k in range(count):
-            at = (b % 2 * count + k) * rows
-            held[k, b] = total[b // 2, at : at + rows]
+    count, tall, _ = held.shape
+    rows = tall // 4
+    total = keep_ref[...].astype(F32) + got_ref[...].astype(F32)
+    for k in range(count):
+        at = [(b // 2, (b % 2 * count + k) * rows) for b in range(4)]
+        held[k] = jnp.concatenate([total[h, r : r + rows] for h, r in at], axis=0).astype(BF16)
     for s, out_ref in enumerate(outs):
         out_ref[...] = held[lax.rem(me_ref[0] + s, count)]
 
@@ -283,7 +283,7 @@
 def split_y(me, keep, got):
     count = lax.axis_size("y")
     _, rows, wide = keep.shape
-    part = (4, rows // 2 // count, wide)
+    part = (2 * rows // count, wide)
     return local(
         split_y_kernel,
         [shape(part, BF16)] * count,
@@ -306,52 +306,44 @@
     total = refs[0][...].astype(F32)
     for ref in refs[1:-1]:
         total = total + ref[...].astype(F32)
-    refs[-1][...] = total.astype(BF16)
+    out_ref = refs[-1]
+    rows = out_ref.shape[1]
+    for k in range(out_ref.shape[0]):
+        out_ref[k] = total[k * rows : (k + 1) * rows].astype(BF16)
 
 
 def add_up(*parts):
-    return local(sum_kernel, shape(parts[0].shape, BF16), *parts)
-
-
-def sum_split_y_kernel(me_ref, in_ref, *refs):
-    outs, held = refs[:-1], refs[-1]
+    rows, wide = parts[0].shape
+    return local(sum_kernel, shape((4, rows // 4, wide), BF16), *parts)
+
+
+def sum_split_y_kernel(in_ref, out_ref):
     total = sum_of(in_ref).astype(BF16)
-    count, rows, _ = held.shape
-    for k in range(count):
-        held[k] = total[k * rows : (k + 1) * rows]
-    for s, out_ref in enumerate(outs):
-        out_ref[...] = held[lax.rem(me_ref[0] + s, count)]
-
-
-def sum_split_y(me, parts):
+    rows = out_ref.shape[1]
+    for k in range(out_ref.shape[0]):
+        out_ref[k] = total[k * rows : (k + 1) * rows]
+
+
+def sum_split_y(parts):
     count = lax.axis_size("y")
     _, rows, wide = parts.shape
-    part = (rows // count, wide)
-    return local(
-        sum_split_y_kernel,
-        [shape(part, BF16)] * count,
-        me,
-        parts,
-        scalars=1,
-        scratch=[pltpu.VMEM((count,) + part, BF16)],
-    )
-
-
-def split_z_kernel(img_ref, *refs):
-    txt_refs, out_ref = refs[:-1], refs[-1]
-    txt = txt_refs[0][...].astype(F32)
-    for ref in txt_refs[1:]:
-        txt = txt + ref[...].astype(F32)
-    both = jnp.concatenate([sum_of(img_ref), txt], axis=0).astype(BF16)
+    return local(sum_split_y_kernel, shape((count, rows // count, wide), BF16), parts)
+
+
+def split_z_kernel(img_ref, txt_ref, out_ref):
+    both = jnp.concatenate([sum_of(img_ref), sum_of(txt_ref)], axis=0)
+    cols = [both[:, at : at + 128] for at in range(0, both.shape[1], 128)]
+    tall = jnp.concatenate(cols, axis=0)
     rows = out_ref.shape[1]
     for k in range(out_ref.shape[0]):
-        out_ref[k] = both[k * rows : (k + 1) * rows]
-
-
-def split_z(img, txts):
+        out_ref[k] = tall[k * rows : (k + 1) * rows].astype(BF16)
+
+
+def split_z(img, txt):
     count = lax.axis_size("z")
     _, rows, wide = img.shape
-    return local(split_z_kernel, shape((count, 2 * rows // count, wide), BF16), img, *txts)
+    dims = (count, 2 * rows * wide // 128 // count, 128)
+    return local(split_z_kernel, shape(dims, BF16), img, txt)
 
 
 def sum_spread_kernel(in_ref, out_ref):
@@ -365,14 +357,17 @@
 
 
 def join_z_kernel(in_ref, out_ref):
-    both = jnp.concatenate([in_ref[k] for k in range(in_ref.shape[0])], axis=0)
+    tall = jnp.concatenate([in_ref[k].astype(F32) for k in range(in_ref.shape[0])], axis=0)
+    rows, wide = out_ref.shape[1:]
+    cols = [tall[k * rows : (k + 1) * rows] for k in range(wide // 128)]
+    both = jnp.concatenate(cols, axis=1).astype(BF16)
     for k in range(out_ref.shape[0]):
         out_ref[k] = both
 
 
-def join_z(pieces, copies):
-    count, rows, wide = pieces.shape
-    return local(join_z_kernel, shape((copies, count * rows, wide), BF16), pieces)
+def join_z(pieces, wide, copies):
+    count, rows, lanes = pieces.shape
+    return local(join_z_kernel, shape((copies, count * rows * lanes // wide, wide), BF16), pieces)
 
 
 def finish_kernel(part, in_ref, out_ref):
@@ -495,11 +490,11 @@
     txt, got_img = lax.optimization_barrier((txt, got_img))
     txt = swap(txt, ("xl", "xh"))
     img = along_y(split_y(me_y, keep, got_img))
-    txt, img = lax.optimization_barrier((sum_split_y(me_y, txt), img))
-    img = add_up(*img)
+    txt = swap(sum_split_y(txt), "y")
+    txt, img = lax.optimization_barrier((txt, add_up(*img)))
 
     def second_unit():
-        return split_z(swap(img, ("xl", "xh")), along_y(txt))
+        return split_z(swap(img, ("xl", "xh")), txt)
 
     piece, send = lax.optimization_barrier((unit(second_unit), send))
     back_img = lax.ppermute(send, "xl", SWAP)
@@ -511,7 +506,7 @@
     image_grads = feature_grads(image_feats, image_head, own, back_img)
     text_grads = feature_grads(text_feats, text_head, got["dz_txt"], back_near, back_far)
 
-    piece = join_z(swap(sum_spread(piece), "z"), lax.axis_size(("xh", "y")))
+    piece = join_z(swap(sum_spread(piece), "z"), image_head.shape[1], lax.axis_size(("xh", "y")))
     parts = lax.axis_size(("xh", "z", "y")) * lax.axis_size(("xl", "c"))
     head_grads = finish(1.0 / parts, swap(piece, ("xh", "y")))
     return (image_grads, text_grads, head_grads)

time: 159 us -> 155 us (0.975)
  starting transfers between devices: 40.3 us -> 35.7 us
  blocking collectives: 31.4 us -> 35.7 us
  waiting for transfers between devices: 20.1 us -> 17.1 us
    ppermute x6 -> x3, waiting for transfers between devices: 10 us -> 2.38 us  [along_y(): lax.ppermute(part, 'y', [(i, (i + s) % count) for i in range(count)])]
    ppermute x6 -> x3, starting transfers between devices: 11 us -> 5.22 us  [along_y(): lax.ppermute(part, 'y', [(i, (i + s) % count) for i in range(count)])]
    all_to_all x3, waiting for transfers between devices: 8.59 us -> 13.2 us  [swap(): return lax.all_to_all(block, axes, 0, 0, tiled=True)]
    all_to_all x2 -> x3, blocking collectives: 31.4 us -> 35.7 us  [swap(): return lax.all_to_all(block, axes, 0, 0, tiled=True)]
    unnamed x54 -> x52, local copies, waits for them, and re-layouts: 4.46 us -> 4.44 us
  transfers between devices with their start and end apart: 20 -> 17, of which waited for: 7 -> 5; matrix products, arithmetic and copies ran while one was open for 0% -> 0% of each run, Pallas kernels for 30% -> 31%
where the time goes in v3:
time: 155 us; the launch traced here: 154 us
  Pallas kernels  59.1 us (38%)
  starting transfers between devices  35.7 us (23%)
  blocking collectives  35.7 us (23%)
  waiting for transfers between devices  17.1 us (11%)
  local copies, waits for them, and re-layouts  4.46 us (3%)
  between operations  2.26 us (1%)
    pallas_call x20, Pallas kernels, local(): pl.pallas_call(kernel, out_shape=outs, in_specs=[smem] * scalars + [vmem]...  59.1 us
    all_to_all x3, blocking collectives, swap(): return lax.all_to_all(block, axes, 0, 0, tiled=True)  35.7 us
    all_to_all x3, waiting for transfers between devices, swap(): return lax.all_to_all(block, axes, 0, 0, tiled=True)  13.2 us
    all_to_all x3, starting transfers between devices, swap(): return lax.all_to_all(block, axes, 0, 0, tiled=True)  12.2 us
    ppermute x2, starting transfers between devices, far_z(): lax.ppermute(block, 'z', [(i, (i + count // 2) % count) for i in range(co...  10.6 us
    ppermute x3, starting transfers between devices, along_y(): lax.ppermute(part, 'y', [(i, (i + s) % count) for i in range(count)])  5.22 us
    unnamed x52, local copies, waits for them, and re-layouts  4.44 us
  transfers between devices with their start and end apart: 17, of which 5 were waited for; matrix products, arithmetic and copies ran while one was open for 0% of the time, Pallas kernels for 31%

profile of v3, /device:TPU:2, one launch (start us, length us, event | category | flops | bytes accessed | tf_op | source)
XLA Modules:
  0.0 154.4 jit_solution(3590504050142762212)
XLA Ops:
  0.6 1.6 %collective-permute-start.2 = (bf16[256,1152]{1,0:T(8,128)(2,1)}, bf16[256,1152]{1,0:T(8,128)(2,1)S(1)}, u32[]{:S(2)}, u32[]{:S(2)}) collective-permute-start(bf16[256,1152]{1,0:T(8,128)(2,1)} %feats_ref.3), channel_id=1, source_target_pairs={{0,130},{130,0},{2,128},{128,2},{1,131},{131,1},{3,129},{129,3},{4... | collective-permute-start | bytes 1769480 | tf_op jit(solution)/shard_map/ppermute | solution.py:435
  2.2 1.8 %collective-permute-start.3 = (bf16[256,1152]{1,0:T(8,128)(2,1)}, bf16[256,1152]{1,0:T(8,128)(2,1)S(1)}, u32[]{:S(2)}, u32[]{:S(2)}) collective-permute-start(bf16[256,1152]{1,0:T(8,128)(2,1)} %feats_ref.2), channel_id=1, source_target_pairs={{0,2},{2,0},{1,3},{3,1},{4,6},{6,4},{5,7},{7,5},{8,10},{10,8},{9,1... | collective-permute-start | bytes 1769480 | tf_op jit(solution)/shard_map/ppermute | solution.py:436
  4.0 7.2 %collective-permute-start.4 = (bf16[256,1152]{1,0:T(8,128)(2,1)}, bf16[256,1152]{1,0:T(8,128)(2,1)S(1)}, u32[]{:S(2)}, u32[]{:S(2)}) collective-permute-start(bf16[256,1152]{1,0:T(8,128)(2,1)} %feats_ref.3), channel_id=1, source_target_pairs={{0,64},{16,80},{32,96},{48,112},{64,0},{80,16},{96,32},{112,48},{1... | collective-permute-start | bytes 1769480 | tf_op jit(solution)/shard_map/ppermute | solution.py:407
  12.5 10.4 %conditional.3 = (bf16[256,1152]{1,0:T(8,128)(2,1)}, bf16[256,1152]{1,0:T(8,128)(2,1)}, bf16[256,1152]{1,0:T(8,128)(2,1)}, f32[256,1]{1,0:T(8,128)}, bf16[256,11...) conditional(s32[]{:T(128)} %bitcast.1, () %tuple.39, ...), branch_computations={%region_0.0_spmd, %region_1.0_spmd} | conditional | flops 3000 | bytes 25955436 | solution.py:431
  12.5 0.1 collective-permute-start
  12.6 0.0 copy-start.8
  12.6 4.2 %branch_1_fun.7 = (bf16[256,1152]{1,0:T(8,128)(2,1)}, bf16[256,1152]{1,0:T(8,128)(2,1)}, f32[256,1]{1,0:T(8,128)}) custom-call(bf16[1152,1152]{1,0:T(8,128)(2,1)} %get-tuple-element.38.head_ref, bf16[256,1152]{1,0:T(8,128)(2,1)} %get-tuple-element.42.feats_ref), custom_call_target="tpu_custom_call" | custom-call | flops 1000 | bytes 1000 | tf_op jit(solution)/shard_map/cond/branch_1_fun/pallas_call | solution.py:28
  16.8 0.0 collective-permute-done.feats_ref
  16.8 1.9 %branch_1_fun.8.refs_1_ = bf16[256,1152]{1,0:T(8,128)(2,1)} custom-call(bf16[1152,1152]{1,0:T(8,128)(2,1)S(1)} %copy-done.8, bf16[256,1152]{1,0:T(8,128)(2,1)S(1)} %collective-permute-done.feats_ref), custom_call_target="tpu_custom_call" | custom-call | flops 1000 | bytes 1000 | tf_op jit(solution)/shard_map/cond/branch_1_fun/pallas_call | solution.py:28
  18.8 4.1 %branch_1_fun.9 = (bf16[256,1152]{1,0:T(8,128)(2,1)S(1)}, f32[256,1]{1,0:T(8,128)S(1)}, bf16[2,256,256]{2,1,0:T(8,128)(2,1)S(1)}) custom-call(f32[1]{0:T(128)} %get-tuple-element.46.scale_ref, f32[1]{0:T(128)} %get-tuple-element.47.bias_ref, bf16[256,1152]{1,0:T(8,128)(2,1)S(1)} %copy-done.17, bf16[1152,1152]{1,0:T(8,128)(2,1)S(1)} %copy-done.11, ...), custom_call_target="tpu_custom_call" | custom-call | flops 1000 | bytes 1000 | tf_op jit(solution)/shard_map/cond/branch_1_fun/pallas_call | solution.py:28
  22.9 0.0 copy-start.14
  22.9 0.0 collective-permute-done.3.refs_5_
  23.0 0.8 copy-done.14
  23.7 0.1 copy-done.23
  23.8 0.2 copy-done.26
  24.0 0.2 copy-done.18
  24.2 14.3 %conditional.4 = (bf16[256,1152]{1,0:T(8,128)(2,1)}, bf16[256,1152]{1,0:T(8,128)(2,1)}, bf16[256,1152]{1,0:T(8,128)(2,1)}, bf16[256,1152]{1,0:T(8,128)(2,1)}, bf...) conditional(s32[]{:T(128)} %bitcast.1, () %tuple.41, ...), branch_computations={%region_2.0_spmd, %region_3.0_spmd} | conditional | flops 3000 | bytes 23596144 | solution.py:431
  24.2 0.5 collective-permute-start.1
  24.7 4.1 %branch_1_fun.10 = (bf16[256,1152]{1,0:T(8,128)(2,1)}, bf16[256,1152]{1,0:T(8,128)(2,1)}, f32[256,1]{1,0:T(8,128)}) custom-call(bf16[1152,1152]{1,0:T(8,128)(2,1)} %get-tuple-element.62.head_ref, bf16[256,1152]{1,0:T(8,128)(2,1)S(1)} %get-tuple-element.63.feats_ref), custom_call_target="tpu_custom_call" | custom-call | flops 1000 | bytes 1000 | tf_op jit(solution)/shard_map/cond/branch_1_fun/pallas_call | solution.py:28
  28.8 1.9 %branch_1_fun.11.refs_3_ = bf16[256,1152]{1,0:T(8,128)(2,1)} custom-call(bf16[1152,1152]{1,0:T(8,128)(2,1)S(1)} %copy-done.9, bf16[256,1152]{1,0:T(8,128)(2,1)S(1)} %collective-permute-done.1.feats_ref), custom_call_target="tpu_custom_call" | custom-call | flops 1000 | bytes 1000 | tf_op jit(solution)/shard_map/cond/branch_1_fun/pallas_call | solution.py:28
  30.7 7.7 %branch_1_fun.12 = (bf16[2,256,256]{2,1,0:T(8,128)(2,1)}, bf16[256,1152]{1,0:T(8,128)(2,1)}, bf16[256,1152]{1,0:T(8,128)(2,1)}, bf16[256,1152]{1,0:T(8,128)(2,1)...) custom-call(f32[1]{0:T(128)} %get-tuple-element.53.scale_ref, ...), custom_call_target="tpu_custom_call" | custom-call | flops 1000 | bytes 1000 | tf_op jit(solution)/shard_map/cond/branch_1_fun/pallas_call | solution.py:28
  38.5 0.0 collective-permute-done.4.feats_ref.refs_0_
  38.5 6.1 %shard_map.85 = (bf16[256,1152]{1,0:T(8,128)(2,1)S(1)}, bf16[4,256,256]{2,1,0:T(8,128)(2,1)S(1)}, bf16[256,1152]{1,0:T(8,128)(2,1)}, bf16[256,1152]{1,0:T(8,128)(2,1)S(1)}) custom-call(f32[1]{0:T(128)S(6)} %copy.47.scale_ref, f32[1]{0:T(128)S(6)} %copy.48.bias_ref, bf16[256,1152]{1,0:T(8,128)(2,1)S(1)} %collective-permute-done.4.feats_ref.refs_0_, ...), custom_call_target="tpu_custom_call" | custom-call | flops 1000 | bytes 1000 | tf_op jit(solution)/shard_map/pallas_call | solution.py:28
  44.6 2.2 %shard_map.86 = (f32[2,256,1152]{2,1,0:T(8,128)S(1)}, bf16[2,256,1152]{2,1,0:T(8,128)(2,1)}) custom-call(bf16[256,1152]{1,0:T(8,128)(2,1)S(1)} %copy-done.15, bf16[256,1152]{1,0:T(8,128)(2,1)S(1)} %copy-done.22, bf16[256,1152]{1,0:T(8,128)(2,1)S(1)} %get-tuple-element.150.refs_2_, bf16[4,256,256]{2,1,0:T(8,128)(2,1)S(1)} %copy-done.27, ...), custom_call_target="tpu_custom_call" | custom-call | flops 1000 | bytes 1000 | tf_op jit(solution)/shard_map/pallas_call | solution.py:28
  46.8 0.1 collective-permute-start.5
  47.0 4.5 %shard_map.87 = (bf16[2,288,1152]{2,1,0:T(8,128)(2,1)S(1)}, bf16[2,288,1152]{2,1,0:T(8,128)(2,1)S(1)}) custom-call(s32[1]{0:T(128)} %bitcast.core_ref, bf16[256,1152]{1,0:T(8,128)(2,1)S(1)} %collective-permute-done.4.feats_ref.refs_0_, bf16[256,1152]{1,0:T(8,128)(2,1)S(1)} %get-tuple-element.157.refs_1_, bf16[256,1152]{1,0:T(8,128)(2,1)} %feats_ref.3, ...), custom_call_target="tpu_custom_call" | custom-call | flops 1000 | bytes 1000 | tf_op jit(solution)/shard_map/pallas_call | solution.py:28
  51.5 0.5 collective-permute-start.6
  52.1 0.0 collective-permute-done.5.got_ref
  52.1 3.8 %shard_map.88 = (bf16[256,1152]{1,0:T(8,128)(2,1)S(1)}, bf16[256,1152]{1,0:T(8,128)(2,1)S(1)}, bf16[2,288,1152]{2,1,0:T(8,128)(2,1)S(1)}, bf16[2,288,1152]{2,1,0:T(8,128)(2,1)S(1)}) custom-call(s32[1]{0:T(128)} %bitcast.core_ref, f32[2,256,1152]{2,1,0:T(8,128)S(1)} %get-tuple-element.156.keep_ref, bf16[2,256,1152]{2,1,0:T(8,128)(2,1)} %collective-permute-done.5.got_ref, ...), custom_call_target="tpu_custom_call" | custom-call | flops 1000 | bytes 1000 | tf_op jit(solution)/shard_map/pallas_call | solution.py:28
  55.9 0.0 copy-start.6
  55.9 0.1 collective-permute-start.7
  56.1 1.5 shard_map.89
  57.6 1.5 collective-permute-done.7.got_ref
  59.1 1.1 copy-done.2
  60.1 3.9 %all-to-all-start.1 = ((bf16[4,144,1152]{2,1,0:T(8,128)(2,1)}), bf16[4,144,1152]{2,1,0:T(8,128)(2,1)S(1)}, u32[]{:S(2)}, u32[]{:S(2)}) async-start(bf16[4,144,1152]{2,1,0:T(8,128)(2,1)} %shard_map.89), calls=%async_computation.1 | async-start | bytes 2654208 | tf_op jit(solution)/shard_map/all_to_all | solution.py:420
  64.1 0.0 copy-start.3
  64.1 1.3 copy-done.3
  65.4 1.7 %shard_map.91 = (bf16[144,1152]{1,0:T(8,128)(2,1)S(1)}, bf16[144,1152]{1,0:T(8,128)(2,1)}, bf16[144,1152]{1,0:T(8,128)(2,1)}, bf16[144,1152]{1,0:T(8,128)(2,1)}) custom-call(s32[1]{0:T(128)} %bitcast.2.me_ref, bf16[2,288,1152]{2,1,0:T(8,128)(2,1)S(1)} %copy-done.3, bf16[2,288,1152]{2,1,0:T(8,128)(2,1)S(1)} %copy-done.1), custom_call_target="tpu_custom_call" | custom-call | flops 1000 | bytes 1000 | tf_op jit(solution)/shard_map/pallas_call | solution.py:28
  67.1 0.7 copy-done.4
  67.8 3.0 %collective-permute-start.10 = (bf16[144,1152]{1,0:T(8,128)(2,1)}, bf16[144,1152]{1,0:T(8,128)(2,1)}, u32[]{:S(2)}, u32[]{:S(2)}) collective-permute-start(bf16[144,1152]{1,0:T(8,128)(2,1)} %get-tuple-element.177), channel_id=1, source_target_pairs={{0,12},{4,0},{8,4},{12,8},{1,13},{5,1},{9,5},{13,9},{2,14},{6,2},{... | collective-permute-start | bytes 995336 | tf_op jit(solution)/shard_map/ppermute | solution.py:413
  70.9 0.0 collective-permute-start.8
  70.9 2.2 %collective-permute-start.9 = (bf16[144,1152]{1,0:T(8,128)(2,1)}, bf16[144,1152]{1,0:T(8,128)(2,1)}, u32[]{:S(2)}, u32[]{:S(2)}) collective-permute-start(bf16[144,1152]{1,0:T(8,128)(2,1)} %get-tuple-element.176), channel_id=1, source_target_pairs={{0,8},{4,12},{8,0},{12,4},{1,9},{5,13},{9,1},{13,5},{2,10},{6,14},... | collective-permute-start | bytes 995336 | tf_op jit(solution)/shard_map/ppermute | solution.py:413
  73.1 3.4 %collective-permute-start.11 = (bf16[256,1152]{1,0:T(8,128)(2,1)}, bf16[256,1152]{1,0:T(8,128)(2,1)S(1)}, u32[]{:S(2)}, u32[]{:S(2)}) collective-permute-start(bf16[256,1152]{1,0:T(8,128)(2,1)} %get-tuple-element.182), channel_id=1, source_target_pairs={{0,64},{16,80},{32,96},{48,112},{64,0},{80,16},{96,32},{112,48},{1... | collective-permute-start | bytes 1769480 | tf_op jit(solution)/shard_map/ppermute | solution.py:407
  76.4 1.5 collective-permute-start.12
  77.9 3.4 %all-to-all-done.1.in_ref = bf16[4,144,1152]{2,1,0:T(8,128)(2,1)S(1)} async-done(((bf16[4,144,1152]{2,1,0:T(8,128)(2,1)}), bf16[4,144,1152]{2,1,0:T(8,128)(2,1)S(1)}, u32[]{:S(2)}, u32[]{:S(2)}) %all-to-all-start.1) | async-done | bytes 1327136 | tf_op jit(solution)/shard_map/all_to_all | solution.py:420
  81.3 0.9 shard_map.90
  82.2 4.5 %all-to-all-start.2 = ((bf16[4,36,1152]{2,1,0:T(8,128)(2,1)}), bf16[4,36,1152]{2,1,0:T(8,128)(2,1)S(1)}, u32[]{:S(2)}, u32[]{:S(2)}) async-start(bf16[4,36,1152]{2,1,0:T(8,128)(2,1)} %shard_map.90), calls=%async_computation.2 | async-start | bytes 737280 | tf_op jit(solution)/shard_map/all_to_all | solution.py:420
  86.7 2.4 %collective-permute-done.8.refs_1_ = bf16[144,1152]{1,0:T(8,128)(2,1)} collective-permute-done((bf16[144,1152]{1,0:T(8,128)(2,1)}, bf16[144,1152]{1,0:T(8,128)(2,1)}, u32[]{:S(2)}, u32[]{:S(2)}) %collective-permute-start.8) | collective-permute-done | bytes 331808 | tf_op jit(solution)/shard_map/ppermute | solution.py:413
  89.1 1.4 shard_map.92
  90.4 0.0 copy-start.7
  90.4 3.5 %all-to-all-done.2 = bf16[4,36,1152]{2,1,0:T(8,128)(2,1)S(1)} async-done(((bf16[4,36,1152]{2,1,0:T(8,128)(2,1)}), bf16[4,36,1152]{2,1,0:T(8,128)(2,1)S(1)}, u32[]{:S(2)}, u32[]{:S(2)}) %all-to-all-start.2) | async-done | bytes 331808 | tf_op jit(solution)/shard_map/all_to_all | solution.py:420
  93.9 9.6 %conditional.5 = (bf16[8,81,128]{2,1,0:T(8,128)(2,1)S(1)}) conditional(s32[]{:T(128)} %bitcast.1, () %tuple.47, (bf16[4,36,1152]{2,1,0:T(8,128)(2,1)S(1)}, bf16[4,36,1152]{2,1,0:T(8,128)(2,1)S(1)}) %tuple.50), branch_computations={%region_4.0_spmd, %region_5.0_spmd} | conditional | flops 1000 | bytes 664560 | solution.py:431
  93.9 9.5 %all_to_all.29.img_ref = bf16[4,36,1152]{2,1,0:T(8,128)(2,1)S(1)} all-to-all(bf16[4,36,1152]{2,1,0:T(8,128)(2,1)S(1)} %get-tuple-element.74), channel_id=1, replica_groups=mesh['xh'=2,'z'=8,'y'=4,'xl'=2,'c'=2] {'xl','xh'}, dimensions={0} | all-to-all | bytes 663552 | tf_op jit(solution)/shard_map/cond/branch_1_fun/all_to_all | solution.py:420
  103.4 0.2 branch_1_fun.13
  103.6 1.5 collective-permute-start.13
  105.1 14.3 %all_to_all.30.in_ref = bf16[8,81,128]{2,1,0:T(8,128)(2,1)S(1)} all-to-all(bf16[8,81,128]{2,1,0:T(8,128)(2,1)S(1)} %get-tuple-element.229), channel_id=1, replica_groups=mesh['xh'=2,'z'=8,'y'=4,'xl'=2,'c'=2] {'z'}, dimensions={0} | all-to-all | bytes 331776 | tf_op jit(solution)/shard_map/all_to_all | solution.py:420
  119.4 12.0 %all_to_all.31.in_ref = bf16[8,81,128]{2,1,0:T(8,128)(2,1)S(1)} all-to-all(bf16[8,81,128]{2,1,0:T(8,128)(2,1)S(1)} %shard_map.95), channel_id=1, replica_groups=mesh['xh'=2,'z'=8,'y'=4,'xl'=2,'c'=2] {'z'}, dimensions={0} | all-to-all | bytes 331776 | tf_op jit(solution)/shard_map/all_to_all | solution.py:420
  131.4 1.2 shard_map.96
  132.6 3.8 %all-to-all-start.5 = ((bf16[8,72,1152]{2,1,0:T(8,128)(2,1)}), bf16[8,72,1152]{2,1,0:T(8,128)(2,1)S(1)}, u32[]{:S(2)}, u32[]{:S(2)}) async-start(bf16[8,72,1152]{2,1,0:T(8,128)(2,1)} %shard_map.96), calls=%async_computation.5 | async-start | bytes 2654208 | tf_op jit(solution)/shard_map/all_to_all | solution.py:420
  136.4 0.0 copy-start.16
  136.4 5.4 %shard_map.93 = bf16[256,1152]{1,0:T(8,128)(2,1)} custom-call(bf16[256,1152]{1,0:T(8,128)(2,1)} %feats_ref.2, bf16[1152,1152]{1,0:T(8,128)(2,1)} %head_ref.4, bf16[256,1152]{1,0:T(8,128)(2,1)S(1)} %get-tuple-element.167.refs_0_, bf16[256,1152]{1,0:T(8,128)(2,1)S(1)} %collective-permute-done.13.refs_1_), custom_call_target="tpu_custom_call" | custom-call | flops 1000 | bytes 1000 | tf_op jit(solution)/shard_map/pallas_call | solution.py:28
  141.8 4.5 %shard_map.94 = bf16[256,1152]{1,0:T(8,128)(2,1)} custom-call(bf16[256,1152]{1,0:T(8,128)(2,1)S(1)} %copy-done.16, bf16[1152,1152]{1,0:T(8,128)(2,1)S(1)} %copy-done.10, bf16[256,1152]{1,0:T(8,128)(2,1)S(1)} %copy-done.25, bf16[256,1152]{1,0:T(8,128)(2,1)} %collective-permute-done.12.refs_1_, bf16[256,1152]{1,0:T(8,128)(2,1)S(1)} %collective-permute-done.11.refs_2_), custom_call_target="tpu_custom_call" | custom-call | flops 1000 | bytes 1000 | tf_op jit(solution)/shard_map/pallas_call | solution.py:28
  146.3 6.3 %all-to-all-done.5.in_ref = bf16[8,72,1152]{2,1,0:T(8,128)(2,1)S(1)} async-done(((bf16[8,72,1152]{2,1,0:T(8,128)(2,1)}), bf16[8,72,1152]{2,1,0:T(8,128)(2,1)S(1)}, u32[]{:S(2)}, u32[]{:S(2)}) %all-to-all-start.5) | async-done | bytes 1327136 | tf_op jit(solution)/shard_map/all_to_all | solution.py:420
  152.6 1.8 %shard_map.97 = f32[288,2304]{1,0:T(8,128)} custom-call(bf16[8,72,1152]{2,1,0:T(8,128)(2,1)S(1)} %all-to-all-done.5.in_ref), custom_call_target="tpu_custom_call" | custom-call | flops 1000 | bytes 1000 | tf_op jit(solution)/shard_map/pallas_call | solution.py:28
  (58 shorter events, 0.2 us)
Async XLA Ops:
  0.6 22.3 %collective-permute-start.2 = (bf16[256,1152]{1,0:T(8,128)(2,1)}, bf16[256,1152]{1,0:T(8,128)(2,1)S(1)}, u32[]{:S(2)}, u32[]{:S(2)}) collective-permute-start(bf16[256,1152]{1,0:T(8,128)(2,1)} %feats_ref.3), channel_id=1, source_target_pairs={{0,130},{130,0},{2,128},{128,2},{1,131},{131,1},{3,129},{129,3},{4... | collective-permute-start | bytes 1769480 | tf_op jit(solution)/shard_map/ppermute | solution.py:435
  2.2 20.7 %collective-permute-start.3 = (bf16[256,1152]{1,0:T(8,128)(2,1)}, bf16[256,1152]{1,0:T(8,128)(2,1)S(1)}, u32[]{:S(2)}, u32[]{:S(2)}) collective-permute-start(bf16[256,1152]{1,0:T(8,128)(2,1)} %feats_ref.2), channel_id=1, source_target_pairs={{0,2},{2,0},{1,3},{3,1},{4,6},{6,4},{5,7},{7,5},{8,10},{10,8},{9,1... | collective-permute-start | bytes 1769480 | tf_op jit(solution)/shard_map/ppermute | solution.py:436
  4.0 34.5 %collective-permute-start.4 = (bf16[256,1152]{1,0:T(8,128)(2,1)}, bf16[256,1152]{1,0:T(8,128)(2,1)S(1)}, u32[]{:S(2)}, u32[]{:S(2)}) collective-permute-start(bf16[256,1152]{1,0:T(8,128)(2,1)} %feats_ref.3), channel_id=1, source_target_pairs={{0,64},{16,80},{32,96},{48,112},{64,0},{80,16},{96,32},{112,48},{1... | collective-permute-start | bytes 1769480 | tf_op jit(solution)/shard_map/ppermute | solution.py:407
  12.5 4.3 %collective-permute-start = (bf16[256,1152]{1,0:T(8,128)(2,1)}, bf16[256,1152]{1,0:T(8,128)(2,1)S(1)}, u32[]{:S(2)}, u32[]{:S(2)}) collective-permute-start(bf16[256,1152]{1,0:T(8,128)(2,1)} %get-tuple-element.42.feats_ref), channel_id=1, source_target_pairs={{0,1},{1,0},{2,3},{3,2},{4,5},{5,4},{6,7},{7,6},{8,9},{9,8},{10,11... | collective-permute-start | bytes 1769480 | tf_op jit(solution)/shard_map/cond/branch_1_fun/ppermute | solution.py:439
  12.6 4.2 %copy-start.8 = (bf16[1152,1152]{1,0:T(8,128)(2,1)S(1)}, bf16[1152,1152]{1,0:T(8,128)(2,1)}, u32[]{:S(2)}) copy-start(bf16[1152,1152]{1,0:T(8,128)(2,1)} %get-tuple-element.38.head_ref) | copy-start | bytes 7962628 | tf_op jit(solution)/shard_map/cond
  16.8 1.9 %copy-start.11 = (bf16[1152,1152]{1,0:T(8,128)(2,1)S(1)}, bf16[1152,1152]{1,0:T(8,128)(2,1)}, u32[]{:S(2)}) copy-start(bf16[1152,1152]{1,0:T(8,128)(2,1)} %get-tuple-element.49.head_ref) | copy-start | bytes 7962628 | tf_op jit(solution)/shard_map/cond
  16.8 1.9 %copy-start.17 = (bf16[256,1152]{1,0:T(8,128)(2,1)S(1)}, bf16[256,1152]{1,0:T(8,128)(2,1)}, u32[]{:S(2)}) copy-start(bf16[256,1152]{1,0:T(8,128)(2,1)} %get-tuple-element.48.feats_ref) | copy-start | bytes 1769476 | tf_op jit(solution)/shard_map/cond
  22.9 0.8 copy-start.14
  22.9 0.9 copy-start.23
  22.9 1.1 copy-start.26
  22.9 1.2 copy-start.18
  24.2 4.6 %collective-permute-start.1 = (bf16[256,1152]{1,0:T(8,128)(2,1)S(1)}, bf16[256,1152]{1,0:T(8,128)(2,1)S(1)}, u32[]{:S(2)}, u32[]{:S(2)}) collective-permute-start(bf16[256,1152]{1,0:T(8,128)(2,1)S(1)} %get-tuple-element.63.feats_ref), channel_id=1, source_target_pairs={{0,1},{1,0},{2,3},{3,2},{4,5},{5,4},{6,7},{7,6},{8,9},{9,8},{10,11... | collective-permute-start | bytes 1769480 | tf_op jit(solution)/shard_map/cond/branch_1_fun/ppermute | solution.py:451
  24.7 4.1 %copy-start.9 = (bf16[1152,1152]{1,0:T(8,128)(2,1)S(1)}, bf16[1152,1152]{1,0:T(8,128)(2,1)}, u32[]{:S(2)}) copy-start(bf16[1152,1152]{1,0:T(8,128)(2,1)} %get-tuple-element.62.head_ref) | copy-start | bytes 7962628 | tf_op jit(solution)/shard_map/cond
  28.8 1.9 %copy-start.12 = (bf16[1152,1152]{1,0:T(8,128)(2,1)S(1)}, bf16[1152,1152]{1,0:T(8,128)(2,1)}, u32[]{:S(2)}) copy-start(bf16[1152,1152]{1,0:T(8,128)(2,1)} %get-tuple-element.59.head_ref) | copy-start | bytes 7962628 | tf_op jit(solution)/shard_map/cond
  38.5 6.1 %copy-start.15 = (bf16[256,1152]{1,0:T(8,128)(2,1)S(1)}, bf16[256,1152]{1,0:T(8,128)(2,1)}, u32[]{:S(2)}) copy-start(bf16[256,1152]{1,0:T(8,128)(2,1)} %copy-done.14) | copy-start | bytes 1769476
  38.5 6.1 %copy-start.22 = (bf16[256,1152]{1,0:T(8,128)(2,1)S(1)}, bf16[256,1152]{1,0:T(8,128)(2,1)}, u32[]{:S(2)}) copy-start(bf16[256,1152]{1,0:T(8,128)(2,1)} %get-tuple-element.144.refs_1_) | copy-start | bytes 1769476
  38.5 6.1 %copy-start.24 = (bf16[2,256,256]{2,1,0:T(8,128)(2,1)S(1)}, bf16[2,256,256]{2,1,0:T(8,128)(2,1)}, u32[]{:S(2)}) copy-start(bf16[2,256,256]{2,1,0:T(8,128)(2,1)} %copy-done.23) | copy-start | bytes 786436
  38.5 6.1 %copy-start.27 = (bf16[4,256,256]{2,1,0:T(8,128)(2,1)S(1)}, bf16[4,256,256]{2,1,0:T(8,128)(2,1)}, u32[]{:S(2)}) copy-start(bf16[4,256,256]{2,1,0:T(8,128)(2,1)} %get-tuple-element.151.refs_3_) | copy-start | bytes 1572868
  38.5 6.1 %copy-start.28 = (bf16[2,256,256]{2,1,0:T(8,128)(2,1)S(1)}, bf16[2,256,256]{2,1,0:T(8,128)(2,1)}, u32[]{:S(2)}) copy-start(bf16[2,256,256]{2,1,0:T(8,128)(2,1)} %get-tuple-element.153.refs_6_) | copy-start | bytes 786436
  46.8 5.2 %collective-permute-start.5 = (bf16[2,256,1152]{2,1,0:T(8,128)(2,1)}, bf16[2,256,1152]{2,1,0:T(8,128)(2,1)}, u32[]{:S(2)}, u32[]{:S(2)}) collective-permute-start(bf16[2,256,1152]{2,1,0:T(8,128)(2,1)} %get-tuple-element.161), channel_id=1, source_target_pairs={{0,1},{1,0},{2,3},{3,2},{4,5},{5,4},{6,7},{7,6},{8,9},{9,8},{10,11... | collective-permute-start | bytes 3538952 | tf_op jit(solution)/shard_map/ppermute | solution.py:480
  47.0 5.1 %copy-start.13 = (bf16[256,1152]{1,0:T(8,128)(2,1)S(1)}, bf16[256,1152]{1,0:T(8,128)(2,1)}, u32[]{:S(2)}) copy-start(bf16[256,1152]{1,0:T(8,128)(2,1)} %feats_ref.2) | copy-start | bytes 1769476
  47.0 5.1 %copy-start.19 = (bf16[256,1152]{1,0:T(8,128)(2,1)S(1)}, bf16[256,1152]{1,0:T(8,128)(2,1)}, u32[]{:S(2)}) copy-start(bf16[256,1152]{1,0:T(8,128)(2,1)} %copy-done.18) | copy-start | bytes 1769476
  47.0 5.1 %copy-start.20 = (bf16[256,1152]{1,0:T(8,128)(2,1)S(1)}, bf16[256,1152]{1,0:T(8,128)(2,1)}, u32[]{:S(2)}) copy-start(bf16[256,1152]{1,0:T(8,128)(2,1)} %get-tuple-element.164.refs_1_) | copy-start | bytes 1769476
  47.0 5.1 %copy-start.21 = (bf16[256,1152]{1,0:T(8,128)(2,1)S(1)}, bf16[256,1152]{1,0:T(8,128)(2,1)}, u32[]{:S(2)}) copy-start(bf16[256,1152]{1,0:T(8,128)(2,1)} %get-tuple-element.163.refs_0_) | copy-start | bytes 1769476
  47.0 5.1 %copy-start.29 = (f32[256,1]{1,0:T(8,128)S(1)}, f32[256,1]{1,0:T(8,128)}, u32[]{:S(2)}) copy-start(f32[256,1]{1,0:T(8,128)} %get-tuple-element.166.refs_3_) | copy-start | bytes 3076
  47.0 5.1 %copy-start.30 = (f32[256,1]{1,0:T(8,128)S(1)}, f32[256,1]{1,0:T(8,128)}, u32[]{:S(2)}) copy-start(f32[256,1]{1,0:T(8,128)} %get-tuple-element.165.refs_2_) | copy-start | bytes 3076
  51.5 4.6 %collective-permute-start.6 = (bf16[2,288,1152]{2,1,0:T(8,128)(2,1)S(1)}, bf16[2,288,1152]{2,1,0:T(8,128)(2,1)S(1)}, u32[]{:S(2)}, u32[]{:S(2)}) collective-permute-start(bf16[2,288,1152]{2,1,0:T(8,128)(2,1)S(1)} %get-tuple-element.168), channel_id=1, source_target_pairs={{0,1},{1,0},{2,3},{3,2},{4,5},{5,4},{6,7},{7,6},{8,9},{9,8},{10,11... | collective-permute-start | bytes 3981320 | tf_op jit(solution)/shard_map/ppermute | solution.py:483
  55.9 1.7 %copy-start = (bf16[2,288,1152]{2,1,0:T(8,128)(2,1)}, bf16[2,288,1152]{2,1,0:T(8,128)(2,1)S(1)}, u32[]{:S(2)}) copy-start(bf16[2,288,1152]{2,1,0:T(8,128)(2,1)S(1)} %get-tuple-element.173.keep_ref) | copy-start | bytes 3981316
  55.9 1.7 %copy-start.6 = (bf16[256,1152]{1,0:T(8,128)(2,1)}, bf16[256,1152]{1,0:T(8,128)(2,1)S(1)}, u32[]{:S(2)}) copy-start(bf16[256,1152]{1,0:T(8,128)(2,1)S(1)} %get-tuple-element.185) | copy-start | bytes 1769476
  55.9 3.1 %collective-permute-start.7 = (bf16[2,288,1152]{2,1,0:T(8,128)(2,1)S(1)}, bf16[2,288,1152]{2,1,0:T(8,128)(2,1)S(1)}, u32[]{:S(2)}, u32[]{:S(2)}) collective-permute-start(bf16[2,288,1152]{2,1,0:T(8,128)(2,1)S(1)} %get-tuple-element.170), channel_id=1, source_target_pairs={{0,1},{1,0},{2,3},{3,2},{4,5},{5,4},{6,7},{7,6},{8,9},{9,8},{10,11... | collective-permute-start | bytes 3981320 | tf_op jit(solution)/shard_map/ppermute | solution.py:488
  59.1 1.1 copy-start.2
  60.1 3.9 %copy-start.1 = (bf16[2,288,1152]{2,1,0:T(8,128)(2,1)S(1)}, bf16[2,288,1152]{2,1,0:T(8,128)(2,1)}, u32[]{:S(2)}) copy-start(bf16[2,288,1152]{2,1,0:T(8,128)(2,1)} %copy-done) | copy-start | bytes 3981316
  60.1 21.1 %all-to-all-start.1 = ((bf16[4,144,1152]{2,1,0:T(8,128)(2,1)}), bf16[4,144,1152]{2,1,0:T(8,128)(2,1)S(1)}, u32[]{:S(2)}, u32[]{:S(2)}) async-start(bf16[4,144,1152]{2,1,0:T(8,128)(2,1)} %shard_map.89), calls=%async_computation.1 | async-start | bytes 2654208 | tf_op jit(solution)/shard_map/all_to_all | solution.py:420
  64.1 1.3 copy-start.3
  67.1 0.7 copy-start.4
  67.8 21.2 %copy-start.5 = (bf16[144,1152]{1,0:T(8,128)(2,1)S(1)}, bf16[144,1152]{1,0:T(8,128)(2,1)}, u32[]{:S(2)}) copy-start(bf16[144,1152]{1,0:T(8,128)(2,1)} %copy-done.4) | copy-start | bytes 995332
  67.8 18.8 %collective-permute-start.10 = (bf16[144,1152]{1,0:T(8,128)(2,1)}, bf16[144,1152]{1,0:T(8,128)(2,1)}, u32[]{:S(2)}, u32[]{:S(2)}) collective-permute-start(bf16[144,1152]{1,0:T(8,128)(2,1)} %get-tuple-element.177), channel_id=1, source_target_pairs={{0,12},{4,0},{8,4},{12,8},{1,13},{5,1},{9,5},{13,9},{2,14},{6,2},{... | collective-permute-start | bytes 995336 | tf_op jit(solution)/shard_map/ppermute | solution.py:413
  70.9 18.2 %collective-permute-start.8 = (bf16[144,1152]{1,0:T(8,128)(2,1)}, bf16[144,1152]{1,0:T(8,128)(2,1)}, u32[]{:S(2)}, u32[]{:S(2)}) collective-permute-start(bf16[144,1152]{1,0:T(8,128)(2,1)} %get-tuple-element.175), channel_id=1, source_target_pairs={{0,4},{4,8},{8,12},{12,0},{1,5},{5,9},{9,13},{13,1},{2,6},{6,10},{... | collective-permute-start | bytes 995336 | tf_op jit(solution)/shard_map/ppermute | solution.py:413
  70.9 18.2 %collective-permute-start.9 = (bf16[144,1152]{1,0:T(8,128)(2,1)}, bf16[144,1152]{1,0:T(8,128)(2,1)}, u32[]{:S(2)}, u32[]{:S(2)}) collective-permute-start(bf16[144,1152]{1,0:T(8,128)(2,1)} %get-tuple-element.176), channel_id=1, source_target_pairs={{0,8},{4,12},{8,0},{12,4},{1,9},{5,13},{9,1},{13,5},{2,10},{6,14},... | collective-permute-start | bytes 995336 | tf_op jit(solution)/shard_map/ppermute | solution.py:413
  73.1 32.1 %collective-permute-start.11 = (bf16[256,1152]{1,0:T(8,128)(2,1)}, bf16[256,1152]{1,0:T(8,128)(2,1)S(1)}, u32[]{:S(2)}, u32[]{:S(2)}) collective-permute-start(bf16[256,1152]{1,0:T(8,128)(2,1)} %get-tuple-element.182), channel_id=1, source_target_pairs={{0,64},{16,80},{32,96},{48,112},{64,0},{80,16},{96,32},{112,48},{1... | collective-permute-start | bytes 1769480 | tf_op jit(solution)/shard_map/ppermute | solution.py:407
  76.4 28.7 %collective-permute-start.12 = (bf16[256,1152]{1,0:T(8,128)(2,1)}, bf16[256,1152]{1,0:T(8,128)(2,1)}, u32[]{:S(2)}, u32[]{:S(2)}) collective-permute-start(bf16[256,1152]{1,0:T(8,128)(2,1)} %get-tuple-element.183), channel_id=1, source_target_pairs={{0,130},{130,0},{2,128},{128,2},{1,131},{131,1},{3,129},{129,3},{4... | collective-permute-start | bytes 1769480 | tf_op jit(solution)/shard_map/ppermute | solution.py:476
  82.2 11.7 %all-to-all-start.2 = ((bf16[4,36,1152]{2,1,0:T(8,128)(2,1)}), bf16[4,36,1152]{2,1,0:T(8,128)(2,1)S(1)}, u32[]{:S(2)}, u32[]{:S(2)}) async-start(bf16[4,36,1152]{2,1,0:T(8,128)(2,1)} %shard_map.90), calls=%async_computation.2 | async-start | bytes 737280 | tf_op jit(solution)/shard_map/all_to_all | solution.py:420
  90.4 13.1 %copy-start.7 = (bf16[256,1152]{1,0:T(8,128)(2,1)S(1)}, bf16[256,1152]{1,0:T(8,128)(2,1)}, u32[]{:S(2)}) copy-start(bf16[256,1152]{1,0:T(8,128)(2,1)} %copy-done.6) | copy-start | bytes 1769476
  103.6 15.8 %collective-permute-start.13 = (bf16[256,1152]{1,0:T(8,128)(2,1)S(1)}, bf16[256,1152]{1,0:T(8,128)(2,1)S(1)}, u32[]{:S(2)}, u32[]{:S(2)}) collective-permute-start(bf16[256,1152]{1,0:T(8,128)(2,1)S(1)} %copy-done.7), channel_id=1, source_target_pairs={{0,2},{2,0},{1,3},{3,1},{4,6},{6,4},{5,7},{7,5},{8,10},{10,8},{9,1... | collective-permute-start | bytes 1769480 | tf_op jit(solution)/shard_map/ppermute | solution.py:500
  132.6 20.0 %all-to-all-start.5 = ((bf16[8,72,1152]{2,1,0:T(8,128)(2,1)}), bf16[8,72,1152]{2,1,0:T(8,128)(2,1)S(1)}, u32[]{:S(2)}, u32[]{:S(2)}) async-start(bf16[8,72,1152]{2,1,0:T(8,128)(2,1)} %shard_map.96), calls=%async_computation.5 | async-start | bytes 2654208 | tf_op jit(solution)/shard_map/all_to_all | solution.py:420
  136.4 5.4 %copy-start.10 = (bf16[1152,1152]{1,0:T(8,128)(2,1)S(1)}, bf16[1152,1152]{1,0:T(8,128)(2,1)}, u32[]{:S(2)}) copy-start(bf16[1152,1152]{1,0:T(8,128)(2,1)} %head_ref.5) | copy-start | bytes 7962628
  136.4 5.4 %copy-start.16 = (bf16[256,1152]{1,0:T(8,128)(2,1)S(1)}, bf16[256,1152]{1,0:T(8,128)(2,1)}, u32[]{:S(2)}) copy-start(bf16[256,1152]{1,0:T(8,128)(2,1)} %feats_ref.3) | copy-start | bytes 1769476
  136.4 5.4 %copy-start.25 = (bf16[256,1152]{1,0:T(8,128)(2,1)S(1)}, bf16[256,1152]{1,0:T(8,128)(2,1)}, u32[]{:S(2)}) copy-start(bf16[256,1152]{1,0:T(8,128)(2,1)} %get-tuple-element.189.refs_0_) | copy-start | bytes 1769476

commit v4 on v3

--- a/solution.py
+++ b/solution.py
@@ -473,32 +473,40 @@
         scale, bias, far, text_head, [zb_img, zb_core] + got["imgs"]
     )
     back_far = far_z(back_far)
-    back_near = lax.ppermute(got["back_near"], X_RING, CROSS)
+    keep_txt, send = text_head_part(core, far, du_far, text_feats, dus[0], near, dus[1])
+    got_txt = lax.ppermute(send, "c", SWAP)
+    keep_txt, w_far = lax.optimization_barrier((keep_txt, w_far))
     keep_dz, send_dz = image_side(
         [zb_txt, got["zb_near"], zb_far], [got["w_near"], w_far], [w_first, got["w_rest"]]
     )
     got_dz = lax.ppermute(send_dz, "c", SWAP)
-    keep_dz, du_far = lax.optimization_barrier((keep_dz, du_far))
-    keep_txt, send = text_head_part(core, far, du_far, text_feats, dus[0], near, dus[1])
-    got_txt = lax.ppermute(send, "c", SWAP)
-    keep_txt, got_dz = lax.optimization_barrier((keep_txt, got_dz))
-    own, send, keep, part = image_head_part(
-        core, keep_dz, got_dz, [late_img, got["late"]], [inv_img, got["inv"]], [image_feats, next_feats]
-    )
-    got_img = lax.ppermute(part, "c", SWAP)
     txt = split_x(keep_txt, got_txt)
-    txt, got_img = lax.optimization_barrier((txt, got_img))
+    txt, got_dz = lax.optimization_barrier((txt, got_dz))
     txt = swap(txt, ("xl", "xh"))
-    img = along_y(split_y(me_y, keep, got_img))
+
+    def image_unit():
+        own, send, keep, part = image_head_part(
+            core,
+            keep_dz,
+            got_dz,
+            [late_img, got["late"]],
+            [inv_img, got["inv"]],
+            [image_feats, next_feats],
+        )
+        return own, send, split_y(me_y, keep, lax.ppermute(part, "c", SWAP))
+
+    own, send, img = unit(image_unit)
+    img = along_y(img)
     txt = swap(sum_split_y(txt), "y")
     txt, img = lax.optimization_barrier((txt, add_up(*img)))
 
     def second_unit():
         return split_z(swap(img, ("xl", "xh")), txt)
 
-    piece, send = lax.optimization_barrier((unit(second_unit), send))
+    piece, send, back_near = lax.optimization_barrier((unit(second_unit), send, got["back_near"]))
     back_img = lax.ppermute(send, "xl", SWAP)
-    piece, back_far, back_near = lax.optimization_barrier((piece, back_far, back_near))
+    back_near = lax.ppermute(back_near, X_RING, CROSS)
+    piece, back_far = lax.optimization_barrier((piece, back_far))
     piece = swap(piece, "z")
     piece, back_img, back_far, back_near = lax.optimization_barrier(
         (piece, back_img, back_far, back_near)

time: 155 us -> 156 us (level)
  waiting for transfers between devices: 17.1 us -> 22.1 us
  local copies, waits for them, and re-layouts: 4.46 us -> 0.94 us
  starting transfers between devices: 35.7 us -> 33.6 us
    ppermute x3, waiting for transfers between devices: 2.38 us -> 9.87 us  [along_y(): lax.ppermute(part, 'y', [(i, (i + s) % count) for i in range(count)])]
    all_to_all x3, waiting for transfers between devices: 13.2 us -> 8.15 us  [swap(): return lax.all_to_all(block, axes, 0, 0, tiled=True)]
    unnamed x52 -> x36, local copies, waits for them, and re-layouts: 4.44 us -> 0.92 us
  transfers between devices with their start and end apart: 17 -> 17, of which waited for: 5 -> 6; matrix products, arithmetic and copies ran while one was open for 0% -> 0% of each run, Pallas kernels for 31% -> 30%
where the time goes in v4:
time: 156 us; the launch traced here: 155 us
  Pallas kernels  59.4 us (38%)
  blocking collectives  36.9 us (24%)
  starting transfers between devices  33.6 us (22%)
  waiting for transfers between devices  22.1 us (14%)
  between operations  2.2 us (1%)
    pallas_call x20, Pallas kernels, local(): pl.pallas_call(kernel, out_shape=outs, in_specs=[smem] * scalars + [vmem]...  59.4 us
    all_to_all x3, blocking collectives, swap(): return lax.all_to_all(block, axes, 0, 0, tiled=True)  36.9 us
    all_to_all x3, starting transfers between devices, swap(): return lax.all_to_all(block, axes, 0, 0, tiled=True)  10.8 us
    ppermute x2, starting transfers between devices, far_z(): lax.ppermute(block, 'z', [(i, (i + count // 2) % count) for i in range(co...  10.7 us
    ppermute x3, waiting for transfers between devices, along_y(): lax.ppermute(part, 'y', [(i, (i + s) % count) for i in range(count)])  9.87 us
    all_to_all x3, waiting for transfers between devices, swap(): return lax.all_to_all(block, axes, 0, 0, tiled=True)  8.15 us
    ppermute x3, starting transfers between devices, along_y(): lax.ppermute(part, 'y', [(i, (i + s) % count) for i in range(count)])  5.22 us
  transfers between devices with their start and end apart: 17, of which 6 were waited for; matrix products, arithmetic and copies ran while one was open for 0% of the time, Pallas kernels for 30%

profile of v4, /device:TPU:2, one launch (start us, length us, event | category | flops | bytes accessed | tf_op | source)
XLA Modules:
  0.0 155.2 jit_solution(17679750317831666191)
XLA Ops:
  0.6 1.6 %collective-permute-start.3 = (bf16[256,1152]{1,0:T(8,128)(2,1)}, bf16[256,1152]{1,0:T(8,128)(2,1)}, u32[]{:S(2)}, u32[]{:S(2)}) collective-permute-start(bf16[256,1152]{1,0:T(8,128)(2,1)} %feats_ref.3), channel_id=1, source_target_pairs={{0,130},{130,0},{2,128},{128,2},{1,131},{131,1},{3,129},{129,3},{4... | collective-permute-start | bytes 1769480 | tf_op jit(solution)/shard_map/ppermute | solution.py:435
  2.2 1.8 %collective-permute-start.4 = (bf16[256,1152]{1,0:T(8,128)(2,1)}, bf16[256,1152]{1,0:T(8,128)(2,1)}, u32[]{:S(2)}, u32[]{:S(2)}) collective-permute-start(bf16[256,1152]{1,0:T(8,128)(2,1)} %feats_ref.2), channel_id=1, source_target_pairs={{0,2},{2,0},{1,3},{3,1},{4,6},{6,4},{5,7},{7,5},{8,10},{10,8},{9,1... | collective-permute-start | bytes 1769480 | tf_op jit(solution)/shard_map/ppermute | solution.py:436
  4.0 7.2 %collective-permute-start.5 = (bf16[256,1152]{1,0:T(8,128)(2,1)}, bf16[256,1152]{1,0:T(8,128)(2,1)S(1)}, u32[]{:S(2)}, u32[]{:S(2)}) collective-permute-start(bf16[256,1152]{1,0:T(8,128)(2,1)} %feats_ref.3), channel_id=1, source_target_pairs={{0,64},{16,80},{32,96},{48,112},{64,0},{80,16},{96,32},{112,48},{1... | collective-permute-start | bytes 1769480 | tf_op jit(solution)/shard_map/ppermute | solution.py:407
  12.5 10.4 %conditional.4 = (bf16[256,1152]{1,0:T(8,128)(2,1)}, bf16[256,1152]{1,0:T(8,128)(2,1)}, bf16[256,1152]{1,0:T(8,128)(2,1)}, f32[256,1]{1,0:T(8,128)}, bf16[256,11...) conditional(s32[]{:T(128)} %bitcast.1, () %tuple.47, ...), branch_computations={%region_0.0_spmd, %region_1.0_spmd} | conditional | flops 3000 | bytes 25955436 | solution.py:431
  12.5 0.1 collective-permute-start
  12.6 0.0 copy-start
  12.6 4.2 %branch_1_fun.9 = (bf16[256,1152]{1,0:T(8,128)(2,1)}, bf16[256,1152]{1,0:T(8,128)(2,1)}, f32[256,1]{1,0:T(8,128)}) custom-call(bf16[1152,1152]{1,0:T(8,128)(2,1)} %get-tuple-element.62.head_ref, bf16[256,1152]{1,0:T(8,128)(2,1)} %get-tuple-element.63.feats_ref), custom_call_target="tpu_custom_call" | custom-call | flops 1000 | bytes 1000 | tf_op jit(solution)/shard_map/cond/branch_1_fun/pallas_call | solution.py:28
  16.8 0.0 collective-permute-done.feats_ref
  16.8 1.9 %branch_1_fun.10.refs_1_ = bf16[256,1152]{1,0:T(8,128)(2,1)} custom-call(bf16[1152,1152]{1,0:T(8,128)(2,1)S(1)} %copy-done, bf16[256,1152]{1,0:T(8,128)(2,1)S(1)} %collective-permute-done.feats_ref), custom_call_target="tpu_custom_call" | custom-call | flops 1000 | bytes 1000 | tf_op jit(solution)/shard_map/cond/branch_1_fun/pallas_call | solution.py:28
  18.8 4.1 %branch_1_fun.11 = (bf16[256,1152]{1,0:T(8,128)(2,1)S(1)}, f32[256,1]{1,0:T(8,128)S(1)}, bf16[2,256,256]{2,1,0:T(8,128)(2,1)S(1)}) custom-call(f32[1]{0:T(128)} %get-tuple-element.67.scale_ref, f32[1]{0:T(128)} %get-tuple-element.68.bias_ref, bf16[256,1152]{1,0:T(8,128)(2,1)S(1)} %copy-done.10, bf16[1152,1152]{1,0:T(8,128)(2,1)S(1)} %copy-done.3, ...), custom_call_target="tpu_custom_call" | custom-call | flops 1000 | bytes 1000 | tf_op jit(solution)/shard_map/cond/branch_1_fun/pallas_call | solution.py:28
  22.9 0.0 copy-start.6
  22.9 0.0 collective-permute-done.3.refs_4_
  22.9 0.0 collective-permute-done.4
  22.9 0.8 copy-done.6
  23.7 0.1 copy-done.13
  23.8 14.6 %conditional.5 = (bf16[256,1152]{1,0:T(8,128)(2,1)}, bf16[256,1152]{1,0:T(8,128)(2,1)}, bf16[256,1152]{1,0:T(8,128)(2,1)}, bf16[256,1152]{1,0:T(8,128)(2,1)}, bf...) conditional(s32[]{:T(128)} %bitcast.1, () %tuple.49, ...), branch_computations={%region_2.0_spmd, %region_3.0_spmd} | conditional | flops 3000 | bytes 23596144 | solution.py:431
  23.8 0.5 collective-permute-start.1
  24.3 4.3 %branch_1_fun.12 = (bf16[256,1152]{1,0:T(8,128)(2,1)}, bf16[256,1152]{1,0:T(8,128)(2,1)}, f32[256,1]{1,0:T(8,128)}) custom-call(bf16[1152,1152]{1,0:T(8,128)(2,1)} %get-tuple-element.83.head_ref, bf16[256,1152]{1,0:T(8,128)(2,1)} %get-tuple-element.84.feats_ref), custom_call_target="tpu_custom_call" | custom-call | flops 1000 | bytes 1000 | tf_op jit(solution)/shard_map/cond/branch_1_fun/pallas_call | solution.py:28
  28.5 0.0 collective-permute-done.1.feats_ref
  28.5 2.0 %branch_1_fun.13.refs_3_ = bf16[256,1152]{1,0:T(8,128)(2,1)} custom-call(bf16[1152,1152]{1,0:T(8,128)(2,1)S(1)} %copy-done.1, bf16[256,1152]{1,0:T(8,128)(2,1)S(1)} %collective-permute-done.1.feats_ref), custom_call_target="tpu_custom_call" | custom-call | flops 1000 | bytes 1000 | tf_op jit(solution)/shard_map/cond/branch_1_fun/pallas_call | solution.py:28
  30.5 7.9 %branch_1_fun.14 = (bf16[2,256,256]{2,1,0:T(8,128)(2,1)}, bf16[256,1152]{1,0:T(8,128)(2,1)}, bf16[256,1152]{1,0:T(8,128)(2,1)}, bf16[256,1152]{1,0:T(8,128)(2,1)...) custom-call(f32[1]{0:T(128)} %get-tuple-element.74.scale_ref, ...), custom_call_target="tpu_custom_call" | custom-call | flops 1000 | bytes 1000 | tf_op jit(solution)/shard_map/cond/branch_1_fun/pallas_call | solution.py:28
  38.4 0.0 collective-permute-done.5.feats_ref.refs_0_
  38.4 5.3 %shard_map.85 = (bf16[256,1152]{1,0:T(8,128)(2,1)S(1)}, bf16[4,256,256]{2,1,0:T(8,128)(2,1)S(1)}, bf16[256,1152]{1,0:T(8,128)(2,1)S(1)}, bf16[256,1152]{1,0:T(8,128)(2,1)S(1)}) custom-call(f32[1]{0:T(128)S(6)} %copy.59.scale_ref, f32[1]{0:T(128)S(6)} %copy.60.bias_ref, bf16[256,1152]{1,0:T(8,128)(2,1)S(1)} %collective-permute-done.5.feats_ref.refs_0_, ...), custom_call_target="tpu_custom_call" | custom-call | flops 1000 | bytes 1000 | tf_op jit(solution)/shard_map/pallas_call | solution.py:28
  43.8 0.0 copy-start.7
  43.8 4.0 %shard_map.86 = (bf16[2,288,1152]{2,1,0:T(8,128)(2,1)S(1)}, bf16[2,288,1152]{2,1,0:T(8,128)(2,1)S(1)}) custom-call(s32[1]{0:T(128)} %bitcast.2.core_ref, bf16[256,1152]{1,0:T(8,128)(2,1)S(1)} %collective-permute-done.5.feats_ref.refs_0_, bf16[256,1152]{1,0:T(8,128)(2,1)S(1)} %get-tuple-element.187.refs_1_, bf16[256,1152]{1,0:T(8,128)(2,1)S(1)} %copy-done.8, ...), custom_call_target="tpu_custom_call" | custom-call | flops 1000 | bytes 1000 | tf_op jit(solution)/shard_map/pallas_call | solution.py:28
  47.8 0.1 collective-permute-start.6
  48.0 3.6 %shard_map.87 = (f32[2,256,1152]{2,1,0:T(8,128)}, bf16[2,256,1152]{2,1,0:T(8,128)(2,1)S(1)}) custom-call(bf16[256,1152]{1,0:T(8,128)(2,1)S(1)} %copy-done.7, bf16[256,1152]{1,0:T(8,128)(2,1)S(1)} %copy-done.12, bf16[256,1152]{1,0:T(8,128)(2,1)S(1)} %get-tuple-element.185.refs_2_, bf16[4,256,256]{2,1,0:T(8,128)(2,1)S(1)} %copy-done.18, ...), custom_call_target="tpu_custom_call" | custom-call | flops 1000 | bytes 1000 | tf_op jit(solution)/shard_map/pallas_call | solution.py:28
  51.6 0.5 collective-permute-start.7
  52.1 1.4 shard_map.88
  53.5 1.2 collective-permute-done.7
  54.7 3.7 %all-to-all-start.1 = ((bf16[4,144,1152]{2,1,0:T(8,128)(2,1)}), bf16[4,144,1152]{2,1,0:T(8,128)(2,1)S(1)}, u32[]{:S(2)}, u32[]{:S(2)}) async-start(bf16[4,144,1152]{2,1,0:T(8,128)(2,1)} %shard_map.88), calls=%async_computation.1 | async-start | bytes 2654208 | tf_op jit(solution)/shard_map/all_to_all | solution.py:420
  58.4 9.8 %conditional.6 = (bf16[256,1152]{1,0:T(8,128)(2,1)}, bf16[256,1152]{1,0:T(8,128)(2,1)}, bf16[144,1152]{1,0:T(8,128)(2,1)}, bf16[144,1152]{1,0:T(8,128)(2,1)}, bf...) conditional(s32[]{:T(128)} %bitcast.1, () %tuple.46, (s32[1]{0:T(128)}, f32[2,256,1152]{2,1,0:T(8,128)}, ...), branch_computations={%region_4.0_spmd, %region_5.0_spmd} | conditional | flops 2000 | bytes 5310504 | solution.py:431
  58.5 4.8 %branch_1_fun.15 = (bf16[256,1152]{1,0:T(8,128)(2,1)}, bf16[256,1152]{1,0:T(8,128)(2,1)}, bf16[2,288,1152]{2,1,0:T(8,128)(2,1)S(1)}, bf16[2,288,1152]{2,1,0:T(8,128)(2,1)S(1)}) custom-call(s32[1]{0:T(128)} %get-tuple-element.95.core_ref, f32[2,256,1152]{2,1,0:T(8,128)} %get-tuple-element.96.keep_ref, bf16[2,256,1152]{2,1,0:T(8,128)(2,1)} %get-tuple-element.97.got_ref, ...), custom_call_target="tpu_custom_call" | custom-call | flops 1000 | bytes 1000 | tf_op jit(solution)/shard_map/cond/branch_1_fun/pallas_call | solution.py:28
  63.2 0.3 collective-permute-start.2
  63.5 2.9 %collective-permute-done.2.got_ref = bf16[2,288,1152]{2,1,0:T(8,128)(2,1)S(1)} collective-permute-done((bf16[2,288,1152]{2,1,0:T(8,128)(2,1)S(1)}, bf16[2,288,1152]{2,1,0:T(8,128)(2,1)S(1)}, u32[]{:S(2)}, u32[]{:S(2)}) %collective-permute-start.2) | collective-permute-done | bytes 1327136 | tf_op jit(solution)/shard_map/cond/branch_1_fun/ppermute | solution.py:496
  66.4 1.8 %branch_1_fun.16 = (bf16[144,1152]{1,0:T(8,128)(2,1)}, bf16[144,1152]{1,0:T(8,128)(2,1)}, bf16[144,1152]{1,0:T(8,128)(2,1)}, bf16[144,1152]{1,0:T(8,128)(2,1)}) custom-call(s32[1]{0:T(128)} %bitcast.me_ref, bf16[2,288,1152]{2,1,0:T(8,128)(2,1)S(1)} %collective-permute-done.2.got_ref, bf16[2,288,1152]{2,1,0:T(8,128)(2,1)S(1)} %get-tuple-element.108.keep_ref), custom_call_target="tpu_custom_call" | custom-call | flops 1000 | bytes 1000 | tf_op jit(solution)/shard_map/cond/branch_1_fun/pallas_call | solution.py:28
  68.2 3.0 %collective-permute-start.10 = (bf16[144,1152]{1,0:T(8,128)(2,1)}, bf16[144,1152]{1,0:T(8,128)(2,1)S(1)}, u32[]{:S(2)}, u32[]{:S(2)}) collective-permute-start(bf16[144,1152]{1,0:T(8,128)(2,1)} %get-tuple-element.208), channel_id=1, source_target_pairs={{0,12},{4,0},{8,4},{12,8},{1,13},{5,1},{9,5},{13,9},{2,14},{6,2},{... | collective-permute-start | bytes 995336 | tf_op jit(solution)/shard_map/ppermute | solution.py:413
  71.2 2.2 %collective-permute-start.9 = (bf16[144,1152]{1,0:T(8,128)(2,1)}, bf16[144,1152]{1,0:T(8,128)(2,1)S(1)}, u32[]{:S(2)}, u32[]{:S(2)}) collective-permute-start(bf16[144,1152]{1,0:T(8,128)(2,1)} %get-tuple-element.207), channel_id=1, source_target_pairs={{0,8},{4,12},{8,0},{12,4},{1,9},{5,13},{9,1},{13,5},{2,10},{6,14},... | collective-permute-start | bytes 995336 | tf_op jit(solution)/shard_map/ppermute | solution.py:413
  73.4 3.5 %collective-permute-start.11 = (bf16[256,1152]{1,0:T(8,128)(2,1)S(1)}, bf16[256,1152]{1,0:T(8,128)(2,1)S(1)}, u32[]{:S(2)}, u32[]{:S(2)}) collective-permute-start(bf16[256,1152]{1,0:T(8,128)(2,1)S(1)} %get-tuple-element.214), channel_id=1, source_target_pairs={{0,64},{16,80},{32,96},{48,112},{64,0},{80,16},{96,32},{112,48},{1... | collective-permute-start | bytes 1769480 | tf_op jit(solution)/shard_map/ppermute | solution.py:407
  76.9 0.0 all-to-all-done.1.in_ref
  76.9 0.9 shard_map.89
  77.8 3.5 %all-to-all-start.2 = ((bf16[4,36,1152]{2,1,0:T(8,128)(2,1)}), bf16[4,36,1152]{2,1,0:T(8,128)(2,1)S(1)}, u32[]{:S(2)}, u32[]{:S(2)}) async-start(bf16[4,36,1152]{2,1,0:T(8,128)(2,1)} %shard_map.89), calls=%async_computation.2 | async-start | bytes 737280 | tf_op jit(solution)/shard_map/all_to_all | solution.py:420
  81.3 6.0 %collective-permute-done.10.refs_3_ = bf16[144,1152]{1,0:T(8,128)(2,1)S(1)} collective-permute-done((bf16[144,1152]{1,0:T(8,128)(2,1)}, bf16[144,1152]{1,0:T(8,128)(2,1)S(1)}, u32[]{:S(2)}, u32[]{:S(2)}) %collective-permute-start.10) | collective-permute-done | bytes 331808 | tf_op jit(solution)/shard_map/ppermute | solution.py:413
  87.3 3.8 %collective-permute-done.8.refs_1_ = bf16[144,1152]{1,0:T(8,128)(2,1)S(1)} collective-permute-done((bf16[144,1152]{1,0:T(8,128)(2,1)}, bf16[144,1152]{1,0:T(8,128)(2,1)S(1)}, u32[]{:S(2)}, u32[]{:S(2)}) %collective-permute-start.8) | collective-permute-done | bytes 331808 | tf_op jit(solution)/shard_map/ppermute | solution.py:413
  91.2 1.2 shard_map.90
  92.3 1.0 all-to-all-done.2
  93.3 10.2 %conditional.7 = (bf16[8,81,128]{2,1,0:T(8,128)(2,1)S(1)}) conditional(s32[]{:T(128)} %bitcast.1, () %tuple.56, (bf16[4,36,1152]{2,1,0:T(8,128)(2,1)S(1)}, bf16[4,36,1152]{2,1,0:T(8,128)(2,1)S(1)}) %tuple.58), branch_computations={%region_6.0_spmd, %region_7.0_spmd} | conditional | flops 1000 | bytes 664560 | solution.py:431
  93.3 10.0 %all_to_all.29.img_ref = bf16[4,36,1152]{2,1,0:T(8,128)(2,1)S(1)} all-to-all(bf16[4,36,1152]{2,1,0:T(8,128)(2,1)S(1)} %get-tuple-element.113), channel_id=1, replica_groups=mesh['xh'=2,'z'=8,'y'=4,'xl'=2,'c'=2] {'xl','xh'}, dimensions={0} | all-to-all | bytes 663552 | tf_op jit(solution)/shard_map/cond/branch_1_fun/all_to_all | solution.py:420
  103.4 0.2 branch_1_fun.17
  103.5 1.5 collective-permute-start.12
  105.1 0.6 collective-permute-start.13
  105.7 0.0 collective-permute-done.11.refs_2_
  105.7 14.3 %all_to_all.30.in_ref = bf16[8,81,128]{2,1,0:T(8,128)(2,1)S(1)} all-to-all(bf16[8,81,128]{2,1,0:T(8,128)(2,1)S(1)} %get-tuple-element.272), channel_id=1, replica_groups=mesh['xh'=2,'z'=8,'y'=4,'xl'=2,'c'=2] {'z'}, dimensions={0} | all-to-all | bytes 331776 | tf_op jit(solution)/shard_map/all_to_all | solution.py:420
  120.0 0.0 collective-permute-done.12.refs_1_
  120.0 0.0 collective-permute-done.13.refs_1_
  120.0 12.5 %all_to_all.31.in_ref = bf16[8,81,128]{2,1,0:T(8,128)(2,1)S(1)} all-to-all(bf16[8,81,128]{2,1,0:T(8,128)(2,1)S(1)} %shard_map.93), channel_id=1, replica_groups=mesh['xh'=2,'z'=8,'y'=4,'xl'=2,'c'=2] {'z'}, dimensions={0} | all-to-all | bytes 331776 | tf_op jit(solution)/shard_map/all_to_all | solution.py:420
  132.5 1.2 shard_map.94
  133.7 3.6 %all-to-all-start.5 = ((bf16[8,72,1152]{2,1,0:T(8,128)(2,1)}), bf16[8,72,1152]{2,1,0:T(8,128)(2,1)S(1)}, u32[]{:S(2)}, u32[]{:S(2)}) async-start(bf16[8,72,1152]{2,1,0:T(8,128)(2,1)} %shard_map.94), calls=%async_computation.5 | async-start | bytes 2654208 | tf_op jit(solution)/shard_map/all_to_all | solution.py:420
  137.3 0.0 copy-start.2
  137.3 0.0 copy-start.9
  137.3 5.5 %shard_map.91 = bf16[256,1152]{1,0:T(8,128)(2,1)} custom-call(bf16[256,1152]{1,0:T(8,128)(2,1)} %feats_ref.2, bf16[1152,1152]{1,0:T(8,128)(2,1)} %head_ref.4, bf16[256,1152]{1,0:T(8,128)(2,1)} %get-tuple-element.203.refs_0_, bf16[256,1152]{1,0:T(8,128)(2,1)S(1)} %collective-permute-done.12.refs_1_), custom_call_target="tpu_custom_call" | custom-call | flops 1000 | bytes 1000 | tf_op jit(solution)/shard_map/pallas_call | solution.py:28
  142.8 3.4 %shard_map.92 = bf16[256,1152]{1,0:T(8,128)(2,1)} custom-call(bf16[256,1152]{1,0:T(8,128)(2,1)S(1)} %copy-done.9, bf16[1152,1152]{1,0:T(8,128)(2,1)S(1)} %copy-done.2, bf16[256,1152]{1,0:T(8,128)(2,1)S(1)} %copy-done.15, bf16[256,1152]{1,0:T(8,128)(2,1)S(1)} %collective-permute-done.13.refs_1_, bf16[256,1152]{1,0:T(8,128)(2,1)S(1)} %collective-permute-done.11.refs_2_), custom_call_target="tpu_custom_call" | custom-call | flops 1000 | bytes 1000 | tf_op jit(solution)/shard_map/pallas_call | solution.py:28
  146.2 7.2 %all-to-all-done.5.in_ref = bf16[8,72,1152]{2,1,0:T(8,128)(2,1)S(1)} async-done(((bf16[8,72,1152]{2,1,0:T(8,128)(2,1)}), bf16[8,72,1152]{2,1,0:T(8,128)(2,1)S(1)}, u32[]{:S(2)}, u32[]{:S(2)}) %all-to-all-start.5) | async-done | bytes 1327136 | tf_op jit(solution)/shard_map/all_to_all | solution.py:420
  153.4 1.8 %shard_map.95 = f32[288,2304]{1,0:T(8,128)} custom-call(bf16[8,72,1152]{2,1,0:T(8,128)(2,1)S(1)} %all-to-all-done.5.in_ref), custom_call_target="tpu_custom_call" | custom-call | flops 1000 | bytes 1000 | tf_op jit(solution)/shard_map/pallas_call | solution.py:28
  (43 shorter events, 0.1 us)
Async XLA Ops:
  0.6 22.3 %collective-permute-start.3 = (bf16[256,1152]{1,0:T(8,128)(2,1)}, bf16[256,1152]{1,0:T(8,128)(2,1)}, u32[]{:S(2)}, u32[]{:S(2)}) collective-permute-start(bf16[256,1152]{1,0:T(8,128)(2,1)} %feats_ref.3), channel_id=1, source_target_pairs={{0,130},{130,0},{2,128},{128,2},{1,131},{131,1},{3,129},{129,3},{4... | collective-permute-start | bytes 1769480 | tf_op jit(solution)/shard_map/ppermute | solution.py:435
  2.2 20.7 %collective-permute-start.4 = (bf16[256,1152]{1,0:T(8,128)(2,1)}, bf16[256,1152]{1,0:T(8,128)(2,1)}, u32[]{:S(2)}, u32[]{:S(2)}) collective-permute-start(bf16[256,1152]{1,0:T(8,128)(2,1)} %feats_ref.2), channel_id=1, source_target_pairs={{0,2},{2,0},{1,3},{3,1},{4,6},{6,4},{5,7},{7,5},{8,10},{10,8},{9,1... | collective-permute-start | bytes 1769480 | tf_op jit(solution)/shard_map/ppermute | solution.py:436
  4.0 34.4 %collective-permute-start.5 = (bf16[256,1152]{1,0:T(8,128)(2,1)}, bf16[256,1152]{1,0:T(8,128)(2,1)S(1)}, u32[]{:S(2)}, u32[]{:S(2)}) collective-permute-start(bf16[256,1152]{1,0:T(8,128)(2,1)} %feats_ref.3), channel_id=1, source_target_pairs={{0,64},{16,80},{32,96},{48,112},{64,0},{80,16},{96,32},{112,48},{1... | collective-permute-start | bytes 1769480 | tf_op jit(solution)/shard_map/ppermute | solution.py:407
  12.5 4.3 %collective-permute-start = (bf16[256,1152]{1,0:T(8,128)(2,1)}, bf16[256,1152]{1,0:T(8,128)(2,1)S(1)}, u32[]{:S(2)}, u32[]{:S(2)}) collective-permute-start(bf16[256,1152]{1,0:T(8,128)(2,1)} %get-tuple-element.63.feats_ref), channel_id=1, source_target_pairs={{0,1},{1,0},{2,3},{3,2},{4,5},{5,4},{6,7},{7,6},{8,9},{9,8},{10,11... | collective-permute-start | bytes 1769480 | tf_op jit(solution)/shard_map/cond/branch_1_fun/ppermute | solution.py:439
  12.6 4.2 %copy-start = (bf16[1152,1152]{1,0:T(8,128)(2,1)S(1)}, bf16[1152,1152]{1,0:T(8,128)(2,1)}, u32[]{:S(2)}) copy-start(bf16[1152,1152]{1,0:T(8,128)(2,1)} %get-tuple-element.62.head_ref) | copy-start | bytes 7962628 | tf_op jit(solution)/shard_map/cond
  16.8 1.9 %copy-start.3 = (bf16[1152,1152]{1,0:T(8,128)(2,1)S(1)}, bf16[1152,1152]{1,0:T(8,128)(2,1)}, u32[]{:S(2)}) copy-start(bf16[1152,1152]{1,0:T(8,128)(2,1)} %get-tuple-element.70.head_ref) | copy-start | bytes 7962628 | tf_op jit(solution)/shard_map/cond
  16.8 1.9 %copy-start.10 = (bf16[256,1152]{1,0:T(8,128)(2,1)S(1)}, bf16[256,1152]{1,0:T(8,128)(2,1)}, u32[]{:S(2)}) copy-start(bf16[256,1152]{1,0:T(8,128)(2,1)} %get-tuple-element.69.feats_ref) | copy-start | bytes 1769476 | tf_op jit(solution)/shard_map/cond
  22.9 0.8 copy-start.6
  22.9 0.9 copy-start.13
  23.8 4.8 %collective-permute-start.1 = (bf16[256,1152]{1,0:T(8,128)(2,1)}, bf16[256,1152]{1,0:T(8,128)(2,1)S(1)}, u32[]{:S(2)}, u32[]{:S(2)}) collective-permute-start(bf16[256,1152]{1,0:T(8,128)(2,1)} %get-tuple-element.84.feats_ref), channel_id=1, source_target_pairs={{0,1},{1,0},{2,3},{3,2},{4,5},{5,4},{6,7},{7,6},{8,9},{9,8},{10,11... | collective-permute-start | bytes 1769480 | tf_op jit(solution)/shard_map/cond/branch_1_fun/ppermute | solution.py:451
  24.3 4.3 %copy-start.1 = (bf16[1152,1152]{1,0:T(8,128)(2,1)S(1)}, bf16[1152,1152]{1,0:T(8,128)(2,1)}, u32[]{:S(2)}) copy-start(bf16[1152,1152]{1,0:T(8,128)(2,1)} %get-tuple-element.83.head_ref) | copy-start | bytes 7962628 | tf_op jit(solution)/shard_map/cond
  28.5 2.0 %copy-start.4 = (bf16[1152,1152]{1,0:T(8,128)(2,1)S(1)}, bf16[1152,1152]{1,0:T(8,128)(2,1)}, u32[]{:S(2)}) copy-start(bf16[1152,1152]{1,0:T(8,128)(2,1)} %get-tuple-element.80.head_ref) | copy-start | bytes 7962628 | tf_op jit(solution)/shard_map/cond
  38.4 5.3 %copy-start.8 = (bf16[256,1152]{1,0:T(8,128)(2,1)S(1)}, bf16[256,1152]{1,0:T(8,128)(2,1)}, u32[]{:S(2)}) copy-start(bf16[256,1152]{1,0:T(8,128)(2,1)} %feats_ref.3) | copy-start | bytes 1769476
  38.4 5.3 %copy-start.16 = (bf16[256,1152]{1,0:T(8,128)(2,1)S(1)}, bf16[256,1152]{1,0:T(8,128)(2,1)}, u32[]{:S(2)}) copy-start(bf16[256,1152]{1,0:T(8,128)(2,1)} %get-tuple-element.188.refs_3_) | copy-start | bytes 1769476
  38.4 5.3 %copy-start.17 = (bf16[256,1152]{1,0:T(8,128)(2,1)S(1)}, bf16[256,1152]{1,0:T(8,128)(2,1)}, u32[]{:S(2)}) copy-start(bf16[256,1152]{1,0:T(8,128)(2,1)} %get-tuple-element.189.refs_5_) | copy-start | bytes 1769476
  43.8 4.2 %copy-start.7 = (bf16[256,1152]{1,0:T(8,128)(2,1)S(1)}, bf16[256,1152]{1,0:T(8,128)(2,1)}, u32[]{:S(2)}) copy-start(bf16[256,1152]{1,0:T(8,128)(2,1)} %copy-done.6) | copy-start | bytes 1769476
  43.8 4.1 %copy-start.12 = (bf16[256,1152]{1,0:T(8,128)(2,1)S(1)}, bf16[256,1152]{1,0:T(8,128)(2,1)}, u32[]{:S(2)}) copy-start(bf16[256,1152]{1,0:T(8,128)(2,1)} %get-tuple-element.179.refs_1_) | copy-start | bytes 1769476
  43.8 4.1 %copy-start.14 = (bf16[2,256,256]{2,1,0:T(8,128)(2,1)S(1)}, bf16[2,256,256]{2,1,0:T(8,128)(2,1)}, u32[]{:S(2)}) copy-start(bf16[2,256,256]{2,1,0:T(8,128)(2,1)} %copy-done.13) | copy-start | bytes 786436
  43.8 4.1 %copy-start.18 = (bf16[4,256,256]{2,1,0:T(8,128)(2,1)S(1)}, bf16[4,256,256]{2,1,0:T(8,128)(2,1)}, u32[]{:S(2)}) copy-start(bf16[4,256,256]{2,1,0:T(8,128)(2,1)} %get-tuple-element.186.refs_3_) | copy-start | bytes 1572868
  43.8 4.1 %copy-start.19 = (bf16[2,256,256]{2,1,0:T(8,128)(2,1)S(1)}, bf16[2,256,256]{2,1,0:T(8,128)(2,1)}, u32[]{:S(2)}) copy-start(bf16[2,256,256]{2,1,0:T(8,128)(2,1)} %get-tuple-element.193.refs_6_) | copy-start | bytes 786436
  47.8 4.3 %collective-permute-start.6 = (bf16[2,288,1152]{2,1,0:T(8,128)(2,1)S(1)}, bf16[2,288,1152]{2,1,0:T(8,128)(2,1)S(1)}, u32[]{:S(2)}, u32[]{:S(2)}) collective-permute-start(bf16[2,288,1152]{2,1,0:T(8,128)(2,1)S(1)} %get-tuple-element.195), channel_id=1, source_target_pairs={{0,1},{1,0},{2,3},{3,2},{4,5},{5,4},{6,7},{7,6},{8,9},{9,8},{10,11... | collective-permute-start | bytes 3981320 | tf_op jit(solution)/shard_map/ppermute | solution.py:477
  51.6 3.1 %collective-permute-start.7 = (bf16[2,256,1152]{2,1,0:T(8,128)(2,1)S(1)}, bf16[2,256,1152]{2,1,0:T(8,128)(2,1)}, u32[]{:S(2)}, u32[]{:S(2)}) collective-permute-start(bf16[2,256,1152]{2,1,0:T(8,128)(2,1)S(1)} %get-tuple-element.197), channel_id=1, source_target_pairs={{0,1},{1,0},{2,3},{3,2},{4,5},{5,4},{6,7},{7,6},{8,9},{9,8},{10,11... | collective-permute-start | bytes 3538952 | tf_op jit(solution)/shard_map/ppermute | solution.py:482
  53.5 5.0 %copy-start.5 = (bf16[256,1152]{1,0:T(8,128)(2,1)S(1)}, bf16[256,1152]{1,0:T(8,128)(2,1)}, u32[]{:S(2)}) copy-start(bf16[256,1152]{1,0:T(8,128)(2,1)} %feats_ref.2) | copy-start | bytes 1769476
  53.5 5.0 %copy-start.11 = (bf16[256,1152]{1,0:T(8,128)(2,1)S(1)}, bf16[256,1152]{1,0:T(8,128)(2,1)}, u32[]{:S(2)}) copy-start(bf16[256,1152]{1,0:T(8,128)(2,1)} %get-tuple-element.200) | copy-start | bytes 1769476
  53.5 5.0 %copy-start.21 = (f32[256,1]{1,0:T(8,128)S(1)}, f32[256,1]{1,0:T(8,128)}, u32[]{:S(2)}) copy-start(f32[256,1]{1,0:T(8,128)} %get-tuple-element.202) | copy-start | bytes 3076
  53.5 5.0 %copy-start.22 = (f32[256,1]{1,0:T(8,128)S(1)}, f32[256,1]{1,0:T(8,128)}, u32[]{:S(2)}) copy-start(f32[256,1]{1,0:T(8,128)} %get-tuple-element.201) | copy-start | bytes 3076
  54.7 22.2 %all-to-all-start.1 = ((bf16[4,144,1152]{2,1,0:T(8,128)(2,1)}), bf16[4,144,1152]{2,1,0:T(8,128)(2,1)S(1)}, u32[]{:S(2)}, u32[]{:S(2)}) async-start(bf16[4,144,1152]{2,1,0:T(8,128)(2,1)} %shard_map.88), calls=%async_computation.1 | async-start | bytes 2654208 | tf_op jit(solution)/shard_map/all_to_all | solution.py:420
  63.2 3.1 %collective-permute-start.2 = (bf16[2,288,1152]{2,1,0:T(8,128)(2,1)S(1)}, bf16[2,288,1152]{2,1,0:T(8,128)(2,1)S(1)}, u32[]{:S(2)}, u32[]{:S(2)}) collective-permute-start(bf16[2,288,1152]{2,1,0:T(8,128)(2,1)S(1)} %get-tuple-element.107), channel_id=1, source_target_pairs={{0,1},{1,0},{2,3},{3,2},{4,5},{5,4},{6,7},{7,6},{8,9},{9,8},{10,11... | collective-permute-start | bytes 3981320 | tf_op jit(solution)/shard_map/cond/branch_1_fun/ppermute | solution.py:496
  68.2 19.1 %collective-permute-start.10 = (bf16[144,1152]{1,0:T(8,128)(2,1)}, bf16[144,1152]{1,0:T(8,128)(2,1)S(1)}, u32[]{:S(2)}, u32[]{:S(2)}) collective-permute-start(bf16[144,1152]{1,0:T(8,128)(2,1)} %get-tuple-element.208), channel_id=1, source_target_pairs={{0,12},{4,0},{8,4},{12,8},{1,13},{5,1},{9,5},{13,9},{2,14},{6,2},{... | collective-permute-start | bytes 995336 | tf_op jit(solution)/shard_map/ppermute | solution.py:413
  71.2 19.9 %collective-permute-start.8 = (bf16[144,1152]{1,0:T(8,128)(2,1)}, bf16[144,1152]{1,0:T(8,128)(2,1)S(1)}, u32[]{:S(2)}, u32[]{:S(2)}) collective-permute-start(bf16[144,1152]{1,0:T(8,128)(2,1)} %get-tuple-element.206), channel_id=1, source_target_pairs={{0,4},{4,8},{8,12},{12,0},{1,5},{5,9},{9,13},{13,1},{2,6},{6,10},{... | collective-permute-start | bytes 995336 | tf_op jit(solution)/shard_map/ppermute | solution.py:413
  71.2 19.9 %collective-permute-start.9 = (bf16[144,1152]{1,0:T(8,128)(2,1)}, bf16[144,1152]{1,0:T(8,128)(2,1)S(1)}, u32[]{:S(2)}, u32[]{:S(2)}) collective-permute-start(bf16[144,1152]{1,0:T(8,128)(2,1)} %get-tuple-element.207), channel_id=1, source_target_pairs={{0,8},{4,12},{8,0},{12,4},{1,9},{5,13},{9,1},{13,5},{2,10},{6,14},... | collective-permute-start | bytes 995336 | tf_op jit(solution)/shard_map/ppermute | solution.py:413
  73.4 32.2 %collective-permute-start.11 = (bf16[256,1152]{1,0:T(8,128)(2,1)S(1)}, bf16[256,1152]{1,0:T(8,128)(2,1)S(1)}, u32[]{:S(2)}, u32[]{:S(2)}) collective-permute-start(bf16[256,1152]{1,0:T(8,128)(2,1)S(1)} %get-tuple-element.214), channel_id=1, source_target_pairs={{0,64},{16,80},{32,96},{48,112},{64,0},{80,16},{96,32},{112,48},{1... | collective-permute-start | bytes 1769480 | tf_op jit(solution)/shard_map/ppermute | solution.py:407
  77.8 15.5 %all-to-all-start.2 = ((bf16[4,36,1152]{2,1,0:T(8,128)(2,1)}), bf16[4,36,1152]{2,1,0:T(8,128)(2,1)S(1)}, u32[]{:S(2)}, u32[]{:S(2)}) async-start(bf16[4,36,1152]{2,1,0:T(8,128)(2,1)} %shard_map.89), calls=%async_computation.2 | async-start | bytes 737280 | tf_op jit(solution)/shard_map/all_to_all | solution.py:420
  92.3 12.8 %copy-start.20 = (bf16[256,1152]{1,0:T(8,128)(2,1)S(1)}, bf16[256,1152]{1,0:T(8,128)(2,1)}, u32[]{:S(2)}) copy-start(bf16[256,1152]{1,0:T(8,128)(2,1)} %get-tuple-element.218) | copy-start | bytes 1769476
  103.5 16.4 %collective-permute-start.12 = (bf16[256,1152]{1,0:T(8,128)(2,1)}, bf16[256,1152]{1,0:T(8,128)(2,1)S(1)}, u32[]{:S(2)}, u32[]{:S(2)}) collective-permute-start(bf16[256,1152]{1,0:T(8,128)(2,1)} %get-tuple-element.216), channel_id=1, source_target_pairs={{0,2},{2,0},{1,3},{3,1},{4,6},{6,4},{5,7},{7,5},{8,10},{10,8},{9,1... | collective-permute-start | bytes 1769480 | tf_op jit(solution)/shard_map/ppermute | solution.py:507
  105.1 14.9 %collective-permute-start.13 = (bf16[256,1152]{1,0:T(8,128)(2,1)S(1)}, bf16[256,1152]{1,0:T(8,128)(2,1)S(1)}, u32[]{:S(2)}, u32[]{:S(2)}) collective-permute-start(bf16[256,1152]{1,0:T(8,128)(2,1)S(1)} %copy-done.20), channel_id=1, source_target_pairs={{0,130},{130,0},{2,128},{128,2},{1,131},{131,1},{3,129},{129,3},{4... | collective-permute-start | bytes 1769480 | tf_op jit(solution)/shard_map/ppermute | solution.py:508
  133.7 19.7 %all-to-all-start.5 = ((bf16[8,72,1152]{2,1,0:T(8,128)(2,1)}), bf16[8,72,1152]{2,1,0:T(8,128)(2,1)S(1)}, u32[]{:S(2)}, u32[]{:S(2)}) async-start(bf16[8,72,1152]{2,1,0:T(8,128)(2,1)} %shard_map.94), calls=%async_computation.5 | async-start | bytes 2654208 | tf_op jit(solution)/shard_map/all_to_all | solution.py:420
  137.3 5.5 %copy-start.2 = (bf16[1152,1152]{1,0:T(8,128)(2,1)S(1)}, bf16[1152,1152]{1,0:T(8,128)(2,1)}, u32[]{:S(2)}) copy-start(bf16[1152,1152]{1,0:T(8,128)(2,1)} %head_ref.5) | copy-start | bytes 7962628
  137.3 5.5 %copy-start.9 = (bf16[256,1152]{1,0:T(8,128)(2,1)S(1)}, bf16[256,1152]{1,0:T(8,128)(2,1)}, u32[]{:S(2)}) copy-start(bf16[256,1152]{1,0:T(8,128)(2,1)} %feats_ref.3) | copy-start | bytes 1769476
  137.3 5.5 %copy-start.15 = (bf16[256,1152]{1,0:T(8,128)(2,1)S(1)}, bf16[256,1152]{1,0:T(8,128)(2,1)}, u32[]{:S(2)}) copy-start(bf16[256,1152]{1,0:T(8,128)(2,1)} %get-tuple-element.220.refs_0_) | copy-start | bytes 1769476
